TPU v7x, 32 devices: a whole 2x2x4 slice. The times are simulated.
32 devices in a mesh: vol: 4 (over z), win: 8 (over y, x, core).
Axes of the slice: x: 2, y: 2, z: 4, core: 2. Of those that a mesh axis runs over, the one named last changes fastest.
Arguments:
- tokens: bfloat16 [16, 32, 343, 96], P(None, ('vol', 'win')), may hold values from -6 to 6
- cotangent: bfloat16 [16, 32, 343, 96], P(None, ('vol', 'win')), may hold values from -6 to 6
- position_bias: bfloat16 [2, 6, 343, 343], replicated, may hold values from -4 to 4
- window_volume: int32 [16, 32], P(None, ('vol', 'win')), may hold values from 0 to 7, as said below
- clip_extent: int32 [16, 32, 3], P(None, ('vol', 'win')), may hold values from 2 to 7, as said below
- master: float32 [223488], P(('vol', 'win'))
- first_moment: float32 [223488], P(('vol', 'win'))
- second_moment: float32 [223488], P(('vol', 'win')), as said below
Outputs:
- output: bfloat16 [16, 32, 343, 96], P(None, ('vol', 'win'))
- input_grad: float32 [16, 32, 343, 96], P(None, ('vol', 'win'))
- new_master: float32 [223488], P(('vol', 'win'))
- new_first: float32 [223488], P(('vol', 'win'))
- new_second: float32 [223488], P(('vol', 'win'))
- new_copy: bfloat16 [223488], P(('vol', 'win'))
Inputs may be any that keep to these rules, and one draw needn't show every extreme that they name: `window_volume`: windows of one micro-batch and one group with equal labels belong to one volume, which covers a box of places of the group's grid. `clip_extent`: a window has 7 voxels along a dimension unless it is the last of its volume along it. `second_moment`: positive.
All inputs are finite; a program needn't handle non-finite values.
Results may differ from a plain program's by a relative error of at most 0.012.
The roundings to bfloat16 on the way count: a program that leaves them out, or rounds other values in their place, can miss the bound.
Values may be sent and summed in bfloat16 or wider, within the bound.
A program may use at most 384 MiB of HBM per device.

v0:
```python
import jax
import jax.numpy as jnp
from jax import lax
from jax.sharding import PartitionSpec as P

C = 96
HEADS = 6
HEAD_DIM = 16
FF = 384
SIDE = 7
SHIFT = 3
WS = 343
STEP = 6


NORM_EPS = 1e-05
MASK_FILL = -1000000000.0
BETA_FIRST = 0.5
BETA_SECOND = 0.5
ADAM_EPS = 1e-08
RATE_MATRIX = 0.1
RATE_VECTOR = 0.4
DECAY_MATRIX = 0.05


def layer_norm(values, gain_vec, offset_vec):
    centred = values - jnp.mean(values, axis=-1, keepdims=True)
    scaled = centred * lax.rsqrt(jnp.mean(centred * centred, axis=-1, keepdims=True) + NORM_EPS)
    return scaled * gain_vec + offset_vec


def gelu_exact(values):
    return jax.nn.gelu(values, approximate=False)


def block_length():
    return 4 * C * C + 2 * C * FF + 8 * C + FF


def unpack(params, which_layer):
    start_at = which_layer * block_length()
    w_qkv = params[start_at : start_at + 3 * C * C].reshape(C, 3 * C)
    start_at = start_at + 3 * C * C
    w_proj = params[start_at : start_at + C * C].reshape(C, C)
    start_at = start_at + C * C
    w_up = params[start_at : start_at + C * FF].reshape(C, FF)
    start_at = start_at + C * FF
    w_down = params[start_at : start_at + FF * C].reshape(FF, C)
    start_at = start_at + FF * C
    vectors = params[start_at : start_at + 8 * C + FF].astype(jnp.float32)
    return (w_qkv, w_proj, w_up, w_down, vectors)


def norm_pull(stream, gain_vec, offset_vec):
    leading = stream.shape[0]
    gains = jnp.broadcast_to(gain_vec, (leading, 1, C))
    offsets = jnp.broadcast_to(offset_vec, (leading, 1, C))
    return jax.vjp(layer_norm, stream, gains, offsets)


def heads_of(values):
    return values.reshape(values.shape[0], WS, HEADS, HEAD_DIM)


def window_index(grid_place, octant_bits, step_sign, groups_a):
    along_a = (grid_place[0] + step_sign * octant_bits[0]) % groups_a
    along_b = (grid_place[1] + step_sign * octant_bits[1]) % 2
    along_c = (grid_place[2] + step_sign * octant_bits[2]) % 2
    return (along_a * 2 + along_b) * 2 + along_c


def exchange_roll(cube, forward, index_win, groups_a):
    window_count = 4 * groups_a
    long_part = SIDE - SHIFT
    leading = cube.shape[0]
    channels = cube.shape[-1]
    grid_place = (index_win // 4, index_win // 2 % 2, index_win % 2)
    direction = -1 if forward else 1
    outgoing = jnp.zeros((window_count, leading, long_part**3, channels), cube.dtype)
    for octant in range(8):
        octant_bits = (octant >> 2 & 1, octant >> 1 & 1, octant & 1)
        portion = cube
        for grid_dim in range(3):
            if forward:
                start_at, stop_at = (SHIFT, SIDE) if octant_bits[grid_dim] == 0 else (0, SHIFT)
            else:
                start_at, stop_at = (
                    (0, long_part) if octant_bits[grid_dim] == 0 else (long_part, SIDE)
                )
            portion = lax.slice_in_dim(portion, start_at, stop_at, axis=grid_dim + 1)
        padding = (
            [(0, 0)]
            + [(0, long_part - portion.shape[axis_no + 1]) for axis_no in range(3)]
            + [(0, 0)]
        )
        portion = jnp.pad(portion, padding).reshape(leading, long_part**3, channels)
        target = window_index(grid_place, octant_bits, direction, groups_a)
        outgoing = lax.dynamic_update_index_in_dim(outgoing, portion, target, 0)
    incoming = lax.all_to_all(outgoing, "win", split_axis=0, concat_axis=0, tiled=True)
    blocks = {}
    for octant in range(8):
        octant_bits = (octant >> 2 & 1, octant >> 1 & 1, octant & 1)
        source = window_index(grid_place, octant_bits, -direction, groups_a)
        portion = lax.dynamic_index_in_dim(incoming, source, 0, keepdims=False)
        portion = portion.reshape(leading, long_part, long_part, long_part, channels)
        part_lengths = [long_part if octant_bits[axis_no] == 0 else SHIFT for axis_no in range(3)]
        blocks[octant_bits] = portion[:, : part_lengths[0], : part_lengths[1], : part_lengths[2]]
    sequence = (0, 1) if forward else (1, 0)
    rows_a = []
    for bit_a in sequence:
        rows_b = []
        for bit_b in sequence:
            rows_c = [blocks[bit_a, bit_b, bit_c] for bit_c in sequence]
            rows_b.append(jnp.concatenate(rows_c, axis=3))
        rows_a.append(jnp.concatenate(rows_b, axis=2))
    return jnp.concatenate(rows_a, axis=1)


def roll_windows(windows, forward, index_win, groups_a):
    leading = windows.shape[0]
    channels = windows.shape[-1]
    cube = windows.reshape(leading, SIDE, SIDE, SIDE, channels)
    cube = exchange_roll(cube, forward, index_win, groups_a)
    return cube.reshape(leading, WS, channels)


def window_masks(own_info, group_info, index_win, groups_a):
    coords = jnp.arange(SIDE, dtype=jnp.int32)
    cube_shape = (SIDE, SIDE, SIDE)
    slot_i = jnp.broadcast_to(coords[:, None, None], cube_shape).reshape(WS)
    slot_j = jnp.broadcast_to(coords[None, :, None], cube_shape).reshape(WS)
    slot_k = jnp.broadcast_to(coords[None, None, :], cube_shape).reshape(WS)
    extents = own_info[:, 0, 1:]
    plain_valid = (
        (slot_i[None] < extents[:, 0:1])
        & (slot_j[None] < extents[:, 1:2])
        & (slot_k[None] < extents[:, 2:3])
    )
    diagonal = jnp.eye(WS, dtype=bool)[None]
    plain_allowed = plain_valid[:, None, :] | diagonal
    from_next = (coords >= SIDE - SHIFT).astype(jnp.int32)
    source_local = jnp.where(from_next > 0, coords - (SIDE - SHIFT), coords + SHIFT)
    place_a = index_win // 4
    place_b = index_win // 2 % 2
    place_c = index_win % 2
    window_a = (place_a + from_next) % groups_a
    window_b = (place_b + from_next) % 2
    window_c = (place_c + from_next) % 2
    wrap_a = from_next * (place_a == groups_a - 1).astype(jnp.int32)
    wrap_b = from_next * (place_b == 1).astype(jnp.int32)
    wrap_c = from_next * (place_c == 1).astype(jnp.int32)
    source_window = (
        (window_a[:, None, None] * 2 + window_b[None, :, None]) * 2 + window_c[None, None, :]
    ).reshape(WS)
    wrap_pattern = (
        wrap_a[:, None, None] * 4 + wrap_b[None, :, None] * 2 + wrap_c[None, None, :]
    ).reshape(WS)
    picker = (source_window[:, None] == jnp.arange(4 * groups_a, dtype=jnp.int32)[None]).astype(
        jnp.int32
    )
    source_info = jnp.sum(picker[None, :, :, None] * group_info[:, None, :, :], axis=2)
    local_i = jnp.broadcast_to(source_local[:, None, None], cube_shape).reshape(WS)
    local_j = jnp.broadcast_to(source_local[None, :, None], cube_shape).reshape(WS)
    local_k = jnp.broadcast_to(source_local[None, None, :], cube_shape).reshape(WS)
    shift_valid = (
        (local_i[None] < source_info[..., 1])
        & (local_j[None] < source_info[..., 2])
        & (local_k[None] < source_info[..., 3])
    )
    shift_label = source_info[..., 0] * 8 + wrap_pattern[None]
    same_region = shift_label[:, :, None] == shift_label[:, None, :]
    shift_allowed = same_region & shift_valid[:, None, :] | diagonal
    keep_mask = plain_valid.astype(jnp.float32)[..., None]
    return (plain_allowed, shift_allowed, keep_mask)


def score_matrix(queries, key_heads, bias_table, allowed):
    raw = jnp.einsum("mqhd,mkhd->mhqk", queries, key_heads, preferred_element_type=jnp.float32)
    biased = raw * HEAD_DIM ** (-0.5) + bias_table.astype(jnp.float32)[None]
    return jnp.where(allowed[:, None], biased, MASK_FILL)


def layer_forward(stream, weights, bias_table, allowed, shifted, roller):
    w_qkv, w_proj, w_up, w_down, vectors = weights
    leading = stream.shape[0]
    normed, pull_first = norm_pull(stream, vectors[0:C], vectors[C : 2 * C])
    shuffled = normed.astype(jnp.bfloat16)
    if shifted:
        shuffled = roller(shuffled, True)
    projected = jnp.einsum("mtc,co->mto", shuffled, w_qkv, preferred_element_type=jnp.float32)
    queries = heads_of((projected[..., :C] + vectors[2 * C : 3 * C]).astype(jnp.bfloat16))
    key_heads = heads_of(projected[..., C : 2 * C].astype(jnp.bfloat16))
    values = heads_of((projected[..., 2 * C :] + vectors[3 * C : 4 * C]).astype(jnp.bfloat16))
    scores = score_matrix(queries, key_heads, bias_table, allowed)
    highest = jnp.max(scores, axis=-1, keepdims=True)
    raised = jnp.exp(scores - highest)
    denominator = jnp.sum(raised, axis=-1, keepdims=True)
    softmax_w = (raised / denominator).astype(jnp.bfloat16)
    attended = jnp.einsum("mhqk,mkhd->mqhd", softmax_w, values, preferred_element_type=jnp.float32)
    attended = attended.reshape(leading, WS, C).astype(jnp.bfloat16)
    branch = (
        jnp.einsum("mtc,co->mto", attended, w_proj, preferred_element_type=jnp.float32)
        + vectors[4 * C : 5 * C]
    )
    if shifted:
        branch = roller(branch.astype(jnp.bfloat16), False).astype(jnp.float32)
    middle = stream + branch
    normed_two, pull_second = norm_pull(middle, vectors[5 * C : 6 * C], vectors[6 * C : 7 * C])
    normed_two = normed_two.astype(jnp.bfloat16)
    hidden = (
        jnp.einsum("mtc,cf->mtf", normed_two, w_up, preferred_element_type=jnp.float32)
        + vectors[8 * C :]
    )
    active, pull_gelu = jax.vjp(gelu_exact, hidden)
    active = active.astype(jnp.bfloat16)
    output = middle + (
        jnp.einsum("mtf,fc->mtc", active, w_down, preferred_element_type=jnp.float32)
        + vectors[7 * C : 8 * C]
    )
    kept_state = (
        pull_first,
        shuffled,
        queries,
        key_heads,
        values,
        highest + jnp.log(denominator),
        attended,
        pull_second,
        normed_two,
        pull_gelu,
        active,
    )
    return (output, kept_state)


def layer_backward(grad_out, weights, bias_table, allowed, shifted, roller, kept_state):
    w_qkv, w_proj, w_up, w_down, vectors = weights
    (
        pull_first,
        shuffled,
        queries,
        key_heads,
        values,
        log_total,
        attended,
        pull_second,
        normed_two,
        pull_gelu,
        active,
    ) = kept_state
    leading = grad_out.shape[0]
    grad_down = grad_out.astype(jnp.bfloat16)
    g_down = jnp.einsum("mtf,mtc->mfc", active, grad_down, preferred_element_type=jnp.float32)
    grad_active = jnp.einsum("mtc,fc->mtf", grad_down, w_down, preferred_element_type=jnp.float32)
    grad_hidden = pull_gelu(grad_active)[0].astype(jnp.bfloat16)
    g_up = jnp.einsum("mtc,mtf->mcf", normed_two, grad_hidden, preferred_element_type=jnp.float32)
    grad_normed = jnp.einsum("mtf,cf->mtc", grad_hidden, w_up, preferred_element_type=jnp.float32)
    grad_middle, g_gain_two, g_offset_two = pull_second(grad_normed)
    grad_middle = grad_middle + grad_out
    grad_branch = grad_middle.astype(jnp.bfloat16)
    if shifted:
        grad_branch = roller(grad_branch, True)
    g_proj = jnp.einsum("mtc,mto->mco", attended, grad_branch, preferred_element_type=jnp.float32)
    grad_attended = heads_of(
        jnp.einsum("mto,co->mtc", grad_branch, w_proj, preferred_element_type=jnp.float32).astype(
            jnp.bfloat16
        )
    )
    scores = score_matrix(queries, key_heads, bias_table, allowed)
    softmax_f = jnp.exp(scores - log_total)
    grad_soft = jnp.einsum(
        "mqhd,mkhd->mhqk", grad_attended, values, preferred_element_type=jnp.float32
    )
    grad_values = jnp.einsum(
        "mhqk,mqhd->mkhd",
        softmax_f.astype(jnp.bfloat16),
        grad_attended,
        preferred_element_type=jnp.float32,
    )
    inner_sum = jnp.sum(grad_soft * softmax_f, axis=-1, keepdims=True)
    grad_raw = (softmax_f * (grad_soft - inner_sum) * HEAD_DIM ** (-0.5)).astype(jnp.bfloat16)
    grad_queries = jnp.einsum(
        "mhqk,mkhd->mqhd", grad_raw, key_heads, preferred_element_type=jnp.float32
    )
    grad_keys = jnp.einsum("mhqk,mqhd->mkhd", grad_raw, queries, preferred_element_type=jnp.float32)
    grad_mixed = jnp.concatenate(
        (
            grad_queries.reshape(leading, WS, C),
            grad_keys.reshape(leading, WS, C),
            grad_values.reshape(leading, WS, C),
        ),
        axis=-1,
    ).astype(jnp.bfloat16)
    g_qkv = jnp.einsum("mtc,mto->mco", shuffled, grad_mixed, preferred_element_type=jnp.float32)
    grad_shuffled = jnp.einsum("mto,co->mtc", grad_mixed, w_qkv, preferred_element_type=jnp.float32)
    if shifted:
        grad_shuffled = roller(grad_shuffled.astype(jnp.bfloat16), False).astype(jnp.float32)
    grad_stream, g_gain_one, g_offset_one = pull_first(grad_shuffled)
    grad_stream = grad_stream + grad_middle
    mixed_float = grad_mixed.astype(jnp.float32)
    g_bias_q = jnp.sum(mixed_float[..., :C], axis=1)
    g_bias_v = jnp.sum(mixed_float[..., 2 * C :], axis=1)
    g_bias_proj = jnp.sum(grad_branch.astype(jnp.float32), axis=1)
    g_bias_down = jnp.sum(grad_down.astype(jnp.float32), axis=1)
    g_bias_up = jnp.sum(grad_hidden.astype(jnp.float32), axis=1)
    flat_grads = jnp.concatenate(
        (
            g_qkv.reshape(leading, -1),
            g_proj.reshape(leading, -1),
            g_up.reshape(leading, -1),
            g_down.reshape(leading, -1),
            g_gain_one.reshape(leading, C),
            g_offset_one.reshape(leading, C),
            g_bias_q,
            g_bias_v,
            g_bias_proj,
            g_gain_two.reshape(leading, C),
            g_offset_two.reshape(leading, C),
            g_bias_down,
            g_bias_up,
        ),
        axis=1,
    )
    return (grad_stream, flat_grads)


def on_device(
    tokens,
    cotangent,
    position_bias,
    window_volume,
    clip_extent,
    master,
    first_moment,
    second_moment,
):
    groups_a = lax.axis_size("win") // 4
    index_win = lax.axis_index("win")
    params = lax.all_gather(master.astype(jnp.bfloat16), ("vol", "win"), axis=0, tiled=True)
    own_info = jnp.concatenate((window_volume[:, :, None], clip_extent), axis=2)
    group_info = lax.all_gather(own_info, "win", axis=1, tiled=True)
    plain_allowed, shift_allowed, keep_mask = window_masks(
        own_info, group_info, index_win, groups_a
    )

    def roller(windows, forward):
        return roll_windows(windows, forward, index_win, groups_a)

    first_weights = unpack(params, 0)
    second_weights = unpack(params, 1)
    stream = tokens[:, 0].astype(jnp.float32)
    stream, kept_one = layer_forward(
        stream, first_weights, position_bias[0], plain_allowed, False, roller
    )
    stream, kept_two = layer_forward(
        stream, second_weights, position_bias[1], shift_allowed, True, roller
    )
    output = (stream * keep_mask).astype(jnp.bfloat16)
    grad_out = cotangent[:, 0].astype(jnp.float32) * keep_mask
    grad_out, flat_two = layer_backward(
        grad_out, second_weights, position_bias[1], shift_allowed, True, roller, kept_two
    )
    grad_in, flat_one = layer_backward(
        grad_out, first_weights, position_bias[0], plain_allowed, False, roller, kept_one
    )
    all_grads = jnp.concatenate((flat_one, flat_two), axis=1)
    shard_grad = jnp.sum(
        lax.psum_scatter(all_grads, ("vol", "win"), scatter_dimension=1, tiled=True), axis=0
    )
    shard_len = master.shape[0]
    position = (
        lax.axis_index(("vol", "win")) * shard_len + jnp.arange(shard_len, dtype=jnp.int32)
    ) % block_length()
    is_vector = position >= 4 * C * C + 2 * C * FF
    step_rate = jnp.where(is_vector, RATE_VECTOR, RATE_MATRIX)
    weight_decay = jnp.where(is_vector, 0.0, DECAY_MATRIX)
    moment_one = BETA_FIRST * first_moment + (1.0 - BETA_FIRST) * shard_grad
    moment_two = BETA_SECOND * second_moment + (1.0 - BETA_SECOND) * shard_grad * shard_grad
    corrected_one = moment_one / (1.0 - BETA_FIRST**STEP)
    corrected_two = moment_two / (1.0 - BETA_SECOND**STEP)
    normalized = corrected_one / (jnp.sqrt(corrected_two) + ADAM_EPS)
    new_master = master - step_rate * (normalized + weight_decay * master)
    return (
        output[:, None],
        grad_in[:, None],
        new_master,
        moment_one,
        moment_two,
        new_master.astype(jnp.bfloat16),
    )


def solution(mesh):
    placed = (
        P(None, ("vol", "win"), None, None),
        P(None, ("vol", "win"), None, None),
        P(),
        P(None, ("vol", "win")),
        P(None, ("vol", "win"), None),
        P(("vol", "win")),
        P(("vol", "win")),
        P(("vol", "win")),
    )
    return jax.shard_map(
        on_device,
        mesh=mesh,
        in_specs=placed,
        out_specs=(
            P(None, ("vol", "win"), None, None),
            P(None, ("vol", "win"), None, None),
            P(("vol", "win")),
            P(("vol", "win")),
            P(("vol", "win")),
            P(("vol", "win")),
        ),
        check_vma=False,
    )
```

profile of v0, /device:TPU:0, one launch (start us, length us, event | category | flops | bytes accessed | tf_op | source)
XLA Modules:
  0.0 1258.2 jit_solution(9034223672970209911)
XLA Ops:
  10.9 10.3 all_gather.7
  24.0 8.3 fusion.191
  35.4 4.9 copy.115
  41.1 4.8 and_or_fusion
  45.9 96.6 %all-reduce.33.cloned.1.call-done = bf16[223488]{0:T(1024)(128)(2,1)} async-done(((bf16[223488]{0:T(1024)(128)(2,1)}), bf16[223488]{0:T(1024)(128)(2,1)}) %all-reduce.33.cloned.1.call-update) | async-done | bytes 446992
  156.7 22.4 %fusion.199 = (f32[16,6,343]{2,1,0:T(8,128)S(1)}, f32[16,6,343,343]{2,3,1,0:T(8,128)}) fusion(f32[6,343,343]{1,2,0:T(8,128)S(1)} %copy-done.43, bf16[16,343,6,16]{1,3,2,0:T(8,128)(2,1)} %bitcast.405, bf16[16,343,6,16]{1,3,2,0:T(8,128)(2,1)S(1)} %bitcast.389, pred[16,343,343]{1,2,0:T(8,128)(4,1)S(1)} %get-tuple-element.125), kind=kOutput, calls=%fused_computation.394 | convolution fusion | flops 406562016 | bytes 52122280 | tf_op jit(solution)/shard_map/mqhd,mkhd->mhqk/dot_general | solution.py:178
  179.1 20.1 %fusion.4 = f32[16,6,343]{2,1,0:T(8,128)S(1)} fusion(f32[16,6,343,343]{2,3,1,0:T(8,128)} %get-tuple-element.153, f32[16,6,343]{2,1,0:T(8,128)S(1)} %get-tuple-element.152), kind=kLoop, calls=%fused_computation.16 | loop fusion | flops 22555680 | bytes 45440640 | tf_op jit(solution)/shard_map/reduce_sum | solution.py:197
  199.3 18.9 %fusion.106 = bf16[16,6,16,343]{3,2,1,0:T(8,128)(2,1)S(1)} fusion(bf16[16,343,6,16]{1,3,2,0:T(8,128)(2,1)S(1)} %bitcast.347, f32[16,6,343,343]{2,3,1,0:T(8,128)} %get-tuple-element.153, f32[16,6,343]{2,1,0:T(8,128)S(1)} %fusion.4, f32[16,6,343]{2,1,0:T(8,128)S(1)} %get-tuple-element.152), kind=kOutput, calls=%fused_computation.169 | convolution fusion | flops 395827488 | bytes 47548032 | tf_op jit(solution)/shard_map/mhqk,mkhd->mqhd/dot_general | solution.py:199
  220.2 3.8 fusion.58
  224.0 20.4 %multiply_convert_fusion.3 = (bf16[16,343,384]{2,1,0:T(8,128)(2,1)S(1)}, f32[16,343,384]{2,1,0:T(8,128)}) fusion(f32[16,343,384]{2,1,0:T(8,128)S(1)} %get-tuple-element.156, f32[384]{0:T(512)S(1)} %slice.628, u16[343,384]{1,0:T(8,128)(2,1)S(1)} %get-tuple-element.33, u16[343,384]{1,0:T(8,128)(2,1)S(1)} %get-tuple-element.32), kind=kLoop, calls=%fused_computation.68 | loop fusion | flops 149624832 | bytes 21602304 | tf_op jit(solution)/shard_map/convert_element_type | solution.py:215
  265.5 4.5 all-to-all-start
  270.1 5.0 copy.127
  276.6 20.1 %all-to-all-done = bf16[8,16,64,96]{3,1,2,0:T(8,128)(2,1)} async-done(((bf16[8,16,64,96]{3,1,2,0:T(8,128)(2,1)}), bf16[8,16,64,96]{3,1,2,0:T(8,128)(2,1)}, u32[]{:S(2)}, u32[]{:S(2)}) %all-to-all-start) | async-done | bytes 1572896 | tf_op jit(solution)/shard_map/all_to_all | solution.py:99
  308.2 23.2 %fusion.202 = (f32[16,6,343]{2,1,0:T(8,128)S(1)}, f32[16,6,343,343]{2,3,1,0:T(8,128)}) fusion(f32[6,343,343]{1,2,0:T(8,128)S(1)} %copy-done.44, bf16[16,343,6,16]{1,3,2,0:T(8,128)(2,1)} %bitcast.407, bf16[16,343,6,16]{1,3,2,0:T(8,128)(2,1)} %bitcast.391, pred[16,343,343]{1,2,0:T(8,128)(4,1)S(1)} %copy-done.47), kind=kOutput, calls=%fused_computation.397 | convolution fusion | flops 406562016 | bytes 52122280 | tf_op jit(solution)/shard_map/mqhd,mkhd->mhqk/dot_general | solution.py:178
  331.5 20.1 %fusion.5 = f32[16,6,343]{2,1,0:T(8,128)S(1)} fusion(f32[16,6,343,343]{2,3,1,0:T(8,128)} %get-tuple-element.160, f32[16,6,343]{2,1,0:T(8,128)S(1)} %get-tuple-element.159), kind=kLoop, calls=%fused_computation.17 | loop fusion | flops 22555680 | bytes 45440640 | tf_op jit(solution)/shard_map/reduce_sum | solution.py:197
  351.6 18.5 %fusion.105 = bf16[16,6,16,343]{3,2,1,0:T(8,128)(2,1)S(1)} fusion(bf16[16,343,6,16]{1,3,2,0:T(8,128)(2,1)S(1)} %bitcast.349, f32[16,6,343,343]{2,3,1,0:T(8,128)} %get-tuple-element.160, f32[16,6,343]{2,1,0:T(8,128)S(1)} %fusion.5, f32[16,6,343]{2,1,0:T(8,128)S(1)} %get-tuple-element.159), kind=kOutput, calls=%fused_computation.168 | convolution fusion | flops 395827488 | bytes 47548032 | tf_op jit(solution)/shard_map/mhqk,mkhd->mqhd/dot_general | solution.py:199
  391.1 4.4 all-to-all-start.1
  399.5 22.7 %all-to-all-done.1 = bf16[8,16,64,96]{3,1,2,0:T(8,128)(2,1)} async-done(((bf16[8,16,64,96]{3,1,2,0:T(8,128)(2,1)}), bf16[8,16,64,96]{3,1,2,0:T(8,128)(2,1)}, u32[]{:S(2)}, u32[]{:S(2)}) %all-to-all-start.1) | async-done | bytes 1572896 | tf_op jit(solution)/shard_map/all_to_all | solution.py:99
  426.5 3.3 copy.131
  432.8 3.9 fusion.59
  436.7 20.1 %multiply_convert_fusion.2 = (bf16[16,343,384]{2,1,0:T(8,128)(2,1)}, f32[16,343,384]{2,1,0:T(8,128)S(1)}) fusion(f32[16,343,384]{2,1,0:T(8,128)S(1)} %get-tuple-element.161, f32[384]{0:T(512)S(1)} %slice.679, u16[343,384]{1,0:T(8,128)(2,1)S(1)} %get-tuple-element.31, u16[343,384]{1,0:T(8,128)(2,1)S(1)} %get-tuple-element.30), kind=kLoop, calls=%fused_computation.55 | loop fusion | flops 149624832 | bytes 21602304 | tf_op jit(solution)/shard_map/convert_element_type | solution.py:215
  456.8 5.3 convert_reduce_fusion
  478.1 4.5 all-to-all-start.2
  492.1 4.7 fusion.178
  496.8 12.5 all-to-all-done.2
  516.8 19.1 %fusion.203 = f32[16,6,343,343]{2,3,1,0:T(8,128)} fusion(bf16[16,343,6,16]{1,3,2,0:T(8,128)(2,1)S(1)} %bitcast.332, bf16[16,343,6,16]{1,3,2,0:T(8,128)(2,1)S(1)} %bitcast.350), kind=kOutput, calls=%fused_computation.398 | convolution fusion | flops 361417728 | bytes 47284608 | tf_op jit(solution)/shard_map/mqhd,mkhd->mhqk/dot_general | solution.py:271
  535.8 18.7 %fusion.90 = bf16[16,6,16,343]{3,2,1,0:T(8,128)(2,1)S(1)} fusion(bf16[16,343,6,16]{1,3,2,0:T(8,128)(2,1)S(1)} %bitcast.333, f32[16,6,343,343]{2,3,1,0:T(8,128)} %get-tuple-element.160, f32[16,6,343]{2,1,0:T(8,128)} %log_add_fusion), kind=kOutput, calls=%fused_computation.160 | convolution fusion | flops 384533184 | bytes 47416320 | tf_op jit(solution)/shard_map/mhqk,mqhd->mkhd/dot_general | solution.py:274
  554.6 64.0 %fusion.99 = bf16[16,6,16,343]{3,2,1,0:T(8,128)(2,1)S(1)} fusion(bf16[16,343,6,16]{1,3,2,0:T(8,128)(2,1)} %bitcast.392, f32[16,6,343,343]{2,3,1,0:T(8,128)} %fusion.203, f32[16,6,343,343]{2,3,1,0:T(8,128)} %get-tuple-element.160, f32[16,6,343]{2,1,0:T(8,128)} %log_add_fusion), kind=kOutput, calls=%fused_computation.163 | convolution fusion | flops 441037984 | bytes 92593536 | tf_op jit(solution)/shard_map/mhqk,mkhd->mqhd/dot_general | solution.py:282
  618.7 64.5 %fusion.102 = bf16[16,6,16,343]{3,2,1,0:T(8,128)(2,1)} fusion(bf16[16,343,6,16]{1,3,2,0:T(8,128)(2,1)} %bitcast.408, f32[16,6,343,343]{2,3,1,0:T(8,128)} %fusion.203, f32[16,6,343,343]{2,3,1,0:T(8,128)} %get-tuple-element.160, f32[16,6,343]{2,1,0:T(8,128)S(1)} %copy-done.51), kind=kOutput, calls=%fused_computation.164 | convolution fusion | flops 441037984 | bytes 92593536 | tf_op jit(solution)/shard_map/mhqk,mqhd->mkhd/dot_general | solution.py:285
  683.2 3.3 convolution_convert_fusion.2
  696.6 4.4 all-to-all-start.3
  701.0 4.1 fusion.128
  708.4 4.6 copy.190
  714.9 4.5 fusion.173
  719.3 4.3 reshape.1068
  731.6 3.6 copy.141
  746.1 7.5 convert_reduce_fusion.1
  763.6 19.4 %fusion.204 = f32[16,6,343,343]{2,3,1,0:T(8,128)} fusion(bf16[16,343,6,16]{1,3,2,0:T(8,128)(2,1)S(1)} %bitcast.330, bf16[16,343,6,16]{1,3,2,0:T(8,128)(2,1)S(1)} %bitcast.348), kind=kOutput, calls=%fused_computation.399 | convolution fusion | flops 361417728 | bytes 47284608 | tf_op jit(solution)/shard_map/mqhd,mkhd->mhqk/dot_general | solution.py:271
  783.0 18.7 %fusion.87 = bf16[16,6,16,343]{3,2,1,0:T(8,128)(2,1)S(1)} fusion(bf16[16,343,6,16]{1,3,2,0:T(8,128)(2,1)S(1)} %bitcast.331, f32[16,6,343,343]{2,3,1,0:T(8,128)} %get-tuple-element.153, f32[16,6,343]{2,1,0:T(8,128)S(1)} %copy-done.49), kind=kOutput, calls=%fused_computation.159 | convolution fusion | flops 384533184 | bytes 47416320 | tf_op jit(solution)/shard_map/mhqk,mqhd->mkhd/dot_general | solution.py:274
  801.7 63.8 %fusion.93 = bf16[16,6,16,343]{3,2,1,0:T(8,128)(2,1)} fusion(bf16[16,343,6,16]{1,3,2,0:T(8,128)(2,1)} %bitcast.390, f32[16,6,343,343]{2,3,1,0:T(8,128)} %fusion.204, f32[16,6,343,343]{2,3,1,0:T(8,128)} %get-tuple-element.153, f32[16,6,343]{2,1,0:T(8,128)S(1)} %copy-done.49), kind=kOutput, calls=%fused_computation.161 | convolution fusion | flops 441037984 | bytes 92593536 | tf_op jit(solution)/shard_map/mhqk,mkhd->mqhd/dot_general | solution.py:282
  865.6 63.9 %fusion.96 = bf16[16,6,16,343]{3,2,1,0:T(8,128)(2,1)} fusion(bf16[16,343,6,16]{1,3,2,0:T(8,128)(2,1)} %bitcast.406, f32[16,6,343,343]{2,3,1,0:T(8,128)} %fusion.204, f32[16,6,343,343]{2,3,1,0:T(8,128)} %get-tuple-element.153, f32[16,6,343]{2,1,0:T(8,128)S(1)} %copy-done.50), kind=kOutput, calls=%fused_computation.162 | convolution fusion | flops 441037984 | bytes 92593536 | tf_op jit(solution)/shard_map/mhqk,mqhd->mkhd/dot_general | solution.py:285
  929.6 4.6 fusion.114
  937.3 4.6 reshape.1067
  947.0 3.7 fusion.180
  951.4 4.2 reshape.1064
  955.7 3.7 slice_reduce_fusion.2
  1000.7 5.0 fusion.107
  1008.5 240.5 %all-reduce.35.cloned.1.call-done = f32[16,223488]{1,0:T(8,128)} async-done(((f32[16,223488]{1,0:T(8,128)}), f32[16,223488]{1,0:T(8,128)}) %all-reduce.35.cloned.1.call-update) | async-done | bytes 14303248
  (587 shorter events, 222.8 us)
Async XLA Ops:
  7.2 135.3 %all-reduce.33.cloned.1.call-start = ((), (), s32[]{:S(2)}) async-start(), calls=%async_computation.4 | async-start | bytes 897024
  22.2 129.4 %copy-start.70 = (f32[16,343]{1,0:T(8,128)}, f32[16,343]{1,0:T(8,128)S(1)}, u32[]{:S(2)}) copy-start(f32[16,343]{1,0:T(8,128)S(1)} %broadcast_multiply_fusion.3) | copy-start | bytes 65860
  22.6 23.3 %copy-start.101 = (f32[16,343]{1,0:T(8,128)}, f32[16,343]{1,0:T(8,128)S(1)}, u32[]{:S(2)}) copy-start(f32[16,343]{1,0:T(8,128)S(1)} %fusion.75) | copy-start | bytes 65860
  45.9 107.8 %copy-start.76 = (f32[16,343]{1,0:T(8,128)}, f32[16,343]{1,0:T(8,128)S(1)}, u32[]{:S(2)}) copy-start(f32[16,343]{1,0:T(8,128)S(1)} %fusion.150) | copy-start | bytes 65860
  143.2 80.8 %copy-start.126 = (f32[384]{0:T(512)}, f32[384]{0:T(512)S(1)}, u32[]{:S(2)}) copy-start(f32[384]{0:T(512)S(1)} %slice.628) | copy-start | bytes 4612
  144.4 75.7 %copy-start.123 = (f32[96]{0:T(128)}, f32[96]{0:T(128)S(1)}, u32[]{:S(2)}) copy-start(f32[96]{0:T(128)S(1)} %get-tuple-element.174) | copy-start | bytes 1156
  144.4 75.7 %copy-start.135 = (f32[96]{0:T(128)}, f32[96]{0:T(128)S(1)}, u32[]{:S(2)}) copy-start(f32[96]{0:T(128)S(1)} %get-tuple-element.175) | copy-start | bytes 1156
  144.4 103.3 %copy-start.120 = (f32[96]{0:T(128)}, f32[96]{0:T(128)S(1)}, u32[]{:S(2)}) copy-start(f32[96]{0:T(128)S(1)} %get-tuple-element.138) | copy-start | bytes 1156
  151.5 92.9 %copy-start.85 = (bf16[384,96]{1,0:T(8,128)(2,1)}, bf16[384,96]{1,0:T(8,128)(2,1)S(1)}, u32[]{:S(2)}) copy-start(bf16[384,96]{1,0:T(8,128)(2,1)S(1)} %reshape.1011) | copy-start | bytes 221188
  155.9 43.4 %copy-start.33 = (bf16[16,343,96]{1,2,0:T(8,128)(2,1)}, bf16[16,343,96]{1,2,0:T(8,128)(2,1)S(1)}, u32[]{:S(2)}) copy-start(bf16[16,343,96]{1,2,0:T(8,128)(2,1)S(1)} %get-tuple-element.77) | copy-start | bytes 3161092
  179.1 20.1 %copy-start.60 = (f32[16,6,343]{2,1,0:T(8,128)}, f32[16,6,343]{2,1,0:T(8,128)S(1)}, u32[]{:S(2)}) copy-start(f32[16,6,343]{2,1,0:T(8,128)S(1)} %get-tuple-element.152) | copy-start | bytes 395140
  199.2 19.0 %copy-start.61 = (f32[16,6,343]{2,1,0:T(8,128)}, f32[16,6,343]{2,1,0:T(8,128)S(1)}, u32[]{:S(2)}) copy-start(f32[16,6,343]{2,1,0:T(8,128)S(1)} %fusion.4) | copy-start | bytes 395140
  219.2 25.2 %copy-start.5 = (f32[16,343,96]{1,2,0:T(8,128)}, f32[16,343,96]{1,2,0:T(8,128)S(1)}, u32[]{:S(2)}) copy-start(f32[16,343,96]{1,2,0:T(8,128)S(1)} %get-tuple-element.155) | copy-start | bytes 6322180
  224.0 20.4 %copy-start.29 = (f32[16,343,384]{2,1,0:T(8,128)}, f32[16,343,384]{2,1,0:T(8,128)S(1)}, u32[]{:S(2)}) copy-start(f32[16,343,384]{2,1,0:T(8,128)S(1)} %get-tuple-element.156) | copy-start | bytes 25288708
  224.0 20.4 %copy-start.141 = (f32[96]{0:T(128)S(1)}, f32[96]{0:T(128)}, u32[]{:S(2)}) copy-start(f32[96]{0:T(128)} %get-tuple-element.176) | copy-start | bytes 1156
  246.5 183.3 %copy-start = (f32[16,343,96]{1,2,0:T(8,128)}, f32[16,343,96]{1,2,0:T(8,128)S(1)}, u32[]{:S(2)}) copy-start(f32[16,343,96]{1,2,0:T(8,128)S(1)} %get-tuple-element.158) | copy-start | bytes 6322180
  265.5 31.2 %all-to-all-start = ((bf16[8,16,64,96]{3,1,2,0:T(8,128)(2,1)}), bf16[8,16,64,96]{3,1,2,0:T(8,128)(2,1)}, u32[]{:S(2)}, u32[]{:S(2)}) async-start(bf16[8,16,64,96]{3,1,2,0:T(8,128)(2,1)} %constant_dynamic-update-slice_fusion.34), calls=%async_computation | async-start | bytes 4194304 | tf_op jit(solution)/shard_map/all_to_all | solution.py:99
  331.5 20.1 %copy-start.62 = (f32[16,6,343]{2,1,0:T(8,128)}, f32[16,6,343]{2,1,0:T(8,128)S(1)}, u32[]{:S(2)}) copy-start(f32[16,6,343]{2,1,0:T(8,128)S(1)} %get-tuple-element.159) | copy-start | bytes 395140
  351.6 18.5 %copy-start.63 = (f32[16,6,343]{2,1,0:T(8,128)}, f32[16,6,343]{2,1,0:T(8,128)S(1)}, u32[]{:S(2)}) copy-start(f32[16,6,343]{2,1,0:T(8,128)S(1)} %fusion.5) | copy-start | bytes 395140
  351.6 19.6 %copy-start.108 = (bf16[96,96]{1,0:T(8,128)(2,1)S(1)}, bf16[96,96]{1,0:T(8,128)(2,1)}, u32[]{:S(2)}) copy-start(bf16[96,96]{1,0:T(8,128)(2,1)} %reshape.1026) | copy-start | bytes 55300
  351.6 19.6 %copy-start.138 = (f32[96]{0:T(128)S(1)}, f32[96]{0:T(128)}, u32[]{:S(2)}) copy-start(f32[96]{0:T(128)} %get-tuple-element.134) | copy-start | bytes 1156
  391.1 31.1 %all-to-all-start.1 = ((bf16[8,16,64,96]{3,1,2,0:T(8,128)(2,1)}), bf16[8,16,64,96]{3,1,2,0:T(8,128)(2,1)}, u32[]{:S(2)}, u32[]{:S(2)}) async-start(bf16[8,16,64,96]{3,1,2,0:T(8,128)(2,1)} %constant_dynamic-update-slice_fusion.26), calls=%async_computation.1 | async-start | bytes 4194304 | tf_op jit(solution)/shard_map/all_to_all | solution.py:99
  431.8 33.0 %copy-start.2 = (f32[16,343,96]{1,2,0:T(8,128)}, f32[16,343,96]{1,2,0:T(8,128)S(1)}, u32[]{:S(2)}) copy-start(f32[16,343,96]{1,2,0:T(8,128)S(1)} %get-tuple-element.71) | copy-start | bytes 6322180
  431.9 32.9 %copy-start.69 = (f32[16,343]{1,0:T(8,128)}, f32[16,343]{1,0:T(8,128)S(1)}, u32[]{:S(2)}) copy-start(f32[16,343]{1,0:T(8,128)S(1)} %broadcast_multiply_fusion) | copy-start | bytes 65860
  432.2 32.6 %copy-start.84 = (f32[16,343]{1,0:T(8,128)}, f32[16,343]{1,0:T(8,128)S(1)}, u32[]{:S(2)}) copy-start(f32[16,343]{1,0:T(8,128)S(1)} %fusion.153) | copy-start | bytes 65860
  436.7 20.1 %copy-start.18 = (bf16[16,1,343,96]{2,3,1,0:T(8,128)(2,1)S(1)}, bf16[16,1,343,96]{2,3,1,0:T(8,128)(2,1)}, u32[]{:S(2)}) copy-start(bf16[16,1,343,96]{2,3,1,0:T(8,128)(2,1)} %param.9) | copy-start | bytes 3161092
  436.7 20.1 %copy-start.64 = (f32[16,343]{1,0:T(8,128)S(1)}, f32[16,343]{1,0:T(8,128)}, u32[]{:S(2)}) copy-start(f32[16,343]{1,0:T(8,128)} %get-tuple-element.66) | copy-start | bytes 65860
  436.7 20.1 %copy-start.87 = (bf16[384,96]{1,0:T(8,128)(2,1)S(1)}, bf16[384,96]{1,0:T(8,128)(2,1)}, u32[]{:S(2)}) copy-start(bf16[384,96]{1,0:T(8,128)(2,1)} %reshape.1036) | copy-start | bytes 221188
  478.1 31.1 %all-to-all-start.2 = ((bf16[8,16,64,96]{3,1,2,0:T(8,128)(2,1)}), bf16[8,16,64,96]{3,1,2,0:T(8,128)(2,1)}, u32[]{:S(2)}, u32[]{:S(2)}) async-start(bf16[8,16,64,96]{3,1,2,0:T(8,128)(2,1)} %constant_dynamic-update-slice_fusion.18), calls=%async_computation.2 | async-start | bytes 4194304 | tf_op jit(solution)/shard_map/all_to_all | solution.py:99
  515.5 20.3 %copy-start.20 = (bf16[16,343,96]{1,2,0:T(8,128)(2,1)}, bf16[16,343,96]{1,2,0:T(8,128)(2,1)S(1)}, u32[]{:S(2)}) copy-start(bf16[16,343,96]{1,2,0:T(8,128)(2,1)S(1)} %copy.136) | copy-start | bytes 3161092
  554.6 128.6 %copy-start.30 = (bf16[16,6,16,343]{3,2,1,0:T(8,128)(2,1)}, bf16[16,6,16,343]{3,2,1,0:T(8,128)(2,1)S(1)}, u32[]{:S(2)}) copy-start(bf16[16,6,16,343]{3,2,1,0:T(8,128)(2,1)S(1)} %fusion.90) | copy-start | bytes 3161092
  554.6 64.1 %copy-start.51 = (f32[16,6,343]{2,1,0:T(8,128)S(1)}, f32[16,6,343]{2,1,0:T(8,128)}, u32[]{:S(2)}) copy-start(f32[16,6,343]{2,1,0:T(8,128)} %log_add_fusion) | copy-start | bytes 395140
  618.7 64.5 %copy-start.53 = (bf16[16,6,16,343]{3,2,1,0:T(8,128)(2,1)}, bf16[16,6,16,343]{3,2,1,0:T(8,128)(2,1)S(1)}, u32[]{:S(2)}) copy-start(bf16[16,6,16,343]{3,2,1,0:T(8,128)(2,1)S(1)} %fusion.99) | copy-start | bytes 3161092
  618.7 64.5 %copy-start.109 = (bf16[96,288,1]{1,0,2:T(8,128)(2,1)S(1)}, bf16[96,288,1]{1,0,2:T(8,128)(2,1)}, u32[]{:S(2)}) copy-start(bf16[96,288,1]{1,0,2:T(8,128)(2,1)} %reshape.1089) | copy-start | bytes 165892
  696.6 31.0 %all-to-all-start.3 = ((bf16[8,16,64,96]{3,1,2,0:T(8,128)(2,1)}), bf16[8,16,64,96]{3,1,2,0:T(8,128)(2,1)}, u32[]{:S(2)}, u32[]{:S(2)}) async-start(bf16[8,16,64,96]{3,1,2,0:T(8,128)(2,1)} %constant_dynamic-update-slice_fusion.10), calls=%async_computation.3 | async-start | bytes 4194304 | tf_op jit(solution)/shard_map/all_to_all | solution.py:99
  701.0 548.0 %all-reduce.35.cloned.1.call-start = ((), (), s32[]{:S(2)}) async-start(), calls=%async_computation.5 | async-start | bytes 28606464
  742.7 16.8 %copy-start.11 = (f32[16,343,96]{1,2,0:T(8,128)}, f32[16,343,96]{1,2,0:T(8,128)S(1)}, u32[]{:S(2)}) copy-start(f32[16,343,96]{1,2,0:T(8,128)S(1)} %get-tuple-element.59) | copy-start | bytes 6322180
  763.6 19.4 %copy-start.49 = (f32[16,6,343]{2,1,0:T(8,128)S(1)}, f32[16,6,343]{2,1,0:T(8,128)}, u32[]{:S(2)}) copy-start(f32[16,6,343]{2,1,0:T(8,128)} %log_add_fusion.1) | copy-start | bytes 395140
  801.7 132.5 %copy-start.32 = (bf16[16,6,16,343]{3,2,1,0:T(8,128)(2,1)}, bf16[16,6,16,343]{3,2,1,0:T(8,128)(2,1)S(1)}, u32[]{:S(2)}) copy-start(bf16[16,6,16,343]{3,2,1,0:T(8,128)(2,1)S(1)} %fusion.87) | copy-start | bytes 3161092
  801.7 63.8 %copy-start.50 = (f32[16,6,343]{2,1,0:T(8,128)S(1)}, f32[16,6,343]{2,1,0:T(8,128)}, u32[]{:S(2)}) copy-start(f32[16,6,343]{2,1,0:T(8,128)} %log_add_fusion.1) | copy-start | bytes 395140
  865.5 64.0 %copy-start.8 = (bf16[16,1,343,96]{2,3,1,0:T(8,128)(2,1)S(1)}, bf16[16,1,343,96]{2,3,1,0:T(8,128)(2,1)}, u32[]{:S(2)}) copy-start(bf16[16,1,343,96]{2,3,1,0:T(8,128)(2,1)} %param.8) | copy-start | bytes 3161092
  865.6 64.0 %copy-start.71 = (f32[16,343]{1,0:T(8,128)S(1)}, f32[16,343]{1,0:T(8,128)}, u32[]{:S(2)}) copy-start(f32[16,343]{1,0:T(8,128)} %copy-done.70) | copy-start | bytes 65860
  865.6 64.0 %copy-start.77 = (f32[16,343]{1,0:T(8,128)S(1)}, f32[16,343]{1,0:T(8,128)}, u32[]{:S(2)}) copy-start(f32[16,343]{1,0:T(8,128)} %copy-done.76) | copy-start | bytes 65860
  865.6 64.0 %copy-start.129 = (f32[96]{0:T(128)S(1)}, f32[96]{0:T(128)}, u32[]{:S(2)}) copy-start(f32[96]{0:T(128)} %copy-done.128) | copy-start | bytes 1156
  865.6 64.0 %copy-start.134 = (f32[96]{0:T(128)S(1)}, f32[96]{0:T(128)}, u32[]{:S(2)}) copy-start(f32[96]{0:T(128)} %copy-done.133) | copy-start | bytes 1156
  1005.8 244.4 %copy-start.105 = (f32[6984]{0:T(1024)S(1)}, f32[6984]{0:T(1024)}, u32[]{:S(2)}) copy-start(f32[6984]{0:T(1024)} %param.13) | copy-start | bytes 83812
  1005.8 244.4 %copy-start.116 = (f32[6984]{0:T(1024)S(1)}, f32[6984]{0:T(1024)}, u32[]{:S(2)}) copy-start(f32[6984]{0:T(1024)} %param.14) | copy-start | bytes 83812
  1005.8 244.4 %copy-start.117 = (f32[6984]{0:T(1024)S(1)}, f32[6984]{0:T(1024)}, u32[]{:S(2)}) copy-start(f32[6984]{0:T(1024)} %param.15) | copy-start | bytes 83812
  (107 other events, 442.1 us)
Sparse Core Ops, SparseCore 0:
  13.9 128.5 all-reduce.32
  999.1 249.8 all-reduce.34
where the time goes:
time: 1260 us
  matrix products  488 us (39%)
  waiting for transfers between devices  395 us (31%)
  local copies, waits for them, and re-layouts  192 us (15%)
  other arithmetic  138 us (11%)
  starting transfers between devices  17.8 us (1%)
  between operations  17.2 us (1%)
    unnamed x4, waiting for transfers between devices  337 us
    dot_general x2, matrix products, layer_backward(): jnp.einsum('mhqk,mqhd->mkhd', grad_raw, queries, preferred_element_type=j...  128 us
    dot_general x2, matrix products, layer_backward(): jnp.einsum('mhqk,mkhd->mqhd', grad_raw, key_heads, preferred_element_type...  128 us
    all_to_all x4, waiting for transfers between devices, exchange_roll(): lax.all_to_all(outgoing, 'win', split_axis=0, concat_axis=0, tiled=True)  57.6 us
    unnamed x329, local copies, waits for them, and re-layouts  56.9 us
    dot_general x2, matrix products, score_matrix(): jnp.einsum('mqhd,mkhd->mhqk', queries, key_heads, preferred_element_type=...  45.7 us
    convert_element_type x2, other arithmetic, layer_forward(): active = active.astype(jnp.bfloat16)  40.5 us
    reduce_sum x2, other arithmetic, layer_forward(): denominator = jnp.sum(raised, axis=-1, keepdims=True)  40.2 us
  transfers between devices with their start and end apart: 6, of which 6 were waited for; matrix products, arithmetic and copies ran while one was open for 7% of the time, Pallas kernels for 0%

commit v1 on v0

v1 whole, which is shorter than its diff:
```python
from types import SimpleNamespace

import jax
import jax.numpy as jnp
import numpy as np
from jax import lax
from jax.experimental import pallas as pl
from jax.experimental.pallas import tpu as pltpu
from jax.sharding import PartitionSpec as P

C = 96
HEADS = 6
HEAD_DIM = 16
FF = 384
SIDE = 7
SHIFT = 3
WS = 343
STEP = 6
T = 384
CA = 128
BLOCK_ROWS = 1164

NORM_EPS = 1e-05
MASK_FILL = -1000000000.0
BETA_FIRST = 0.5
BETA_SECOND = 0.5
ADAM_EPS = 1e-08
RATE_MATRIX = 0.1
RATE_VECTOR = 0.4
DECAY_MATRIX = 0.05

BF = jnp.bfloat16
F32 = jnp.float32
NN = (((1,), (0,)), ((), ()))
NT = (((1,), (1,)), ((), ()))
BY_STEP, WHOLE, SMEM = -1, -2, -3
VOL, WIN = "vol", "win"


def octant_bits(octant):
    return (octant >> 2 & 1, octant >> 1 & 1, octant & 1)


OCT_SIZE = []
OCT_LEN = []
OCT_OFF = []
for _octant in range(8):
    _size = 1
    for _bit in octant_bits(_octant):
        _size *= SHIFT if _bit else SIDE - SHIFT
    OCT_OFF.append(sum(OCT_LEN))
    OCT_SIZE.append(_size)
    OCT_LEN.append(-(-_size // 16) * 16)


def slot_tables():
    perm = np.zeros((T, T), np.float32)
    order = np.zeros((T, WS), np.float32)
    rolled = np.full((T, 4), 99, np.int32)
    plain = np.full((T, 4), 99, np.int32)
    plain[:, 3] = 0
    for octant in range(8):
        bits = octant_bits(octant)
        lens = [SHIFT if bit else SIDE - SHIFT for bit in bits]
        rolled[OCT_OFF[octant] : OCT_OFF[octant] + OCT_LEN[octant], 3] = octant
        for i in range(lens[0]):
            for j in range(lens[1]):
                for k in range(lens[2]):
                    source = [v if bit else v + SHIFT for v, bit in zip((i, j, k), bits)]
                    q = OCT_OFF[octant] + (i * lens[1] + j) * lens[2] + k
                    t = (source[0] * SIDE + source[1]) * SIDE + source[2]
                    perm[q, t] = 1
                    own = [v + bit * (SIDE - SHIFT) for v, bit in zip((i, j, k), bits)]
                    order[q, (own[0] * SIDE + own[1]) * SIDE + own[2]] = 1
                    rolled[q, :3] = source
    for i in range(SIDE):
        for j in range(SIDE):
            for k in range(SIDE):
                plain[(i * SIDE + j) * SIDE + k, :3] = (i, j, k)
    return perm, order, plain, rolled


PERM, ORDER, PLAIN, ROLLED = slot_tables()


def dot(a, b, dims=NN):
    return lax.dot_general(a, b, dims, preferred_element_type=F32)


def wide(column):
    return jnp.concatenate([column] * (T // 128), axis=1)


def ln_stats(x):
    centred = x - jnp.mean(x, axis=0, keepdims=True)
    scale = lax.rsqrt(jnp.mean(centred * centred, axis=0, keepdims=True) + NORM_EPS)
    return centred * scale, scale


def norm_back(e, z, scale, gain):
    eg = e * gain
    return scale * (
        eg - jnp.mean(eg, axis=0, keepdims=True) - z * jnp.mean(eg * z, axis=0, keepdims=True)
    )


def gelu_pair(h):
    base = 1.0 + (0.3275911 * 0.7071067811865476) * jnp.abs(h)
    t = pl.reciprocal(base, approx=True)
    t = t * (2.0 - base * t)
    poly = t * (
        0.5 * 0.254829592
        + t
        * (
            0.5 * -0.284496736
            + t * (0.5 * 1.421413741 + t * (0.5 * -1.453152027 + t * (0.5 * 1.061405429)))
        )
    )
    bell = jnp.exp(-0.5 * (h * h))
    tail = poly * bell
    phi = jnp.where(h < 0.0, tail, 1.0 - tail)
    return h * phi, phi + h * bell * 0.3989422804014327


def ones_row(shape, row=0):
    return jnp.where(lax.broadcasted_iota(jnp.int32, shape, 0) == row, 1.0, 0.0)


def init_forward(r, sc):
    sc.qb[...] = jnp.zeros((CA, HEADS * T), BF)
    for h in range(HEADS):
        sc.vt[h, 16:32, :] = ones_row((16, T)).astype(BF)
        turned = dot(r.order[...], r.table[0, h], NT).astype(BF)
        sc.bias[h] = dot(turned, r.order[...], NT)


def init_backward(sc):
    sc.dab[...] = jnp.zeros((CA, HEADS * T), BF)
    sc.rb[...] = jnp.zeros((2 * C, 2 * HEADS * T), BF)
    for name, (shape, dtype) in GRADS.items():
        getattr(sc, name)[...] = jnp.zeros(shape, dtype)


def set_queries(sc, queries):
    for h in range(HEADS):
        sc.qb[16 * h : 16 * h + 16, T * h : T * h + T] = queries[16 * h : 16 * h + 16, :]


def forward_attention(sc, w, x, code_row):
    z, _ = ln_stats(x)
    sc.n1aug[C:CA, :] = ones_row((CA - C, T)).astype(BF)
    sc.attaug[C:CA, :] = ones_row((CA - C, T)).astype(BF)
    sc.n1aug[0:C, :] = (z * wide(w.vec[0]) + wide(w.vec[1])).astype(BF)
    qkv = dot(w.qkvT[...], sc.n1aug[...])
    queries = qkv[0:C].astype(BF)
    set_queries(sc, queries)
    sc.qT[...] = queries
    sc.kT[...] = qkv[C : 2 * C].astype(BF)
    values = qkv[2 * C :].astype(BF)
    for h in range(HEADS):
        sc.vt[h, 0:16, :] = values[16 * h : 16 * h + 16, :]
    kv = dot(sc.n1aug[...].T, w.kv[...]).astype(BF)
    sc.kn[...] = kv[:, 0:CA]
    sc.vn[...] = kv[:, CA:]
    eye = lax.broadcasted_iota(jnp.int32, (128, 128), 0) == lax.broadcasted_iota(
        jnp.int32, (128, 128), 1
    )
    tops = [None] * HEADS

    def scores(h, c):
        rows = slice(128 * c, 128 * c + 128)
        x_all = dot(sc.kn[rows], sc.qb[:, T * h : T * h + T])
        codes = sc.codes[rows]
        parts = []
        for j in range(3):
            lanes = slice(128 * j, 128 * j + 128)
            allowed = codes == code_row[:, lanes]
            if j == c:
                allowed = allowed | eye
            part = jnp.where(allowed, x_all[:, lanes] + sc.bias[h, rows, lanes], MASK_FILL)
            sc.s[h % 3, rows, lanes] = part
            parts.append(jnp.max(part.reshape(16, 8, 128), axis=0))
        top = jnp.concatenate(parts, axis=1)
        tops[h] = top if tops[h] is None else jnp.maximum(tops[h], top)

    def raise_(h, c):
        rows = slice(128 * c, 128 * c + 128)
        sc.e[rows, T * h : T * h + T] = jnp.exp(sc.s[h % 3, rows] - tops[h]).astype(BF)

    def attend(h):
        out = dot(sc.vt[h], sc.e[:, T * h : T * h + T])
        inverse = 1.0 / out[16:17]
        part = out[0:16] * inverse
        sc.att[16 * h : 16 * h + 16, :] = part
        sc.inv[h : h + 1, :] = inverse
        sc.attaug[16 * h : 16 * h + 16, :] = part.astype(BF)

    for h in range(HEADS + 3):
        for c in range(3):
            if h < HEADS:
                scores(h, c)
            if 0 <= h - 1 < HEADS:
                raise_(h - 1, c)
            if c == 0 and 0 <= h - 2 < HEADS:
                attend(h - 2)
        if h < HEADS:
            tops[h] = jnp.max(tops[h], axis=0, keepdims=True)
    return dot(w.projT[...], sc.attaug[...])


def backward_attention(sc, w, d_mid, z, scale, shifted):
    db = d_mid.astype(BF)
    sc.gproj[...] += dot(sc.attaug[...], db, NT)
    d_att = dot(w.proj[...], db).astype(BF).astype(F32)
    row = lax.broadcasted_iota(jnp.int32, (16, T), 0)
    for h in range(HEADS):
        part = (d_att[16 * h : 16 * h + 16] * sc.inv[h : h + 1, :]).astype(BF)
        cols = slice(T * h, T * h + T)
        sc.dab[16 * h : 16 * h + 16, cols] = part
        sc.rb[C + 16 * h : C + 16 * h + 16, 2 * T * h : 2 * T * h + T] = part
        sc.rb[16 * h : 16 * h + 16, 2 * T * h + T : 2 * T * h + 2 * T] = sc.qT[
            16 * h : 16 * h + 16, :
        ]
        inner = -jnp.sum(
            part.astype(F32) * sc.att[16 * h : 16 * h + 16, :], axis=0, keepdims=True
        )
        high = inner.astype(BF).astype(F32)
        low = inner - high
        sc.dab[C : C + 16, cols] = jnp.where(
            row == 0, high, jnp.where(row == 1, low, 0.0)
        ).astype(BF)
    total = None

    def soft(h):
        cols = slice(T * h, T * h + T)
        pull = dot(sc.vn[...], sc.dab[:, cols])
        sc.ds[:, cols] = (pull * sc.e[:, cols].astype(F32)).astype(BF)

    def to_queries(h):
        sc.dq[16 * h : 16 * h + 16, :] = dot(
            sc.kT[16 * h : 16 * h + 16, :], sc.ds[:, T * h : T * h + T]
        ).astype(BF)

    for h in range(HEADS + 1):
        if h < HEADS:
            soft(h)
        if h > 0:
            cols = slice(T * (h - 1), T * h)
            to_queries(h - 1)
            both = jnp.concatenate([sc.e[:, cols], sc.ds[:, cols]], axis=1)
            term = dot(both, sc.rb[:, 2 * T * (h - 1) : 2 * T * h], NT)
            total = term if total is None else total + term
    dkv = total.astype(BF)
    dq = sc.dq[...]
    sc.gkv[...] += dot(sc.n1aug[...], dkv)
    sc.gq[...] += dot(dq, sc.n1aug[...], NT)
    dn = dot(w.q[...], dq) + dot(w.kv96[...], dkv, NT)
    if shifted:
        dn = dn.astype(BF).astype(F32)
    sc.gvec[0] += dn * z
    sc.gvec[1] += dn
    return d_mid + norm_back(dn, z, scale, wide(w.vec[0]))


def feed_forward_back(sc, w, d, dd, z, scale):
    sc.gdown[...] += dot(sc.act[...], dd, NT)
    sc.gup[...] += dot(sc.dh[...], sc.n2aug[...], NT)
    sc.gvec[4] += dd.astype(F32)
    dn = dot(w.up[...], sc.dh[...])
    sc.gvec[2] += dn * z
    sc.gvec[3] += dn
    return d + norm_back(dn, z, scale, wide(w.vec[2]))


def write_grads(sc, out):
    gq = sc.gq[...].T
    gkv = sc.gkv[...]
    gup = sc.gup[...].T
    out[pl.ds(0, C, 3), :] = gq[0:C]
    out[pl.ds(1, C, 3), :] = gkv[0:C, 0:C]
    out[pl.ds(2, C, 3), :] = gkv[0:C, C : 2 * C]
    out[3 * C : 4 * C, :] = sc.gproj[0:C, :]
    for j in range(4):
        out[pl.ds(4 * C + j, C, 4), :] = gup[0:C, C * j : C * j + C]
    out[8 * C : 12 * C, :] = sc.gdown[...]
    sums = [jnp.sum(sc.gvec[n].T, axis=0, keepdims=True) for n in range(5)]
    rows = [
        sums[0],
        sums[1],
        gq[C : C + 1],
        gkv[C : C + 1, C : 2 * C],
        sc.gproj[C : C + 1, :],
        sums[2],
        sums[3],
        sums[4],
    ] + [gup[C : C + 1, C * j : C * j + C] for j in range(4)]
    for n, value in enumerate(rows):
        out[12 * C + n : 12 * C + n + 1, :] = value


FWD = dict(
    qb=((CA, HEADS * T), BF),
    vt=((HEADS, 32, T), BF),
    kn=((T, CA), BF),
    codes=((T, 128), F32),
    bias=((HEADS, T, T), F32),
    s=((3, T, T), F32),
)
KEPT = dict(
    qT=((C, T), BF),
    kT=((C, T), BF),
    vn=((T, CA), BF),
    e=((T, HEADS * T), BF),
    att=((C, T), F32),
    inv=((8, T), F32),
    attaug=((CA, T), BF),
    n1aug=((CA, T), BF),
    n2aug=((CA, T), BF),
    act=((FF, T), BF),
    gp=((FF, T), BF),
    xT=((C, T), F32),
    x1=((C, T), F32),
)
GRADS = dict(
    gq=((C, CA), F32),
    gkv=((CA, 2 * C), F32),
    gproj=((CA, C), F32),
    gup=((FF, CA), F32),
    gdown=((FF, C), F32),
    gvec=((5, C, T), F32),
)
BWD = dict(
    **GRADS,
    dab=((CA, HEADS * T), BF),
    rb=((2 * C, 2 * HEADS * T), BF),
    ds=((T, HEADS * T), BF),
    dq=((C, T), BF),
    dh=((FF, T), BF),
)


def by_step(r):
    return SimpleNamespace(**{**vars(r), **{n: getattr(r, n).at[0] for n in KEPT}})


def second_norm(sc, w, x):
    z, scale = ln_stats(x)
    sc.n2aug[C:CA, :] = ones_row((CA - C, T)).astype(BF)
    sc.n2aug[0:C, :] = (z * wide(w.vec[2]) + wide(w.vec[3])).astype(BF)
    return z, scale


def first_forward_kernel(r):
    w, sc = r, by_step(r)
    m = pl.program_id(0)

    @pl.when(m == 0)
    def _():
        init_forward(r, sc)
        sc.pad[...] = jnp.zeros((2, T, C), BF)

    sc.pad[0, 0:WS, :] = r.tokens[0, 0]
    sc.pad[1, 0:WS, :] = r.cotangent[0, 0]
    r.sent_cot[0] = dot(r.perm[...], sc.pad[1]).astype(BF)
    place = r.place
    valid = (
        (place[0] < r.info[m, 1]) & (place[1] < r.info[m, 2]) & (place[2] < r.info[m, 3])
    )
    sc.codes[...] = jnp.where(valid, 0.0, -1.0)
    x = dot(r.eye[...], sc.pad[0], NT)
    sc.xT[...] = x
    x = x + forward_attention(sc, w, x, jnp.zeros((1, T), F32))
    sc.x1[...] = x
    second_norm(sc, w, x)
    for c in range(3):
        rows = slice(128 * c, 128 * c + 128)
        active, slope = gelu_pair(dot(w.upT[rows], sc.n2aug[...]))
        sc.act[rows, :] = active.astype(BF)
        sc.gp[rows, :] = slope.astype(BF)
    x = x + (dot(w.downT[...], sc.act[...]) + wide(w.vec[4]))
    r.sent_x[0] = dot(r.perm[...], x.astype(BF), NT).astype(BF)


def second_kernel(r):
    w, sc = r, r
    m = pl.program_id(0)

    @pl.when(m == 0)
    def _():
        init_forward(r, sc)
        init_backward(sc)

    place, rows4 = r.place, r.places
    octant_row = rows4[3:4, :]
    label_row = jnp.zeros((1, T), F32)
    ends = [jnp.zeros((1, T), jnp.int32)] * 3
    for o in range(8):
        rows = slice(OCT_OFF[o], OCT_OFF[o] + OCT_LEN[o])
        item = [r.info[m, 4 * o + n] for n in range(4)]
        label = item[0].astype(F32)
        valid = (
            (place[0, rows] < item[1]) & (place[1, rows] < item[2]) & (place[2, rows] < item[3])
        )
        sc.codes[rows, :] = jnp.where(valid, label, -1.0)
        here = octant_row == o
        label_row = jnp.where(here, label, label_row)
        ends = [jnp.where(here, item[n + 1], ends[n]) for n in range(3)]
    keep = jnp.where(
        (rows4[0:1, :] < ends[0]) & (rows4[1:2, :] < ends[1]) & (rows4[2:3, :] < ends[2]), 1.0, 0.0
    )
    x = dot(r.eye[...], r.got_x[0], NT)
    d = dot(r.eye[...], r.got_cot[0], NT) * keep
    dd = d.astype(BF)
    sc.xT[...] = x
    branch = forward_attention(sc, w, x, label_row)
    x = x + branch.astype(BF).astype(F32)
    z, scale = second_norm(sc, w, x)
    for c in range(3):
        rows = slice(128 * c, 128 * c + 128)
        active, slope = gelu_pair(dot(w.upT[rows], sc.n2aug[...]))
        sc.act[rows, :] = active.astype(BF)
        sc.dh[rows, :] = (dot(w.down[rows], dd) * slope).astype(BF)
    x = x + (dot(w.downT[...], sc.act[...]) + wide(w.vec[4]))
    r.sent_out[0] = (x * keep).T.astype(BF)
    d = feed_forward_back(sc, w, d, dd, z, scale)
    z, scale = ln_stats(sc.xT[...])
    d = backward_attention(sc, w, d, z, scale, True)
    r.sent_d[0] = d.T.astype(BF)

    @pl.when(m == pl.num_programs(0) - 1)
    def _():
        write_grads(sc, r.grads)


def first_backward_kernel(r):
    w, sc = r, by_step(r)
    m = pl.program_id(0)

    @pl.when(m == 0)
    def _():
        init_backward(sc)

    r.output[0, 0] = dot(r.perm_back[...], r.got_out[0]).astype(BF)[0:WS]
    d = dot(dot(r.eye[...], r.got_d[0], NT).astype(BF), r.perm[...])
    dd = d.astype(BF)
    z, scale = ln_stats(sc.x1[...])
    for c in range(3):
        rows = slice(128 * c, 128 * c + 128)
        sc.dh[rows, :] = (dot(w.down[rows], dd) * sc.gp[rows, :].astype(F32)).astype(BF)
    d = feed_forward_back(sc, w, d, dd, z, scale)
    z, scale = ln_stats(sc.xT[...])
    d = backward_attention(sc, w, d, z, scale, False)
    r.input_grad[0, 0] = d.T[0:WS]

    @pl.when(m == pl.num_programs(0) - 1)
    def _():
        write_grads(sc, r.grads)


def call(kernel, steps, ins, outs, scratch):
    def spec(shape, kind):
        if kind is SMEM:
            return pl.BlockSpec(memory_space=pltpu.SMEM)
        zeros = (0,) * (len(shape) - 1)
        if kind is BY_STEP:
            return pl.BlockSpec((1,) + tuple(shape[1:]), lambda m: (m,) + zeros)
        if kind in (0, 1):
            return pl.BlockSpec((1,) + tuple(shape[1:]), lambda m: (kind,) + zeros)
        return pl.BlockSpec(tuple(shape), lambda m: (0,) + zeros)

    names = tuple(ins) + tuple(outs) + tuple(scratch)

    def body(*refs):
        kernel(SimpleNamespace(**dict(zip(names, refs))))

    results = pl.pallas_call(
        body,
        grid=(steps,),
        in_specs=[spec(a.shape, kind) for a, kind in ins.values()],
        out_specs=[spec(shape, kind) for shape, _, kind in outs.values()],
        out_shape=[jax.ShapeDtypeStruct(shape, dtype) for shape, dtype, _ in outs.values()],
        scratch_shapes=[pltpu.VMEM(shape, dtype) for shape, dtype in scratch.values()],
        compiler_params=pltpu.CompilerParams(vmem_limit_bytes=60 * 2**20),
    )(*[a for a, _ in ins.values()])
    return SimpleNamespace(**dict(zip(outs, results)))


def layer_operands(params, which_layer):
    rows = params[which_layer * BLOCK_ROWS : (which_layer + 1) * BLOCK_ROWS]
    wq, wk, wv = (rows[0 : 3 * C].reshape(C, 3, C)[:, n] for n in range(3))
    proj = rows[3 * C : 4 * C]
    up = rows[4 * C : 8 * C].reshape(C, FF)
    down = rows[8 * C : 12 * C]
    vectors = rows[12 * C : 12 * C + 8]
    bias_up = rows[12 * C + 8 :].reshape(FF)
    gain1, offset1, bias_q, bias_v, bias_proj, gain2, offset2, bias_down = vectors
    quarter = jnp.asarray(0.25, BF)

    def aug(matrix, bias):
        return jnp.concatenate(
            [matrix, bias[:, None], jnp.zeros((matrix.shape[0], CA - C - 1), BF)], axis=1
        )

    none = jnp.zeros((C,), BF)
    kn = aug(wk.T, none).T
    vn = jnp.concatenate([aug(wv.T, bias_v).T, jnp.zeros((CA, CA - C), BF)], axis=1)
    vn = vn.at[C, C : C + 2].set(1.0)
    kn = jnp.concatenate([kn, jnp.zeros((CA, CA - C), BF)], axis=1)
    columns = jnp.stack([gain1, offset1, gain2, offset2, bias_down]).astype(F32)
    return dict(
        qkvT=jnp.concatenate(
            [aug(wq.T * quarter, bias_q * quarter), aug(wk.T * quarter, none), aug(wv.T, bias_v)]
        ),
        kv=jnp.concatenate([kn, vn], axis=1),
        projT=aug(proj.T, bias_proj),
        proj=proj,
        upT=aug(up.T, bias_up),
        up=up,
        downT=down.T,
        down=down,
        q=wq,
        kv96=jnp.concatenate([wk, wv], axis=1),
        vec=jnp.broadcast_to(columns[:, :, None], (5, C, 128)),
    )


def exchange(x, forward, groups_a):
    sign = -1 if forward else 1
    blocks = []
    for octant in range(8):
        part = x[:, OCT_OFF[octant] : OCT_OFF[octant] + OCT_LEN[octant]]
        if octant:
            bits = octant_bits(octant)
            pairs = []
            for w in range(4 * groups_a):
                place = (w // 4, w // 2 % 2, w % 2)
                a, b, c = (
                    (p + sign * bit) % n for p, bit, n in zip(place, bits, (groups_a, 2, 2))
                )
                pairs.append((w, (a * 2 + b) * 2 + c))
            part = lax.ppermute(part, WIN, pairs)
        blocks.append(part)
    return jnp.concatenate(blocks, axis=1)


def octant_info(group_info, groups_a):
    index_win = lax.axis_index(WIN)
    place = (index_win // 4, index_win // 2 % 2, index_win % 2)
    items = []
    for octant in range(8):
        bits = octant_bits(octant)
        a, b, c = ((p + bit) % n for p, bit, n in zip(place, bits, (groups_a, 2, 2)))
        wraps = [
            bit * (p == n - 1).astype(jnp.int32) for p, bit, n in zip(place, bits, (groups_a, 2, 2))
        ]
        source = lax.dynamic_index_in_dim(group_info, (a * 2 + b) * 2 + c, 1, keepdims=False)
        code = wraps[0] * 4 + wraps[1] * 2 + wraps[2]
        items.append(source * jnp.array([8, 1, 1, 1]) + code * jnp.array([1, 0, 0, 0]))
    return jnp.concatenate(items, axis=1)


def on_device(
    tokens,
    cotangent,
    position_bias,
    window_volume,
    clip_extent,
    master,
    first_moment,
    second_moment,
):
    groups_a = lax.axis_size(WIN) // 4
    steps = tokens.shape[0]
    params = lax.all_gather(master.astype(BF), (VOL, WIN), axis=0, tiled=True)
    own_info = jnp.concatenate((window_volume[:, :, None], clip_extent), axis=2)
    group_info = lax.all_gather(own_info, WIN, axis=1, tiled=True)
    info = octant_info(group_info, groups_a)
    params = params.reshape(2 * BLOCK_ROWS, C)
    weights = [layer_operands(params, n) for n in range(2)]

    def whole(table):
        return {n: (a, WHOLE) for n, a in table.items()}

    def tables(which):
        place = (PLAIN, ROLLED)[which]
        order = (np.eye(T, WS), ORDER)[which]
        return dict(
            place=(jnp.asarray(np.broadcast_to(place.T[:3, :, None], (3, T, 128))), WHOLE),
            order=(jnp.asarray(order, BF), WHOLE),
            table=(position_bias, which),
            eye=(jnp.asarray(np.eye(C), BF), WHOLE),
        )

    perm = jnp.asarray(PERM, BF)
    got = call(
        first_forward_kernel,
        steps,
        dict(
            tokens=(tokens, BY_STEP),
            cotangent=(cotangent, BY_STEP),
            info=(own_info[:, 0], SMEM),
            perm=(perm, WHOLE),
            **tables(0),
            **whole(weights[0]),
        ),
        dict(
            sent_x=((steps, T, C), BF, BY_STEP),
            sent_cot=((steps, T, C), BF, BY_STEP),
            **{n: ((steps,) + shape, dtype, BY_STEP) for n, (shape, dtype) in KEPT.items()},
        ),
        dict(**FWD, pad=((2, T, C), BF)),
    )
    kept = {n: (getattr(got, n), BY_STEP) for n in KEPT}
    rows = np.zeros((8, T), np.int32)
    rows[:4] = ROLLED.T
    second = call(
        second_kernel,
        steps,
        dict(
            got_x=(exchange(got.sent_x, True, groups_a), BY_STEP),
            got_cot=(exchange(got.sent_cot, True, groups_a), BY_STEP),
            info=(info, SMEM),
            places=(jnp.asarray(rows), WHOLE),
            **tables(1),
            **whole(weights[1]),
        ),
        dict(
            sent_out=((steps, T, C), BF, BY_STEP),
            sent_d=((steps, T, C), BF, BY_STEP),
            grads=((BLOCK_ROWS, C), F32, WHOLE),
        ),
        dict(**FWD, **KEPT, **BWD),
    )
    first = call(
        first_backward_kernel,
        steps,
        dict(
            got_out=(exchange(second.sent_out, False, groups_a), BY_STEP),
            got_d=(exchange(second.sent_d, False, groups_a), BY_STEP),
            perm=(perm, WHOLE),
            perm_back=(jnp.asarray(PERM.T, BF), WHOLE),
            eye=(jnp.asarray(np.eye(C), BF), WHOLE),
            **kept,
            **whole(weights[0]),
        ),
        dict(
            output=((steps, 1, WS, C), BF, BY_STEP),
            input_grad=((steps, 1, WS, C), F32, BY_STEP),
            grads=((BLOCK_ROWS, C), F32, WHOLE),
        ),
        BWD,
    )
    all_grads = jnp.concatenate((first.grads, second.grads)).reshape(-1)
    shard_grad = lax.psum_scatter(all_grads, (VOL, WIN), scatter_dimension=0, tiled=True)
    shard_len = master.shape[0]
    position = (
        lax.axis_index((VOL, WIN)) * shard_len + jnp.arange(shard_len, dtype=jnp.int32)
    ) % (BLOCK_ROWS * C)
    is_vector = position >= 12 * C * C
    step_rate = jnp.where(is_vector, RATE_VECTOR, RATE_MATRIX)
    weight_decay = jnp.where(is_vector, 0.0, DECAY_MATRIX)
    moment_one = BETA_FIRST * first_moment + (1.0 - BETA_FIRST) * shard_grad
    moment_two = BETA_SECOND * second_moment + (1.0 - BETA_SECOND) * shard_grad * shard_grad
    corrected_one = moment_one / (1.0 - BETA_FIRST**STEP)
    corrected_two = moment_two / (1.0 - BETA_SECOND**STEP)
    normalized = corrected_one / (jnp.sqrt(corrected_two) + ADAM_EPS)
    new_master = master - step_rate * (normalized + weight_decay * master)
    return (
        first.output,
        first.input_grad,
        new_master,
        moment_one,
        moment_two,
        new_master.astype(BF),
    )


def solution(mesh):
    placed = (
        P(None, (VOL, WIN), None, None),
        P(None, (VOL, WIN), None, None),
        P(),
        P(None, (VOL, WIN)),
        P(None, (VOL, WIN), None),
        P((VOL, WIN)),
        P((VOL, WIN)),
        P((VOL, WIN)),
    )
    return jax.shard_map(
        on_device,
        mesh=mesh,
        in_specs=placed,
        out_specs=(
            P(None, (VOL, WIN), None, None),
            P(None, (VOL, WIN), None, None),
            P((VOL, WIN)),
            P((VOL, WIN)),
            P((VOL, WIN)),
            P((VOL, WIN)),
        ),
        check_vma=False,
    )
```

time: 1260 us -> 664 us (0.53)
  matrix products: 488 us -> 0 us
  Pallas kernels: 0 us -> 236 us
  local copies, waits for them, and re-layouts: 192 us -> 59.6 us
  other arithmetic: 138 us -> 15 us
  waiting for transfers between devices: 395 us -> 295 us
  starting transfers between devices: 17.8 us -> 32.7 us
    dot_general x36 -> x0, matrix products: 488 us -> none  [the longest x2 128 us: layer_backward(): jnp.einsum('mhqk,mqhd->mkhd', grad_raw, queries, preferred_element_type=j...]
    pallas_call x0 -> x3, Pallas kernels: none -> 236 us  [call(): pl.pallas_call(body, grid=(steps,), in_specs=[spec(a.shape, kind) for a,...]
    unnamed x4, waiting for transfers between devices: 337 us -> 235 us
    reduce_sum x22 -> x0, other arithmetic: 68 us -> none  [the longest x2 40.2 us: layer_forward(): denominator = jnp.sum(raised, axis=-1, keepdims=True)]
    ppermute x0 -> x28, waiting for transfers between devices: none -> 59.4 us  [exchange(): part = lax.ppermute(part, WIN, pairs)]
    all_to_all x4 -> x0, waiting for transfers between devices: 57.6 us -> none  [exchange_roll(): lax.all_to_all(outgoing, 'win', split_axis=0, concat_axis=0, tiled=True)]
    convert_element_type x13 -> x2, other arithmetic: 52.4 us -> 2.23 us  [the longest x1 1.48 us: on_device(): new_master.astype(BF)]
    unnamed x329 -> x101, local copies, waits for them, and re-layouts: 56.9 us -> 22.9 us
  transfers between devices with their start and end apart: 6 -> 30, of which waited for: 6 -> 15; matrix products, arithmetic and copies ran while one was open for 7% -> 6% of each run, Pallas kernels for 0% -> 0%
where the time goes in v1:
time: 664 us; the launch traced here: 663 us
  waiting for transfers between devices  295 us (44%)
  Pallas kernels  236 us (36%)
  local copies, waits for them, and re-layouts  59.6 us (9%)
  starting transfers between devices  32.7 us (5%)
  other arithmetic  15 us (2%)
  between operations  15 us (2%)
  blocking collectives  10.3 us (2%)
    pallas_call x3, Pallas kernels, call(): pl.pallas_call(body, grid=(steps,), in_specs=[spec(a.shape, kind) for a,...  236 us
    unnamed x4, waiting for transfers between devices  235 us
    ppermute x28, waiting for transfers between devices, exchange(): part = lax.ppermute(part, WIN, pairs)  59.4 us
    ppermute x28, starting transfers between devices, exchange(): part = lax.ppermute(part, WIN, pairs)  32.6 us
    unnamed x101, local copies, waits for them, and re-layouts  22.9 us
  transfers between devices with their start and end apart: 30, of which 15 were waited for; matrix products, arithmetic and copies ran while one was open for 6% of the time, Pallas kernels for 0%

profile of v1, /device:TPU:0, one launch (start us, length us, event | category | flops | bytes accessed | tf_op | source)
XLA Modules:
  0.0 662.9 jit_solution(268926649304002248)
XLA Ops:
  12.8 10.3 %all_gather.7 = s32[16,8,4]{0,2,1:T(4,128)S(1)} all-gather(s32[16,1,4]{0,2,1:T(4,128)S(1)} %pad_add_fusion), channel_id=1, replica_groups=mesh['vol'=4,'win'=8] {'win'}, dimensions={1}, use_global_device_ids=true | all-gather | bytes 2304 | tf_op jit(solution)/shard_map/all_gather | solution.py:576
  23.8 2.6 copy.182.refs_0_
  26.4 2.5 copy.183.refs_1_
  29.0 2.1 copy.185.refs_6_
  31.8 110.7 %all-reduce.7.cloned.1.call-done = bf16[223488]{0:T(1024)(128)(2,1)} async-done(((bf16[223488]{0:T(1024)(128)(2,1)}), bf16[223488]{0:T(1024)(128)(2,1)}) %all-reduce.7.cloned.1.call-update) | async-done | bytes 446992
  146.2 1.5 fusion.21
  148.6 1.9 slice_bitcast_fusion
  157.0 60.8 %shard_map.357 = (bf16[16,384,96]{2,1,0:T(8,128)(2,1)}, bf16[16,384,96]{2,1,0:T(8,128)(2,1)}, bf16[16,96,384]{2,1,0:T(8,128)(2,1)}, bf16[16,96,384]{2,1,0:T(8,12...) custom-call(bf16[16,1,343,96]{3,2,1,0:T(8,128)(2,1)} %copy.182.refs_, ...), custom_call_target="tpu_custom_call" | custom-call | tf_op jit(solution)/shard_map/pallas_call | solution.py:476
  217.8 2.5 fusion.17
  228.0 1.5 collective-permute-start.1
  230.3 1.5 pad_maximum_fusion.6
  231.8 1.5 maximum_maximum_fusion.3.refs_8_
  234.5 1.6 slice.346
  236.1 1.6 slice.354
  237.8 1.6 copy.220.refs_9_
  239.4 1.5 copy.224.refs_17_
  241.6 1.4 copy.221.refs_10_
  244.9 1.5 collective-permute-start.6
  246.5 1.5 collective-permute-start.5
  252.1 8.8 %collective-permute-done.2 = bf16[16,48,96]{2,1,0:T(8,128)(2,1)S(1)} collective-permute-done((bf16[16,48,96]{2,1,0:T(8,128)(2,1)}, bf16[16,48,96]{2,1,0:T(8,128)(2,1)S(1)}, u32[]{:S(2)}, u32[]{:S(2)}) %collective-permute-start.2) | collective-permute-done | bytes 147488 | tf_op jit(solution)/shard_map/ppermute | solution.py:541
  262.3 1.5 collective-permute-start.12
  263.9 8.2 %collective-permute-done.4 = bf16[16,48,96]{2,1,0:T(8,128)(2,1)S(1)} collective-permute-done((bf16[16,48,96]{2,1,0:T(8,128)(2,1)}, bf16[16,48,96]{2,1,0:T(8,128)(2,1)S(1)}, u32[]{:S(2)}, u32[]{:S(2)}) %collective-permute-start.4) | collective-permute-done | bytes 147488 | tf_op jit(solution)/shard_map/ppermute | solution.py:541
  272.4 1.5 collective-permute-start.8
  275.1 5.1 collective-permute-done.8
  280.2 1.5 collective-permute-start.10
  283.0 1.7 collective-permute-start.11
  284.7 1.5 collective-permute-done.10
  286.2 3.6 collective-permute-done.11
  293.8 110.4 %shard_map.358 = (bf16[16,384,96]{2,1,0:T(8,128)(2,1)}, bf16[16,384,96]{2,1,0:T(8,128)(2,1)}, f32[1164,96]{1,0:T(8,128)}) custom-call(bf16[16,384,96]{2,1,0:T(8,128)(2,1)} %copy-done.3, bf16[16,384,96]{2,1,0:T(8,128)(2,1)} %copy-done.2, s32[16,32]{1,0:T(8,128)} %concatenate.108.refs_2_, s32[8,384]{1,0:T(8,128)} %constant.243.clone.refs_3_, ...), custom_call_target="tpu_custom_call" | custom-call | tf_op jit(solution)/shard_map/pallas_call | solution.py:476
  404.3 1.5 fusion.15
  406.8 1.5 collective-permute-start.15
  409.5 1.5 collective-permute-start.27
  412.2 1.5 collective-permute-start.19
  416.1 11.7 %collective-permute-done.16 = bf16[16,48,96]{2,1,0:T(8,128)(2,1)S(1)} collective-permute-done((bf16[16,48,96]{2,1,0:T(8,128)(2,1)S(1)}, bf16[16,48,96]{2,1,0:T(8,128)(2,1)S(1)}, u32[]{:S(2)}, u32[]{:S(2)}) %collective-permute-start.16) | collective-permute-done | bytes 147488 | tf_op jit(solution)/shard_map/ppermute | solution.py:541
  427.7 1.6 collective-permute-start.18
  429.4 1.5 collective-permute-start.26
  431.0 7.4 %collective-permute-done.18 = bf16[16,48,96]{2,1,0:T(8,128)(2,1)S(1)} collective-permute-done((bf16[16,48,96]{2,1,0:T(8,128)(2,1)S(1)}, bf16[16,48,96]{2,1,0:T(8,128)(2,1)S(1)}, u32[]{:S(2)}, u32[]{:S(2)}) %collective-permute-start.18) | collective-permute-done | bytes 147488 | tf_op jit(solution)/shard_map/ppermute | solution.py:541
  439.0 1.5 collective-permute-start.22
  441.5 5.3 collective-permute-done.22
  449.1 1.8 collective-permute-start.25
  451.0 1.8 collective-permute-done.24
  452.8 3.4 collective-permute-done.25
  457.9 64.5 %shard_map.359 = (bf16[16,1,343,96]{3,2,1,0:T(8,128)(2,1)}, f32[16,1,343,96]{3,2,1,0:T(8,128)}, f32[1164,96]{1,0:T(8,128)}) custom-call(bf16[16,384,96]{2,1,0:T(8,128)(2,1)} %copy-done.5, bf16[16,384,96]{2,1,0:T(8,128)(2,1)} %copy-done.4, bf16[384,384]{1,0:T(8,128)(2,1)} %constant.239.clone.refs_3_.refs_2_, bf16[384,384]{1,0:T(8,128)(2,1)} %constant.246.clone.refs_3_, ...), custom_call_target="tpu_custom_call" | custom-call | tf_op jit(solution)/shard_map/pallas_call | solution.py:476
  523.6 1.7 reshape.289
  525.3 2.6 copy.228
  528.0 2.2 copy.229
  530.1 124.5 %all-reduce.9.cloned.1.call-done = f32[223488]{0:T(1024)} async-done(((f32[223488]{0:T(1024)}), f32[223488]{0:T(1024)}) %all-reduce.9.cloned.1.call-update) | async-done | bytes 893968
  654.6 1.5 fusion.12
  (213 shorter events, 55.2 us)
Async XLA Ops:
  7.2 135.3 %all-reduce.7.cloned.1.call-start = ((), (), s32[]{:S(2)}) async-start(), calls=%async_computation | async-start | bytes 897024
  9.2 645.4 %all-reduce.9.cloned.1.call-start = ((), (), s32[]{:S(2)}) async-start(), calls=%async_computation.1 | async-start | bytes 1794048
  23.8 5.2 copy-start
  143.9 8.7 %copy-start.29 = (bf16[128]{0:T(256)(128)(2,1)S(1)}, bf16[128]{0:T(256)(128)(2,1)}, u32[]{:S(2)}) copy-start(bf16[128]{0:T(256)(128)(2,1)} %pad.41.clone) | copy-start | bytes 772
  144.0 8.7 %copy-start.15 = (bf16[96,96]{1,0:T(8,128)(2,1)}, bf16[96,96]{1,0:T(8,128)(2,1)S(1)}, u32[]{:S(2)}) copy-start(bf16[96,96]{1,0:T(8,128)(2,1)S(1)} %slice.360.refs_11_) | copy-start | bytes 55300
  144.1 8.6 %copy-start.14 = (bf16[96,96]{1,0:T(8,128)(2,1)}, bf16[96,96]{1,0:T(8,128)(2,1)S(1)}, u32[]{:S(2)}) copy-start(bf16[96,96]{1,0:T(8,128)(2,1)S(1)} %slice.333.refs_11_.refs_21_) | copy-start | bytes 55300
  145.2 10.7 %copy-start.10 = (bf16[96,384]{1,0:T(8,128)(2,1)}, bf16[96,384]{1,0:T(8,128)(2,1)S(1)}, u32[]{:S(2)}) copy-start(bf16[96,384]{1,0:T(8,128)(2,1)S(1)} %slice.335.refs_13_.refs_23_) | copy-start | bytes 221188
  145.3 10.7 %copy-start.12 = (bf16[96,384]{1,0:T(8,128)(2,1)}, bf16[96,384]{1,0:T(8,128)(2,1)S(1)}, u32[]{:S(2)}) copy-start(bf16[96,384]{1,0:T(8,128)(2,1)S(1)} %slice.362.refs_13_) | copy-start | bytes 221188
  145.3 10.6 %copy-start.25 = (s32[3,384]{1,0:T(4,128)S(1)}, s32[3,384]{1,0:T(4,128)}, u32[]{:S(2)}) copy-start(s32[3,384]{1,0:T(4,128)} %constant.240.clone) | copy-start | bytes 13828
  145.4 11.5 %copy-start.7 = (bf16[384,96]{1,0:T(8,128)(2,1)}, bf16[384,96]{1,0:T(8,128)(2,1)S(1)}, u32[]{:S(2)}) copy-start(bf16[384,96]{1,0:T(8,128)(2,1)S(1)} %slice.338.refs_15_.refs_25_) | copy-start | bytes 221188
  228.0 21.8 %collective-permute-start.1 = (bf16[16,48,96]{2,1,0:T(8,128)(2,1)}, bf16[16,48,96]{2,1,0:T(8,128)(2,1)}, u32[]{:S(2)}, u32[]{:S(2)}) collective-permute-start(bf16[16,48,96]{2,1,0:T(8,128)(2,1)} %get-tuple-element.126), channel_id=1, source_target_pairs={{0,2},{1,3},{2,0},{3,1},{4,6},{5,7},{6,4},{7,5},{8,10},{9,11},{10,... | collective-permute-start | bytes 442376 | tf_op jit(solution)/shard_map/ppermute | solution.py:541
  229.5 19.1 %collective-permute-start = (bf16[16,48,96]{2,1,0:T(8,128)(2,1)}, bf16[16,48,96]{2,1,0:T(8,128)(2,1)}, u32[]{:S(2)}, u32[]{:S(2)}) collective-permute-start(bf16[16,48,96]{2,1,0:T(8,128)(2,1)} %get-tuple-element.127), channel_id=1, source_target_pairs={{0,1},{1,0},{2,3},{3,2},{4,5},{5,4},{6,7},{7,6},{8,9},{9,8},{10,11... | collective-permute-start | bytes 442376 | tf_op jit(solution)/shard_map/ppermute | solution.py:541
  237.8 37.3 %copy-start.11 = (bf16[384,96]{1,0:T(8,128)(2,1)}, bf16[384,96]{1,0:T(8,128)(2,1)S(1)}, u32[]{:S(2)}) copy-start(bf16[384,96]{1,0:T(8,128)(2,1)S(1)} %slice.365.refs_15_) | copy-start | bytes 221188
  243.8 31.1 %copy-start.18 = (bf16[16,48,96]{2,1,0:T(8,128)(2,1)S(1)}, bf16[16,48,96]{2,1,0:T(8,128)(2,1)}, u32[]{:S(2)}) copy-start(bf16[16,48,96]{2,1,0:T(8,128)(2,1)} %get-tuple-element.119) | copy-start | bytes 442372
  243.8 46.9 %collective-permute-start.13 = (bf16[16,32,96]{2,1,0:T(8,128)(2,1)}, bf16[16,32,96]{2,1,0:T(8,128)(2,1)}, u32[]{:S(2)}, u32[]{:S(2)}) collective-permute-start(bf16[16,32,96]{2,1,0:T(8,128)(2,1)} %slice.354), channel_id=1, source_target_pairs={{0,7},{1,6},{2,5},{3,4},{4,3},{5,2},{6,1},{7,0},{8,15},{9,14},{10,... | collective-permute-start | bytes 294920 | tf_op jit(solution)/shard_map/ppermute | solution.py:541
  244.9 44.9 %collective-permute-start.6 = (bf16[16,32,96]{2,1,0:T(8,128)(2,1)}, bf16[16,32,96]{2,1,0:T(8,128)(2,1)}, u32[]{:S(2)}, u32[]{:S(2)}) collective-permute-start(bf16[16,32,96]{2,1,0:T(8,128)(2,1)} %slice.346), channel_id=1, source_target_pairs={{0,7},{1,6},{2,5},{3,4},{4,3},{5,2},{6,1},{7,0},{8,15},{9,14},{10,... | collective-permute-start | bytes 294920 | tf_op jit(solution)/shard_map/ppermute | solution.py:541
  246.5 25.9 %collective-permute-start.5 = (bf16[16,48,96]{2,1,0:T(8,128)(2,1)}, bf16[16,48,96]{2,1,0:T(8,128)(2,1)}, u32[]{:S(2)}, u32[]{:S(2)}) collective-permute-start(bf16[16,48,96]{2,1,0:T(8,128)(2,1)} %get-tuple-element.122), channel_id=1, source_target_pairs={{0,6},{1,7},{2,4},{3,5},{4,2},{5,3},{6,0},{7,1},{8,14},{9,15},{10,... | collective-permute-start | bytes 442376 | tf_op jit(solution)/shard_map/ppermute | solution.py:541
  248.6 23.4 %copy-start.20 = (bf16[16,48,96]{2,1,0:T(8,128)(2,1)S(1)}, bf16[16,48,96]{2,1,0:T(8,128)(2,1)}, u32[]{:S(2)}) copy-start(bf16[16,48,96]{2,1,0:T(8,128)(2,1)} %get-tuple-element.121) | copy-start | bytes 442372
  248.6 23.8 %copy-start.19 = (bf16[16,48,96]{2,1,0:T(8,128)(2,1)S(1)}, bf16[16,48,96]{2,1,0:T(8,128)(2,1)}, u32[]{:S(2)}) copy-start(bf16[16,48,96]{2,1,0:T(8,128)(2,1)} %get-tuple-element.120) | copy-start | bytes 442372
  248.7 34.3 %copy-start.17 = (bf16[16,48,96]{2,1,0:T(8,128)(2,1)S(1)}, bf16[16,48,96]{2,1,0:T(8,128)(2,1)}, u32[]{:S(2)}) copy-start(bf16[16,48,96]{2,1,0:T(8,128)(2,1)} %get-tuple-element.117) | copy-start | bytes 442372
  248.7 12.2 %collective-permute-start.2 = (bf16[16,48,96]{2,1,0:T(8,128)(2,1)}, bf16[16,48,96]{2,1,0:T(8,128)(2,1)S(1)}, u32[]{:S(2)}, u32[]{:S(2)}) collective-permute-start(bf16[16,48,96]{2,1,0:T(8,128)(2,1)} %get-tuple-element.125), channel_id=1, source_target_pairs={{0,3},{1,2},{2,1},{3,0},{4,7},{5,6},{6,5},{7,4},{8,11},{9,10},{10,... | collective-permute-start | bytes 442376 | tf_op jit(solution)/shard_map/ppermute | solution.py:541
  249.8 12.5 %collective-permute-start.3 = (bf16[16,48,96]{2,1,0:T(8,128)(2,1)}, bf16[16,48,96]{2,1,0:T(8,128)(2,1)S(1)}, u32[]{:S(2)}, u32[]{:S(2)}) collective-permute-start(bf16[16,48,96]{2,1,0:T(8,128)(2,1)} %get-tuple-element.124), channel_id=1, source_target_pairs={{0,4},{1,5},{2,6},{3,7},{4,0},{5,1},{6,2},{7,3},{8,12},{9,13},{10,... | collective-permute-start | bytes 442376 | tf_op jit(solution)/shard_map/ppermute | solution.py:541
  260.9 11.2 %collective-permute-start.4 = (bf16[16,48,96]{2,1,0:T(8,128)(2,1)}, bf16[16,48,96]{2,1,0:T(8,128)(2,1)S(1)}, u32[]{:S(2)}, u32[]{:S(2)}) collective-permute-start(bf16[16,48,96]{2,1,0:T(8,128)(2,1)} %get-tuple-element.123), channel_id=1, source_target_pairs={{0,5},{1,4},{2,7},{3,6},{4,1},{5,0},{6,3},{7,2},{8,13},{9,12},{10,... | collective-permute-start | bytes 442376 | tf_op jit(solution)/shard_map/ppermute | solution.py:541
  262.3 27.4 %collective-permute-start.12 = (bf16[16,48,96]{2,1,0:T(8,128)(2,1)}, bf16[16,48,96]{2,1,0:T(8,128)(2,1)S(1)}, u32[]{:S(2)}, u32[]{:S(2)}) collective-permute-start(bf16[16,48,96]{2,1,0:T(8,128)(2,1)} %get-tuple-element.116), channel_id=1, source_target_pairs={{0,6},{1,7},{2,4},{3,5},{4,2},{5,3},{6,0},{7,1},{8,14},{9,15},{10,... | collective-permute-start | bytes 442376 | tf_op jit(solution)/shard_map/ppermute | solution.py:541
  272.1 2.8 collective-permute-start.7
  272.4 7.8 %collective-permute-start.8 = (bf16[16,48,96]{2,1,0:T(8,128)(2,1)S(1)}, bf16[16,48,96]{2,1,0:T(8,128)(2,1)S(1)}, u32[]{:S(2)}, u32[]{:S(2)}) collective-permute-start(bf16[16,48,96]{2,1,0:T(8,128)(2,1)S(1)} %copy-done.19), channel_id=1, source_target_pairs={{0,2},{1,3},{2,0},{3,1},{4,6},{5,7},{6,4},{7,5},{8,10},{9,11},{10,... | collective-permute-start | bytes 442376 | tf_op jit(solution)/shard_map/ppermute | solution.py:541
  274.9 17.9 %copy-start.24 = (s32[3,384]{1,0:T(4,128)S(1)}, s32[3,384]{1,0:T(4,128)}, u32[]{:S(2)}) copy-start(s32[3,384]{1,0:T(4,128)} %constant.244.clone) | copy-start | bytes 13828
  274.9 8.1 %collective-permute-start.9 = (bf16[16,48,96]{2,1,0:T(8,128)(2,1)S(1)}, bf16[16,48,96]{2,1,0:T(8,128)(2,1)S(1)}, u32[]{:S(2)}, u32[]{:S(2)}) collective-permute-start(bf16[16,48,96]{2,1,0:T(8,128)(2,1)S(1)} %copy-done.18), channel_id=1, source_target_pairs={{0,3},{1,2},{2,1},{3,0},{4,7},{5,6},{6,5},{7,4},{8,11},{9,10},{10,... | collective-permute-start | bytes 442376 | tf_op jit(solution)/shard_map/ppermute | solution.py:541
  280.2 5.9 collective-permute-start.10
  283.0 6.8 %collective-permute-start.11 = (bf16[16,48,96]{2,1,0:T(8,128)(2,1)S(1)}, bf16[16,48,96]{2,1,0:T(8,128)(2,1)S(1)}, u32[]{:S(2)}, u32[]{:S(2)}) collective-permute-start(bf16[16,48,96]{2,1,0:T(8,128)(2,1)S(1)} %copy-done.17), channel_id=1, source_target_pairs={{0,5},{1,4},{2,7},{3,6},{4,1},{5,0},{6,3},{7,2},{8,13},{9,12},{10,... | collective-permute-start | bytes 442376 | tf_op jit(solution)/shard_map/ppermute | solution.py:541
  406.8 7.8 %collective-permute-start.15 = (bf16[16,48,96]{2,1,0:T(8,128)(2,1)S(1)}, bf16[16,48,96]{2,1,0:T(8,128)(2,1)S(1)}, u32[]{:S(2)}, u32[]{:S(2)}) collective-permute-start(bf16[16,48,96]{2,1,0:T(8,128)(2,1)S(1)} %get-tuple-element.114), channel_id=1, source_target_pairs={{0,2},{1,3},{2,0},{3,1},{4,6},{5,7},{6,4},{7,5},{8,10},{9,11},{10,... | collective-permute-start | bytes 442376 | tf_op jit(solution)/shard_map/ppermute | solution.py:541
  408.3 5.4 collective-permute-start.14
  409.5 46.8 %collective-permute-start.27 = (bf16[16,32,96]{2,1,0:T(8,128)(2,1)S(1)}, bf16[16,32,96]{2,1,0:T(8,128)(2,1)S(1)}, u32[]{:S(2)}, u32[]{:S(2)}) collective-permute-start(bf16[16,32,96]{2,1,0:T(8,128)(2,1)S(1)} %slice.381), channel_id=1, source_target_pairs={{0,7},{1,6},{2,5},{3,4},{4,3},{5,2},{6,1},{7,0},{8,15},{9,14},{10,... | collective-permute-start | bytes 294920 | tf_op jit(solution)/shard_map/ppermute | solution.py:541
  411.0 45.2 %collective-permute-start.20 = (bf16[16,32,96]{2,1,0:T(8,128)(2,1)S(1)}, bf16[16,32,96]{2,1,0:T(8,128)(2,1)S(1)}, u32[]{:S(2)}, u32[]{:S(2)}) collective-permute-start(bf16[16,32,96]{2,1,0:T(8,128)(2,1)S(1)} %slice.373), channel_id=1, source_target_pairs={{0,7},{1,6},{2,5},{3,4},{4,3},{5,2},{6,1},{7,0},{8,15},{9,14},{10,... | collective-permute-start | bytes 294920 | tf_op jit(solution)/shard_map/ppermute | solution.py:541
  412.2 26.8 %collective-permute-start.19 = (bf16[16,48,96]{2,1,0:T(8,128)(2,1)S(1)}, bf16[16,48,96]{2,1,0:T(8,128)(2,1)S(1)}, u32[]{:S(2)}, u32[]{:S(2)}) collective-permute-start(bf16[16,48,96]{2,1,0:T(8,128)(2,1)S(1)} %get-tuple-element.110), channel_id=1, source_target_pairs={{0,6},{1,7},{2,4},{3,5},{4,2},{5,3},{6,0},{7,1},{8,14},{9,15},{10,... | collective-permute-start | bytes 442376 | tf_op jit(solution)/shard_map/ppermute | solution.py:541
  413.7 14.0 %collective-permute-start.16 = (bf16[16,48,96]{2,1,0:T(8,128)(2,1)S(1)}, bf16[16,48,96]{2,1,0:T(8,128)(2,1)S(1)}, u32[]{:S(2)}, u32[]{:S(2)}) collective-permute-start(bf16[16,48,96]{2,1,0:T(8,128)(2,1)S(1)} %get-tuple-element.113), channel_id=1, source_target_pairs={{0,3},{1,2},{2,1},{3,0},{4,7},{5,6},{6,5},{7,4},{8,11},{9,10},{10,... | collective-permute-start | bytes 442376 | tf_op jit(solution)/shard_map/ppermute | solution.py:541
  414.6 14.8 %collective-permute-start.17 = (bf16[16,48,96]{2,1,0:T(8,128)(2,1)S(1)}, bf16[16,48,96]{2,1,0:T(8,128)(2,1)S(1)}, u32[]{:S(2)}, u32[]{:S(2)}) collective-permute-start(bf16[16,48,96]{2,1,0:T(8,128)(2,1)S(1)} %get-tuple-element.112), channel_id=1, source_target_pairs={{0,4},{1,5},{2,6},{3,7},{4,0},{5,1},{6,2},{7,3},{8,12},{9,13},{10,... | collective-permute-start | bytes 442376 | tf_op jit(solution)/shard_map/ppermute | solution.py:541
  427.7 10.7 %collective-permute-start.18 = (bf16[16,48,96]{2,1,0:T(8,128)(2,1)S(1)}, bf16[16,48,96]{2,1,0:T(8,128)(2,1)S(1)}, u32[]{:S(2)}, u32[]{:S(2)}) collective-permute-start(bf16[16,48,96]{2,1,0:T(8,128)(2,1)S(1)} %get-tuple-element.111), channel_id=1, source_target_pairs={{0,5},{1,4},{2,7},{3,6},{4,1},{5,0},{6,3},{7,2},{8,13},{9,12},{10,... | collective-permute-start | bytes 442376 | tf_op jit(solution)/shard_map/ppermute | solution.py:541
  429.4 26.8 %collective-permute-start.26 = (bf16[16,48,96]{2,1,0:T(8,128)(2,1)S(1)}, bf16[16,48,96]{2,1,0:T(8,128)(2,1)S(1)}, u32[]{:S(2)}, u32[]{:S(2)}) collective-permute-start(bf16[16,48,96]{2,1,0:T(8,128)(2,1)S(1)} %get-tuple-element.104), channel_id=1, source_target_pairs={{0,6},{1,7},{2,4},{3,5},{4,2},{5,3},{6,0},{7,1},{8,14},{9,15},{10,... | collective-permute-start | bytes 442376 | tf_op jit(solution)/shard_map/ppermute | solution.py:541
  438.4 2.2 collective-permute-start.21
  439.0 7.8 %collective-permute-start.22 = (bf16[16,48,96]{2,1,0:T(8,128)(2,1)S(1)}, bf16[16,48,96]{2,1,0:T(8,128)(2,1)S(1)}, u32[]{:S(2)}, u32[]{:S(2)}) collective-permute-start(bf16[16,48,96]{2,1,0:T(8,128)(2,1)S(1)} %get-tuple-element.108), channel_id=1, source_target_pairs={{0,2},{1,3},{2,0},{3,1},{4,6},{5,7},{6,4},{7,5},{8,10},{9,11},{10,... | collective-permute-start | bytes 442376 | tf_op jit(solution)/shard_map/ppermute | solution.py:541
  440.6 8.6 %collective-permute-start.23 = (bf16[16,48,96]{2,1,0:T(8,128)(2,1)S(1)}, bf16[16,48,96]{2,1,0:T(8,128)(2,1)S(1)}, u32[]{:S(2)}, u32[]{:S(2)}) collective-permute-start(bf16[16,48,96]{2,1,0:T(8,128)(2,1)S(1)} %get-tuple-element.107), channel_id=1, source_target_pairs={{0,3},{1,2},{2,1},{3,0},{4,7},{5,6},{6,5},{7,4},{8,11},{9,10},{10,... | collective-permute-start | bytes 442376 | tf_op jit(solution)/shard_map/ppermute | solution.py:541
  446.8 5.9 collective-permute-start.24
  449.1 7.0 %collective-permute-start.25 = (bf16[16,48,96]{2,1,0:T(8,128)(2,1)S(1)}, bf16[16,48,96]{2,1,0:T(8,128)(2,1)S(1)}, u32[]{:S(2)}, u32[]{:S(2)}) collective-permute-start(bf16[16,48,96]{2,1,0:T(8,128)(2,1)S(1)} %get-tuple-element.105), channel_id=1, source_target_pairs={{0,5},{1,4},{2,7},{3,6},{4,1},{5,0},{6,3},{7,2},{8,13},{9,12},{10,... | collective-permute-start | bytes 442376 | tf_op jit(solution)/shard_map/ppermute | solution.py:541
  457.9 64.5 %copy-start.13 = (f32[1164,96]{1,0:T(8,128)S(1)}, f32[1164,96]{1,0:T(8,128)}, u32[]{:S(2)}) copy-start(f32[1164,96]{1,0:T(8,128)} %get-tuple-element.71) | copy-start | bytes 1340932
  527.9 126.7 %copy-start.21 = (f32[6984]{0:T(1024)S(1)}, f32[6984]{0:T(1024)}, u32[]{:S(2)}) copy-start(f32[6984]{0:T(1024)} %param.42) | copy-start | bytes 83812
  527.9 126.7 %copy-start.22 = (f32[6984]{0:T(1024)S(1)}, f32[6984]{0:T(1024)}, u32[]{:S(2)}) copy-start(f32[6984]{0:T(1024)} %param.43) | copy-start | bytes 83812
  528.0 126.7 %copy-start.23 = (f32[6984]{0:T(1024)S(1)}, f32[6984]{0:T(1024)}, u32[]{:S(2)}) copy-start(f32[6984]{0:T(1024)} %param.44) | copy-start | bytes 83812
  (13 other events, 27.6 us)
Sparse Core Ops, SparseCore 0:
  13.9 128.5 all-reduce.6
  525.4 129.1 all-reduce.8

commit v2 on v1

--- a/solution.py
+++ b/solution.py
@@ -33,7 +33,8 @@
 F32 = jnp.float32
 NN = (((1,), (0,)), ((), ()))
 NT = (((1,), (1,)), ((), ()))
-BY_STEP, WHOLE, SMEM = -1, -2, -3
+BY_STEP, WHOLE, SMEM, HBM = -1, -2, -3, -4
+MESH = pl.DeviceIdType.MESH
 VOL, WIN = "vol", "win"
 
 
@@ -56,31 +57,24 @@
 def slot_tables():
     perm = np.zeros((T, T), np.float32)
     order = np.zeros((T, WS), np.float32)
-    rolled = np.full((T, 4), 99, np.int32)
-    plain = np.full((T, 4), 99, np.int32)
-    plain[:, 3] = 0
+    places = np.full((8, T), 99, np.int32)
     for octant in range(8):
         bits = octant_bits(octant)
         lens = [SHIFT if bit else SIDE - SHIFT for bit in bits]
-        rolled[OCT_OFF[octant] : OCT_OFF[octant] + OCT_LEN[octant], 3] = octant
         for i in range(lens[0]):
             for j in range(lens[1]):
                 for k in range(lens[2]):
                     source = [v if bit else v + SHIFT for v, bit in zip((i, j, k), bits)]
+                    own = [v + bit * (SIDE - SHIFT) for v, bit in zip((i, j, k), bits)]
                     q = OCT_OFF[octant] + (i * lens[1] + j) * lens[2] + k
                     t = (source[0] * SIDE + source[1]) * SIDE + source[2]
                     perm[q, t] = 1
-                    own = [v + bit * (SIDE - SHIFT) for v, bit in zip((i, j, k), bits)]
                     order[q, (own[0] * SIDE + own[1]) * SIDE + own[2]] = 1
-                    rolled[q, :3] = source
-    for i in range(SIDE):
-        for j in range(SIDE):
-            for k in range(SIDE):
-                plain[(i * SIDE + j) * SIDE + k, :3] = (i, j, k)
-    return perm, order, plain, rolled
-
-
-PERM, ORDER, PLAIN, ROLLED = slot_tables()
+                    places[:3, t] = source
+    return perm, order, places
+
+
+PERM, ORDER, PLACES = slot_tables()
 
 
 def dot(a, b, dims=NN):
@@ -130,7 +124,7 @@
     sc.qb[...] = jnp.zeros((CA, HEADS * T), BF)
     for h in range(HEADS):
         sc.vt[h, 16:32, :] = ones_row((16, T)).astype(BF)
-        turned = dot(r.order[...], r.table[0, h], NT).astype(BF)
+        turned = dot(r.order[...], r.table[h], NT).astype(BF)
         sc.bias[h] = dot(turned, r.order[...], NT)
 
 
@@ -350,24 +344,94 @@
     return z, scale
 
 
-def first_forward_kernel(r):
+def grid_place(groups_a):
+    win = lax.axis_index(WIN)
+    return (win // 4, win // 2 % 2, win % 2), (groups_a, 2, 2)
+
+
+def neighbour(octant, sign, groups_a):
+    place, sizes = grid_place(groups_a)
+    a, b, c = (
+        (p + sign * bit + n) % n for p, bit, n in zip(place, octant_bits(octant), sizes)
+    )
+    return lax.axis_index(VOL), (a * 2 + b) * 2 + c
+
+
+def greet(peers):
+    barrier = pltpu.get_barrier_semaphore()
+    for peer in peers:
+        pl.semaphore_signal(barrier, inc=1, device_id=peer, device_id_type=MESH)
+    pl.semaphore_wait(barrier, len(peers))
+
+
+def block_copy(r, m, octant, sign, groups_a):
+    rows = pl.ds(OCT_OFF[octant], OCT_LEN[octant])
+    source, target = r.stage.at[m % 2, rows], r.got.at[m, rows]
+    if octant == 0:
+        return pltpu.make_async_copy(source, target, r.sent.at[m % 2, 0])
+    return pltpu.make_async_remote_copy(
+        src_ref=source,
+        dst_ref=target,
+        send_sem=r.sent.at[m % 2, octant],
+        recv_sem=r.arrived.at[m, octant],
+        device_id=neighbour(octant, sign, groups_a),
+        device_id_type=MESH,
+    )
+
+
+def wait_sent(r, m, sign, groups_a):
+    for octant in range(8):
+        copy = block_copy(r, m, octant, sign, groups_a)
+        copy.wait_send() if octant else copy.wait()
+
+
+def send_blocks(r, m, sign, groups_a):
+    for octant in range(8):
+        block_copy(r, m, octant, sign, groups_a).start()
+
+
+def finish_blocks(r, steps, sign, groups_a):
+    for m in range(max(steps - 2, 0), steps):
+        wait_sent(r, m, sign, groups_a)
+
+    def arrival(m, carry):
+        for octant in range(1, 8):
+            block_copy(r, m, octant, sign, groups_a).wait_recv()
+        return carry
+
+    lax.fori_loop(0, steps, arrival, 0)
+
+
+def first_forward_kernel(groups_a, steps, r):
     w, sc = r, by_step(r)
     m = pl.program_id(0)
 
     @pl.when(m == 0)
     def _():
+        greet([neighbour(octant, 1, groups_a) for octant in range(1, 8)])
         init_forward(r, sc)
-        sc.pad[...] = jnp.zeros((2, T, C), BF)
-
-    sc.pad[0, 0:WS, :] = r.tokens[0, 0]
-    sc.pad[1, 0:WS, :] = r.cotangent[0, 0]
-    r.sent_cot[0] = dot(r.perm[...], sc.pad[1]).astype(BF)
-    place = r.place
+        sc.pad[...] = jnp.zeros((C, T), BF)
+        sc.cot[...] = jnp.zeros((C, T), BF)
+
+    @pl.when(m >= 2)
+    def _():
+        wait_sent(r, m - 2, -1, groups_a)
+
+    sc.pad[:, 0:WS] = r.tokens[0, 0]
+    sc.cot[:, 0:WS] = r.cotangent[0, 0]
+    slot = m % 2
+    r.stage[slot, :, CA:] = jnp.concatenate(
+        [dot(r.perm[...], sc.cot[...], NT), jnp.zeros((T, CA - C), F32)], axis=1
+    ).astype(BF)
+    places = r.places
     valid = (
-        (place[0] < r.info[m, 1]) & (place[1] < r.info[m, 2]) & (place[2] < r.info[m, 3])
-    )
-    sc.codes[...] = jnp.where(valid, 0.0, -1.0)
-    x = dot(r.eye[...], sc.pad[0], NT)
+        (places[0:1, :] < r.info[m, 1])
+        & (places[1:2, :] < r.info[m, 2])
+        & (places[2:3, :] < r.info[m, 3])
+    )
+    valid = jnp.where(valid, 1.0, 0.0)
+    sc.codes[...] = jnp.broadcast_to(valid - 1.0, (128, T)).T
+    x = sc.pad[...].astype(F32)
     sc.xT[...] = x
     x = x + forward_attention(sc, w, x, jnp.zeros((1, T), F32))
     sc.x1[...] = x
@@ -378,41 +442,54 @@
         sc.act[rows, :] = active.astype(BF)
         sc.gp[rows, :] = slope.astype(BF)
     x = x + (dot(w.downT[...], sc.act[...]) + wide(w.vec[4]))
-    r.sent_x[0] = dot(r.perm[...], x.astype(BF), NT).astype(BF)
-
-
-def second_kernel(r):
+    row = lax.broadcasted_iota(jnp.int32, (CA - C, T), 0)
+    label = r.info[m, 0].astype(F32)
+    extra = jnp.where(row == 0, label, jnp.where(row == 1, valid, 0.0))
+    x = jnp.concatenate([x, extra], axis=0).astype(BF)
+    r.stage[slot, :, 0:CA] = dot(r.perm[...], x, NT).astype(BF)
+    send_blocks(r, m, -1, groups_a)
+
+    @pl.when(m == steps - 1)
+    def _():
+        finish_blocks(r, steps, -1, groups_a)
+
+
+def second_kernel(groups_a, steps, r):
     w, sc = r, r
     m = pl.program_id(0)
 
     @pl.when(m == 0)
     def _():
+        greet([neighbour(octant, -1, groups_a) for octant in range(1, 8)])
         init_forward(r, sc)
         init_backward(sc)
 
-    place, rows4 = r.place, r.places
-    octant_row = rows4[3:4, :]
-    label_row = jnp.zeros((1, T), F32)
-    ends = [jnp.zeros((1, T), jnp.int32)] * 3
-    for o in range(8):
-        rows = slice(OCT_OFF[o], OCT_OFF[o] + OCT_LEN[o])
-        item = [r.info[m, 4 * o + n] for n in range(4)]
-        label = item[0].astype(F32)
-        valid = (
-            (place[0, rows] < item[1]) & (place[1, rows] < item[2]) & (place[2, rows] < item[3])
-        )
-        sc.codes[rows, :] = jnp.where(valid, label, -1.0)
-        here = octant_row == o
-        label_row = jnp.where(here, label, label_row)
-        ends = [jnp.where(here, item[n + 1], ends[n]) for n in range(3)]
-    keep = jnp.where(
-        (rows4[0:1, :] < ends[0]) & (rows4[1:2, :] < ends[1]) & (rows4[2:3, :] < ends[2]), 1.0, 0.0
-    )
-    x = dot(r.eye[...], r.got_x[0], NT)
-    d = dot(r.eye[...], r.got_cot[0], NT) * keep
+    @pl.when(m >= 2)
+    def _():
+        wait_sent(r, m - 2, 1, groups_a)
+
+    came = r.came[0, :, 0:CA]
+    x = dot(r.eye[...], came, NT)
+    place, sizes = grid_place(groups_a)
+    code_row = []
+    for octant in range(8):
+        rows = slice(OCT_OFF[octant], OCT_OFF[octant] + OCT_LEN[octant])
+        wraps = [
+            bit * jnp.where(p == n - 1, 1, 0)
+            for p, bit, n in zip(place, octant_bits(octant), sizes)
+        ]
+        wrap = (wraps[0] * 4 + wraps[1] * 2 + wraps[2]).astype(F32)
+        columns = came[rows].astype(F32)
+        code = jnp.where(columns[:, C + 1 : C + 2] > 0.0, columns[:, C : C + 1] * 8.0 + wrap, -1.0)
+        sc.codes[rows, :] = jnp.broadcast_to(code, (OCT_LEN[octant], 128))
+        code_row.append(jnp.full((1, OCT_LEN[octant]), wrap))
+    code_row = jnp.concatenate(code_row, axis=1) + 8.0 * x[C : C + 1]
+    keep = x[C + 1 : C + 2]
+    x = x[0:C]
+    d = dot(r.eye[0:C], r.came[0, :, CA:], NT) * keep
     dd = d.astype(BF)
     sc.xT[...] = x
-    branch = forward_attention(sc, w, x, label_row)
+    branch = forward_attention(sc, w, x, code_row)
     x = x + branch.astype(BF).astype(F32)
     z, scale = second_norm(sc, w, x)
     for c in range(3):
@@ -421,18 +498,22 @@
         sc.act[rows, :] = active.astype(BF)
         sc.dh[rows, :] = (dot(w.down[rows], dd) * slope).astype(BF)
     x = x + (dot(w.downT[...], sc.act[...]) + wide(w.vec[4]))
-    r.sent_out[0] = (x * keep).T.astype(BF)
+    slot = m % 2
+    none = jnp.zeros((CA - C, T), F32)
+    r.stage[slot, :, 0:CA] = jnp.concatenate([x * keep, none], axis=0).T.astype(BF)
     d = feed_forward_back(sc, w, d, dd, z, scale)
     z, scale = ln_stats(sc.xT[...])
     d = backward_attention(sc, w, d, z, scale, True)
-    r.sent_d[0] = d.T.astype(BF)
-
-    @pl.when(m == pl.num_programs(0) - 1)
+    r.stage[slot, :, CA:] = jnp.concatenate([d, none], axis=0).T.astype(BF)
+    send_blocks(r, m, 1, groups_a)
+
+    @pl.when(m == steps - 1)
     def _():
+        finish_blocks(r, steps, 1, groups_a)
         write_grads(sc, r.grads)
 
 
-def first_backward_kernel(r):
+def first_backward_kernel(steps, r):
     w, sc = r, by_step(r)
     m = pl.program_id(0)
 
@@ -440,8 +521,10 @@
     def _():
         init_backward(sc)
 
-    r.output[0, 0] = dot(r.perm_back[...], r.got_out[0]).astype(BF)[0:WS]
-    d = dot(dot(r.eye[...], r.got_d[0], NT).astype(BF), r.perm[...])
+    came = dot(r.eye[...], r.came[0], NT).astype(BF)
+    came = dot(came, r.perm[...])
+    r.output[0, 0] = came[0:C, 0:WS].astype(BF)
+    d = came[CA : CA + C]
     dd = d.astype(BF)
     z, scale = ln_stats(sc.x1[...])
     for c in range(3):
@@ -450,25 +533,188 @@
     d = feed_forward_back(sc, w, d, dd, z, scale)
     z, scale = ln_stats(sc.xT[...])
     d = backward_attention(sc, w, d, z, scale, False)
-    r.input_grad[0, 0] = d.T[0:WS]
-
-    @pl.when(m == pl.num_programs(0) - 1)
+    r.input_grad[0, 0] = d[:, 0:WS]
+
+    @pl.when(m == steps - 1)
     def _():
         write_grads(sc, r.grads)
 
 
-def call(kernel, steps, ins, outs, scratch):
+def shard_rows(device, shard_len):
+    return device * shard_len // C, -(-(device + 1) * shard_len // C)
+
+
+def flat_offset(device, shard_len):
+    return device * shard_len % C
+
+
+def slab_rows(shard_len):
+    return -(-((shard_len + C - 2) // C + 1) // 16) * 16
+
+
+def own_place():
+    win = lax.axis_index(WIN)
+    return lax.axis_index(VOL), win // 2, win % 2
+
+
+def all_peers(n_vol, n_plane):
+    vol, plane, core = own_place()
+    return (
+        [((vol + j) % n_vol, plane * 2 + core) for j in range(1, n_vol)]
+        + [(vol, (plane + j) % n_plane * 2 + core) for j in range(1, n_plane)]
+        + [(vol, plane * 2 + 1 - core)]
+    )
+
+
+def transpose_with(matrix, extra):
+    below = jnp.where(lax.broadcasted_iota(jnp.int32, (CA - C, C), 0) == 0, extra, 0.0)
+    return jnp.concatenate([matrix, below], axis=0).T
+
+
+def gather_kernel(n_vol, n_plane, shard_len, r):
+    vol, plane, core = own_place()
+    peers = all_peers(n_vol, n_plane)
+    greet(peers)
+    buf = r.buf
+
+    def copy(ref, n):
+        return pltpu.make_async_remote_copy(
+            src_ref=ref,
+            dst_ref=ref,
+            send_sem=r.sent.at[n],
+            recv_sem=r.arrived.at[n],
+            device_id=peers[n],
+            device_id_type=MESH,
+        )
+
+    buf[core, plane, vol] = r.shard[...]
+    stages = [
+        [copy(buf.at[core, plane, vol], n) for n in range(n_vol - 1)],
+        [copy(buf.at[core, plane], n_vol - 1 + n) for n in range(n_plane - 1)],
+        [copy(buf.at[core], n_vol + n_plane - 2)],
+    ]
+    for copies in stages:
+        for c in copies:
+            c.start()
+        for c in copies:
+            c.wait()
+    flat = r.flat
+    flat[...] = jnp.zeros(flat.shape, F32)
+    for v in range(n_vol):
+        for p in range(n_plane):
+            for c in range(2):
+                start, stop = shard_rows((v * n_plane + p) * 2 + c, shard_len)
+                flat[start:stop, :] += buf[c, p, v, 0 : stop - start].astype(F32)
+    for layer in range(2):
+        at = layer * BLOCK_ROWS
+
+        def rows(start, count=C, stride=1):
+            return flat[pl.ds(at + start, count, stride), :]
+
+        def vector(n):
+            return rows(12 * C + n, 1)
+
+        o = {n: getattr(r, n).at[layer] for n in WEIGHTS}
+        o = SimpleNamespace(**o)
+        none = jnp.zeros((1, C), F32)
+        wq, wk, wv = (rows(n, C, 3) for n in range(3))
+        o.q[...] = wq.astype(BF)
+        o.kv96[...] = jnp.concatenate([wk, wv], axis=1).astype(BF)
+        o.qkvT[0:C, :] = (transpose_with(wq, vector(2)) * 0.25).astype(BF)
+        o.qkvT[C : 2 * C, :] = (transpose_with(wk, none) * 0.25).astype(BF)
+        o.qkvT[2 * C :, :] = transpose_with(wv, vector(3)).astype(BF)
+        row = lax.broadcasted_iota(jnp.int32, (CA - C, CA), 0)
+        lane = lax.broadcasted_iota(jnp.int32, (CA - C, CA), 1)
+        blank = jnp.zeros((C, CA - C), F32)
+        bias_v = jnp.concatenate([vector(3), blank[0:1]], axis=1)
+        ones = jnp.where((lane == C) | (lane == C + 1), 1.0, bias_v)
+        o.kv[0:C, :] = jnp.concatenate([wk, blank, wv, blank], axis=1).astype(BF)
+        o.kv[C:, 0:CA] = jnp.zeros((CA - C, CA), BF)
+        o.kv[C:, CA:] = jnp.where(row == 0, ones, 0.0).astype(BF)
+        proj = rows(3 * C)
+        o.proj[...] = proj.astype(BF)
+        o.projT[...] = transpose_with(proj, vector(4)).astype(BF)
+        ups = [rows(4 * C + j, C, 4) for j in range(4)]
+        o.up[...] = jnp.concatenate(ups, axis=1).astype(BF)
+        for j in range(4):
+            o.upT[C * j : C * j + C, :] = transpose_with(ups[j], vector(8 + j)).astype(BF)
+        down = rows(8 * C, FF)
+        o.down[...] = down.astype(BF)
+        o.downT[...] = down.T.astype(BF)
+        for n, source in enumerate((0, 1, 5, 6, 7)):
+            o.vec[n] = jnp.broadcast_to(vector(source), (128, C)).T
+
+
+def reduce_kernel(n_vol, n_plane, shard_len, r):
+    vol, plane, core = own_place()
+    peers = all_peers(n_vol, n_plane)
+    greet(peers)
+    work = r.work
+    half = 2 * n_vol * n_plane // 2
+    for v in range(n_vol):
+        for p in range(n_plane):
+            for c in range(2):
+                device = (v * n_plane + p) * 2 + c
+                start, stop = shard_rows(device, shard_len)
+                source = (r.first, r.second)[device // half]
+                start, stop = (n - device // half * BLOCK_ROWS for n in (start, stop))
+                work[c, p, v, 0 : stop - start] = source[start:stop, :]
+
+    def copy(source, target, n):
+        return pltpu.make_async_remote_copy(
+            src_ref=source,
+            dst_ref=target,
+            send_sem=r.sent.at[n],
+            recv_sem=r.arrived.at[n],
+            device_id=peers[n],
+            device_id_type=MESH,
+        )
+
+    def exchange(copies):
+        for c in copies:
+            c.start()
+        for c in copies:
+            c.wait()
+
+    exchange([copy(work.at[1 - core], r.from_core, n_vol + n_plane - 2)])
+    work[core] += r.from_core[...]
+    exchange(
+        [
+            copy(work.at[core, (plane + j) % n_plane], r.from_plane.at[j - 1], n_vol - 2 + j)
+            for j in range(1, n_plane)
+        ]
+    )
+    total = work[core, plane]
+    for j in range(n_plane - 1):
+        total = total + r.from_plane[j]
+    work[core, plane] = total
+    exchange(
+        [
+            copy(work.at[core, plane, (vol + j) % n_vol], r.from_vol.at[j - 1], j - 1)
+            for j in range(1, n_vol)
+        ]
+    )
+    total = work[core, plane, vol]
+    for j in range(n_vol - 1):
+        total = total + r.from_vol[j]
+    r.total[...] = total
+
+
+def call(kernel, steps, ins, outs, scratch, semaphores=(), collective_id=None):
     def spec(shape, kind):
         if kind is SMEM:
             return pl.BlockSpec(memory_space=pltpu.SMEM)
+        if kind is HBM:
+            return pl.BlockSpec(memory_space=pl.ANY)
         zeros = (0,) * (len(shape) - 1)
         if kind is BY_STEP:
             return pl.BlockSpec((1,) + tuple(shape[1:]), lambda m: (m,) + zeros)
         if kind in (0, 1):
-            return pl.BlockSpec((1,) + tuple(shape[1:]), lambda m: (kind,) + zeros)
+            return pl.BlockSpec((pl.squeezed,) + tuple(shape[1:]), lambda m: (kind,) + zeros)
         return pl.BlockSpec(tuple(shape), lambda m: (0,) + zeros)
 
-    names = tuple(ins) + tuple(outs) + tuple(scratch)
+    semaphores = dict(semaphores)
+    names = tuple(ins) + tuple(outs) + tuple(scratch) + tuple(semaphores)
 
     def body(*refs):
         kernel(SimpleNamespace(**dict(zip(names, refs))))
@@ -479,84 +725,30 @@
         in_specs=[spec(a.shape, kind) for a, kind in ins.values()],
         out_specs=[spec(shape, kind) for shape, _, kind in outs.values()],
         out_shape=[jax.ShapeDtypeStruct(shape, dtype) for shape, dtype, _ in outs.values()],
-        scratch_shapes=[pltpu.VMEM(shape, dtype) for shape, dtype in scratch.values()],
-        compiler_params=pltpu.CompilerParams(vmem_limit_bytes=60 * 2**20),
+        scratch_shapes=[pltpu.VMEM(shape, dtype) for shape, dtype in scratch.values()]
+        + [pltpu.SemaphoreType.DMA(shape) for shape in semaphores.values()],
+        compiler_params=pltpu.CompilerParams(
+            vmem_limit_bytes=60 * 2**20,
+            collective_id=collective_id,
+            has_side_effects=collective_id is not None,
+        ),
     )(*[a for a, _ in ins.values()])
     return SimpleNamespace(**dict(zip(outs, results)))
 
 
-def layer_operands(params, which_layer):
-    rows = params[which_layer * BLOCK_ROWS : (which_layer + 1) * BLOCK_ROWS]
-    wq, wk, wv = (rows[0 : 3 * C].reshape(C, 3, C)[:, n] for n in range(3))
-    proj = rows[3 * C : 4 * C]
-    up = rows[4 * C : 8 * C].reshape(C, FF)
-    down = rows[8 * C : 12 * C]
-    vectors = rows[12 * C : 12 * C + 8]
-    bias_up = rows[12 * C + 8 :].reshape(FF)
-    gain1, offset1, bias_q, bias_v, bias_proj, gain2, offset2, bias_down = vectors
-    quarter = jnp.asarray(0.25, BF)
-
-    def aug(matrix, bias):
-        return jnp.concatenate(
-            [matrix, bias[:, None], jnp.zeros((matrix.shape[0], CA - C - 1), BF)], axis=1
-        )
-
-    none = jnp.zeros((C,), BF)
-    kn = aug(wk.T, none).T
-    vn = jnp.concatenate([aug(wv.T, bias_v).T, jnp.zeros((CA, CA - C), BF)], axis=1)
-    vn = vn.at[C, C : C + 2].set(1.0)
-    kn = jnp.concatenate([kn, jnp.zeros((CA, CA - C), BF)], axis=1)
-    columns = jnp.stack([gain1, offset1, gain2, offset2, bias_down]).astype(F32)
-    return dict(
-        qkvT=jnp.concatenate(
-            [aug(wq.T * quarter, bias_q * quarter), aug(wk.T * quarter, none), aug(wv.T, bias_v)]
-        ),
-        kv=jnp.concatenate([kn, vn], axis=1),
-        projT=aug(proj.T, bias_proj),
-        proj=proj,
-        upT=aug(up.T, bias_up),
-        up=up,
-        downT=down.T,
-        down=down,
-        q=wq,
-        kv96=jnp.concatenate([wk, wv], axis=1),
-        vec=jnp.broadcast_to(columns[:, :, None], (5, C, 128)),
-    )
-
-
-def exchange(x, forward, groups_a):
-    sign = -1 if forward else 1
-    blocks = []
-    for octant in range(8):
-        part = x[:, OCT_OFF[octant] : OCT_OFF[octant] + OCT_LEN[octant]]
-        if octant:
-            bits = octant_bits(octant)
-            pairs = []
-            for w in range(4 * groups_a):
-                place = (w // 4, w // 2 % 2, w % 2)
-                a, b, c = (
-                    (p + sign * bit) % n for p, bit, n in zip(place, bits, (groups_a, 2, 2))
-                )
-                pairs.append((w, (a * 2 + b) * 2 + c))
-            part = lax.ppermute(part, WIN, pairs)
-        blocks.append(part)
-    return jnp.concatenate(blocks, axis=1)
-
-
-def octant_info(group_info, groups_a):
-    index_win = lax.axis_index(WIN)
-    place = (index_win // 4, index_win // 2 % 2, index_win % 2)
-    items = []
-    for octant in range(8):
-        bits = octant_bits(octant)
-        a, b, c = ((p + bit) % n for p, bit, n in zip(place, bits, (groups_a, 2, 2)))
-        wraps = [
-            bit * (p == n - 1).astype(jnp.int32) for p, bit, n in zip(place, bits, (groups_a, 2, 2))
-        ]
-        source = lax.dynamic_index_in_dim(group_info, (a * 2 + b) * 2 + c, 1, keepdims=False)
-        code = wraps[0] * 4 + wraps[1] * 2 + wraps[2]
-        items.append(source * jnp.array([8, 1, 1, 1]) + code * jnp.array([1, 0, 0, 0]))
-    return jnp.concatenate(items, axis=1)
+WEIGHTS = dict(
+    qkvT=((3 * C, CA), BF),
+    kv=((CA, 2 * CA), BF),
+    projT=((C, CA), BF),
+    proj=((C, C), BF),
+    upT=((FF, CA), BF),
+    up=((C, FF), BF),
+    downT=((C, FF), BF),
+    down=((FF, C), BF),
+    q=((C, C), BF),
+    kv96=((C, 2 * C), BF),
+    vec=((5, C, 128), F32),
+)
 
 
 def on_device(
@@ -569,93 +761,109 @@
     first_moment,
     second_moment,
 ):
-    groups_a = lax.axis_size(WIN) // 4
+    n_vol, n_win = lax.axis_size(VOL), lax.axis_size(WIN)
+    groups_a, n_plane = n_win // 4, n_win // 2
     steps = tokens.shape[0]
-    params = lax.all_gather(master.astype(BF), (VOL, WIN), axis=0, tiled=True)
-    own_info = jnp.concatenate((window_volume[:, :, None], clip_extent), axis=2)
-    group_info = lax.all_gather(own_info, WIN, axis=1, tiled=True)
-    info = octant_info(group_info, groups_a)
-    params = params.reshape(2 * BLOCK_ROWS, C)
-    weights = [layer_operands(params, n) for n in range(2)]
-
-    def whole(table):
-        return {n: (a, WHOLE) for n, a in table.items()}
-
-    def tables(which):
-        place = (PLAIN, ROLLED)[which]
-        order = (np.eye(T, WS), ORDER)[which]
-        return dict(
-            place=(jnp.asarray(np.broadcast_to(place.T[:3, :, None], (3, T, 128))), WHOLE),
-            order=(jnp.asarray(order, BF), WHOLE),
-            table=(position_bias, which),
-            eye=(jnp.asarray(np.eye(C), BF), WHOLE),
-        )
-
-    perm = jnp.asarray(PERM, BF)
+    shard_len = master.shape[0]
+    device = lax.axis_index((VOL, WIN))
+    slab = slab_rows(shard_len)
+    offset = flat_offset(device, shard_len)
+    shard = lax.dynamic_update_slice(jnp.zeros((slab * C,), BF), master.astype(BF), (offset,))
+    n_peers = n_vol + n_plane - 1
+    weights = call(
+        lambda r: gather_kernel(n_vol, n_plane, shard_len, r),
+        1,
+        dict(shard=(shard.reshape(slab, C), WHOLE)),
+        {n: ((2,) + shape, dtype, WHOLE) for n, (shape, dtype) in WEIGHTS.items()},
+        dict(
+            buf=((2, n_plane, n_vol, slab, C), BF),
+            flat=((2 * BLOCK_ROWS + 8, C), F32),
+        ),
+        dict(sent=(n_peers,), arrived=(n_peers,)),
+        collective_id=0,
+    )
+    info = jnp.concatenate((window_volume[:, :, None], clip_extent), axis=2)[:, 0]
+
+    def layer(which):
+        return {n: (a, which) for n, a in vars(weights).items()}
+
+    def table(which, order):
+        return dict(order=(jnp.asarray(order, BF), WHOLE), table=(position_bias, which))
+
+    perm = (jnp.asarray(PERM, BF), WHOLE)
+    eye = (jnp.asarray(np.eye(CA), BF), WHOLE)
+    stage = dict(stage=((2, T, 2 * CA), BF))
+    copies = dict(sent=(2, 8), arrived=(steps, 8))
     got = call(
-        first_forward_kernel,
+        lambda r: first_forward_kernel(groups_a, steps, r),
         steps,
         dict(
-            tokens=(tokens, BY_STEP),
-            cotangent=(cotangent, BY_STEP),
-            info=(own_info[:, 0], SMEM),
-            perm=(perm, WHOLE),
-            **tables(0),
-            **whole(weights[0]),
+            tokens=(tokens.transpose(0, 1, 3, 2), BY_STEP),
+            cotangent=(cotangent.transpose(0, 1, 3, 2), BY_STEP),
+            info=(info, SMEM),
+            perm=perm,
+            places=(jnp.asarray(PLACES), WHOLE),
+            **table(0, np.eye(T, WS)),
+            **layer(0),
         ),
         dict(
-            sent_x=((steps, T, C), BF, BY_STEP),
-            sent_cot=((steps, T, C), BF, BY_STEP),
+            got=((steps, T, 2 * CA), BF, HBM),
             **{n: ((steps,) + shape, dtype, BY_STEP) for n, (shape, dtype) in KEPT.items()},
         ),
-        dict(**FWD, pad=((2, T, C), BF)),
-    )
-    kept = {n: (getattr(got, n), BY_STEP) for n in KEPT}
-    rows = np.zeros((8, T), np.int32)
-    rows[:4] = ROLLED.T
+        dict(**FWD, **stage, pad=((C, T), BF), cot=((C, T), BF)),
+        copies,
+        collective_id=1,
+    )
     second = call(
-        second_kernel,
+        lambda r: second_kernel(groups_a, steps, r),
         steps,
         dict(
-            got_x=(exchange(got.sent_x, True, groups_a), BY_STEP),
-            got_cot=(exchange(got.sent_cot, True, groups_a), BY_STEP),
-            info=(info, SMEM),
-            places=(jnp.asarray(rows), WHOLE),
-            **tables(1),
-            **whole(weights[1]),
+            came=(got.got, BY_STEP),
+            eye=eye,
+            **table(1, ORDER),
+            **layer(1),
         ),
         dict(
-            sent_out=((steps, T, C), BF, BY_STEP),
-            sent_d=((steps, T, C), BF, BY_STEP),
+            got=((steps, T, 2 * CA), BF, HBM),
             grads=((BLOCK_ROWS, C), F32, WHOLE),
         ),
-        dict(**FWD, **KEPT, **BWD),
+        dict(**FWD, **KEPT, **BWD, **stage),
+        copies,
+        collective_id=2,
     )
     first = call(
-        first_backward_kernel,
+        lambda r: first_backward_kernel(steps, r),
         steps,
         dict(
-            got_out=(exchange(second.sent_out, False, groups_a), BY_STEP),
-            got_d=(exchange(second.sent_d, False, groups_a), BY_STEP),
-            perm=(perm, WHOLE),
-            perm_back=(jnp.asarray(PERM.T, BF), WHOLE),
-            eye=(jnp.asarray(np.eye(C), BF), WHOLE),
-            **kept,
-            **whole(weights[0]),
+            came=(second.got, BY_STEP),
+            perm=perm,
+            eye=(jnp.asarray(np.eye(2 * CA), BF), WHOLE),
+            **{n: (getattr(got, n), BY_STEP) for n in KEPT},
+            **layer(0),
         ),
         dict(
-            output=((steps, 1, WS, C), BF, BY_STEP),
-            input_grad=((steps, 1, WS, C), F32, BY_STEP),
+            output=((steps, 1, C, WS), BF, BY_STEP),
+            input_grad=((steps, 1, C, WS), F32, BY_STEP),
             grads=((BLOCK_ROWS, C), F32, WHOLE),
         ),
         BWD,
     )
-    all_grads = jnp.concatenate((first.grads, second.grads)).reshape(-1)
-    shard_grad = lax.psum_scatter(all_grads, (VOL, WIN), scatter_dimension=0, tiled=True)
-    shard_len = master.shape[0]
-    position = (
-        lax.axis_index((VOL, WIN)) * shard_len + jnp.arange(shard_len, dtype=jnp.int32)
-    ) % (BLOCK_ROWS * C)
+    reduced = call(
+        lambda r: reduce_kernel(n_vol, n_plane, shard_len, r),
+        1,
+        dict(first=(first.grads, WHOLE), second=(second.grads, WHOLE)),
+        dict(total=((slab, C), F32, WHOLE)),
+        dict(
+            work=((2, n_plane, n_vol, slab, C), F32),
+            from_core=((n_plane, n_vol, slab, C), F32),
+            from_plane=((n_plane - 1, n_vol, slab, C), F32),
+            from_vol=((n_vol - 1, slab, C), F32),
+        ),
+        dict(sent=(n_peers,), arrived=(n_peers,)),
+        collective_id=3,
+    )
+    shard_grad = lax.dynamic_slice(reduced.total.reshape(-1), (offset,), (shard_len,))
+    position = (device * shard_len + jnp.arange(shard_len, dtype=jnp.int32)) % (BLOCK_ROWS * C)
     is_vector = position >= 12 * C * C
     step_rate = jnp.where(is_vector, RATE_VECTOR, RATE_MATRIX)
     weight_decay = jnp.where(is_vector, 0.0, DECAY_MATRIX)
@@ -666,8 +874,8 @@
     normalized = corrected_one / (jnp.sqrt(corrected_two) + ADAM_EPS)
     new_master = master - step_rate * (normalized + weight_decay * master)
     return (
-        first.output,
-        first.input_grad,
+        first.output.transpose(0, 1, 3, 2),
+        first.input_grad.transpose(0, 1, 3, 2),
         new_master,
         moment_one,
         moment_two,

time: 664 us -> 297 us (0.45)
  waiting for transfers between devices: 295 us -> 0 us
  local copies, waits for them, and re-layouts: 59.6 us -> 6.5 us
  Pallas kernels: 236 us -> 288 us
  starting transfers between devices: 32.7 us -> 0 us
  between operations: 15 us -> 0.75 us
  other arithmetic: 15 us -> 2.16 us
  blocking collectives: 10.3 us -> 0 us
    unnamed x4 -> x0, waiting for transfers between devices: 235 us -> none
    ppermute x28 -> x0, waiting for transfers between devices: 59.4 us -> none  [exchange(): part = lax.ppermute(part, WIN, pairs)]
    pallas_call x3 -> x5, Pallas kernels: 236 us -> 288 us  [call(): pl.pallas_call(body, grid=(steps,), in_specs=[spec(a.shape, kind) for a,...]
    ppermute x28 -> x0, starting transfers between devices: 32.6 us -> none  [exchange(): part = lax.ppermute(part, WIN, pairs)]
    unnamed x101 -> x7, local copies, waits for them, and re-layouts: 22.9 us -> 3.96 us
    slice x22 -> x0, local copies, waits for them, and re-layouts: 16 us -> none  [the longest x8 9.24 us: exchange(): part = x[:, OCT_OFF[octant]:OCT_OFF[octant] + OCT_LEN[octant]]]
    concatenate x16 -> x0, local copies, waits for them, and re-layouts: 10.9 us -> none  [the longest x5 4.23 us: aug(): jnp.concatenate([matrix, bias[:, None], jnp.zeros((matrix.shape[0], CA -...]
    all_gather x1 -> x0, blocking collectives: 10.3 us -> none  [on_device(): group_info = lax.all_gather(own_info, WIN, axis=1, tiled=True)]
  transfers between devices with their start and end apart: 30 -> 0, of which waited for: 15 -> 0; matrix products, arithmetic and copies ran while one was open for 6% -> 0% of each run, Pallas kernels for 0% -> 0%
where the time goes in v2:
time: 297 us
  Pallas kernels  288 us (97%)
  local copies, waits for them, and re-layouts  6.5 us (2%)
    pallas_call x5, Pallas kernels, call(): pl.pallas_call(body, grid=(steps,), in_specs=[spec(a.shape, kind) for a,...  288 us

profile of v2, /device:TPU:0, one launch (start us, length us, event | category | flops | bytes accessed | tf_op | source)
XLA Modules:
  0.0 297.0 jit_solution(11582762504470371980)
XLA Ops:
  0.7 0.7 pad_add_fusion
  1.3 0.7 copy.21.refs_2_
  2.0 0.8 convert_element_type.6
  2.8 0.3 dynamic_update_slice.3
  3.1 0.7 reshape.18.refs_0_
  3.8 16.9 %shard_map.181 = (bf16[2,288,128]{2,1,0:T(8,128)(2,1)}, bf16[2,128,256]{2,1,0:T(8,128)(2,1)}, bf16[2,96,128]{2,1,0:T(8,128)(2,1)}, bf16[2,96,96]{2,1,0:T(8,128)(...) custom-call(bf16[80,96]{1,0:T(8,128)(2,1)} %reshape.18.refs_0_), custom_call_target="tpu_custom_call" | custom-call | tf_op jit(solution)/shard_map/pallas_call | solution.py:722
  20.7 3.9 %copy.22.refs_6_.refs_3_ = bf16[2,6,343,343]{3,2,1,0:T(8,128)(2,1)} copy(bf16[2,6,343,343]{3,0,2,1:T(2,128)(2,1)} %param.16) | data formatting | bytes 5647152 | tf_op args[2]
  24.6 68.8 %shard_map.182 = (bf16[16,384,256]{2,1,0:T(8,128)(2,1)}, bf16[16,96,384]{2,1,0:T(8,128)(2,1)}, bf16[16,96,384]{2,1,0:T(8,128)(2,1)}, bf16[16,384,128]{2,1,0:T(8,...) custom-call(bf16[16,1,96,343]{3,2,1,0:T(8,128)(2,1)} %bitcast.8, ...), custom_call_target="tpu_custom_call" | custom-call | tf_op jit(solution)/shard_map/pallas_call | solution.py:722
  93.5 117.3 %shard_map.183 = (bf16[16,384,256]{2,1,0:T(8,128)(2,1)}, f32[1164,96]{1,0:T(8,128)}) custom-call(bf16[16,384,256]{2,1,0:T(8,128)(2,1)} %get-tuple-element.47.refs_0_, bf16[128,128]{1,0:T(8,128)(2,1)} %constant.69.clone.refs_1_, bf16[384,343]{1,0:T(8,128)(2,1)} %constant.72.clone.refs_2_, bf16[2,6,343,343]{3,2,1,0:T(8,128)(2,1)} %copy.22.refs_6_.refs_3_, ...), custom_call_target="tpu_custom_call" | custom-call | tf_op jit(solution)/shard_map/pallas_call | solution.py:722
  210.8 0.0 copy-start
  210.8 0.0 copy-start.1
  210.8 0.0 copy-start.2
  210.8 64.4 %shard_map.184 = (bf16[16,1,96,343]{3,2,1,0:T(8,128)(2,1)}, f32[16,1,96,343]{3,2,1,0:T(8,128)}, f32[1164,96]{1,0:T(8,128)}) custom-call(bf16[16,384,256]{2,1,0:T(8,128)(2,1)} %get-tuple-element.48.refs_0_, bf16[384,384]{1,0:T(8,128)(2,1)} %constant.68.clone.refs_3_.refs_1_, bf16[256,256]{1,0:T(8,128)(2,1)} %constant.73.clone.refs_2_, ...), custom_call_target="tpu_custom_call" | custom-call | tf_op jit(solution)/shard_map/pallas_call | solution.py:722
  275.2 20.2 %shard_map.185 = f32[80,96]{1,0:T(8,128)} custom-call(f32[1164,96]{1,0:T(8,128)} %get-tuple-element.64.refs_0_, f32[1164,96]{1,0:T(8,128)} %get-tuple-element.65.refs_1_), custom_call_target="tpu_custom_call" | custom-call | tf_op jit(solution)/shard_map/pallas_call | solution.py:722
  295.4 0.9 reshape.19
  296.3 0.0 copy-done
  296.3 0.0 copy-done.1
  296.3 0.0 copy-done.2
  296.3 0.7 fusion.5
  (1 shorter events, 0.0 us)
Async XLA Ops:
  210.8 85.5 %copy-start = (f32[6984]{0:T(1024)S(1)}, f32[6984]{0:T(1024)}, u32[]{:S(2)}) copy-start(f32[6984]{0:T(1024)} %param.19) | copy-start | bytes 83812
  210.8 85.5 %copy-start.1 = (f32[6984]{0:T(1024)S(1)}, f32[6984]{0:T(1024)}, u32[]{:S(2)}) copy-start(f32[6984]{0:T(1024)} %param.20) | copy-start | bytes 83812
  210.8 85.5 %copy-start.2 = (f32[6984]{0:T(1024)S(1)}, f32[6984]{0:T(1024)}, u32[]{:S(2)}) copy-start(f32[6984]{0:T(1024)} %param.21) | copy-start | bytes 83812

commit v3 on v2

--- a/solution.py
+++ b/solution.py
@@ -17,6 +17,7 @@
 WS = 343
 STEP = 6
 T = 384
+WINDOWS = 2
 CA = 128
 BLOCK_ROWS = 1164
 
@@ -120,19 +121,33 @@
     return jnp.where(lax.broadcasted_iota(jnp.int32, shape, 0) == row, 1.0, 0.0)
 
 
-def init_forward(r, sc):
-    sc.qb[...] = jnp.zeros((CA, HEADS * T), BF)
+def weave(tasks, lag):
+    clocks = [lag * n for n in range(len(tasks))]
+    while tasks:
+        n = clocks.index(min(clocks))
+        cost = next(tasks[n], None)
+        if cost is None:
+            tasks, clocks = (x[:n] + x[n + 1 :] for x in (tasks, clocks))
+        else:
+            clocks[n] += cost
+
+
+def init_forward(r, windows):
+    for sc in windows:
+        sc.qb[...] = jnp.zeros((CA, HEADS * T), BF)
+        for h in range(HEADS):
+            sc.vt[h, 16:32, :] = ones_row((16, T)).astype(BF)
     for h in range(HEADS):
-        sc.vt[h, 16:32, :] = ones_row((16, T)).astype(BF)
         turned = dot(r.order[...], r.table[h], NT).astype(BF)
-        sc.bias[h] = dot(turned, r.order[...], NT)
-
-
-def init_backward(sc):
-    sc.dab[...] = jnp.zeros((CA, HEADS * T), BF)
-    sc.rb[...] = jnp.zeros((2 * C, 2 * HEADS * T), BF)
+        r.bias[h] = dot(turned, r.order[...], NT)
+
+
+def init_backward(r, windows):
+    for sc in windows:
+        sc.dab[...] = jnp.zeros((CA, HEADS * T), BF)
+        sc.rb[...] = jnp.zeros((2 * C, 2 * HEADS * T), BF)
     for name, (shape, dtype) in GRADS.items():
-        getattr(sc, name)[...] = jnp.zeros(shape, dtype)
+        getattr(r, name)[...] = jnp.zeros(shape, dtype)
 
 
 def set_queries(sc, queries):
@@ -140,11 +155,16 @@
         sc.qb[16 * h : 16 * h + 16, T * h : T * h + T] = queries[16 * h : 16 * h + 16, :]
 
 
-def forward_attention(sc, w, x, code_row):
-    z, _ = ln_stats(x)
+def forward_attention(sc, w, st, code_row):
+    z, _ = ln_stats(st.x)
     sc.n1aug[C:CA, :] = ones_row((CA - C, T)).astype(BF)
     sc.attaug[C:CA, :] = ones_row((CA - C, T)).astype(BF)
     sc.n1aug[0:C, :] = (z * wide(w.vec[0]) + wide(w.vec[1])).astype(BF)
+    yield 150
+    kv = dot(sc.n1aug[...].T, w.kv[...]).astype(BF)
+    sc.kn[...] = kv[:, 0:CA]
+    sc.vn[...] = kv[:, CA:]
+    yield 200
     qkv = dot(w.qkvT[...], sc.n1aug[...])
     queries = qkv[0:C].astype(BF)
     set_queries(sc, queries)
@@ -153,9 +173,7 @@
     values = qkv[2 * C :].astype(BF)
     for h in range(HEADS):
         sc.vt[h, 0:16, :] = values[16 * h : 16 * h + 16, :]
-    kv = dot(sc.n1aug[...].T, w.kv[...]).astype(BF)
-    sc.kn[...] = kv[:, 0:CA]
-    sc.vn[...] = kv[:, CA:]
+    yield 150
     eye = lax.broadcasted_iota(jnp.int32, (128, 128), 0) == lax.broadcasted_iota(
         jnp.int32, (128, 128), 1
     )
@@ -189,7 +207,7 @@
         sc.inv[h : h + 1, :] = inverse
         sc.attaug[16 * h : 16 * h + 16, :] = part.astype(BF)
 
-    for h in range(HEADS + 3):
+    for h in range(HEADS + 2):
         for c in range(3):
             if h < HEADS:
                 scores(h, c)
@@ -197,15 +215,19 @@
                 raise_(h - 1, c)
             if c == 0 and 0 <= h - 2 < HEADS:
                 attend(h - 2)
+            yield 70
         if h < HEADS:
             tops[h] = jnp.max(tops[h], axis=0, keepdims=True)
-    return dot(w.projT[...], sc.attaug[...])
-
-
-def backward_attention(sc, w, d_mid, z, scale, shifted):
+    st.branch = dot(w.projT[...], sc.attaug[...])
+    yield 100
+
+
+def backward_attention(sc, w, st, z, scale, shifted):
+    d_mid = st.d
     db = d_mid.astype(BF)
+    d_att = dot(w.proj[...], db).astype(BF).astype(F32)
     sc.gproj[...] += dot(sc.attaug[...], db, NT)
-    d_att = dot(w.proj[...], db).astype(BF).astype(F32)
+    yield 150
     row = lax.broadcasted_iota(jnp.int32, (16, T), 0)
     for h in range(HEADS):
         part = (d_att[16 * h : 16 * h + 16] * sc.inv[h : h + 1, :]).astype(BF)
@@ -223,6 +245,7 @@
         sc.dab[C : C + 16, cols] = jnp.where(
             row == 0, high, jnp.where(row == 1, low, 0.0)
         ).astype(BF)
+    yield 100
     total = None
 
     def soft(h):
@@ -238,32 +261,42 @@
     for h in range(HEADS + 1):
         if h < HEADS:
             soft(h)
+            yield 120
         if h > 0:
             cols = slice(T * (h - 1), T * h)
             to_queries(h - 1)
+            yield 60
             both = jnp.concatenate([sc.e[:, cols], sc.ds[:, cols]], axis=1)
             term = dot(both, sc.rb[:, 2 * T * (h - 1) : 2 * T * h], NT)
             total = term if total is None else total + term
+            yield 180
     dkv = total.astype(BF)
     dq = sc.dq[...]
+    dn = dot(w.q[...], dq) + dot(w.kv96[...], dkv, NT)
+    yield 120
     sc.gkv[...] += dot(sc.n1aug[...], dkv)
     sc.gq[...] += dot(dq, sc.n1aug[...], NT)
-    dn = dot(w.q[...], dq) + dot(w.kv96[...], dkv, NT)
+    yield 150
     if shifted:
         dn = dn.astype(BF).astype(F32)
     sc.gvec[0] += dn * z
     sc.gvec[1] += dn
-    return d_mid + norm_back(dn, z, scale, wide(w.vec[0]))
-
-
-def feed_forward_back(sc, w, d, dd, z, scale):
+    st.d = d_mid + norm_back(dn, z, scale, wide(w.vec[0]))
+    yield 150
+
+
+def feed_forward_back(sc, w, st, dd, z, scale):
+    dn = dot(w.up[...], sc.dh[...])
+    yield 120
     sc.gdown[...] += dot(sc.act[...], dd, NT)
+    yield 120
     sc.gup[...] += dot(sc.dh[...], sc.n2aug[...], NT)
+    yield 120
     sc.gvec[4] += dd.astype(F32)
-    dn = dot(w.up[...], sc.dh[...])
     sc.gvec[2] += dn * z
     sc.gvec[3] += dn
-    return d + norm_back(dn, z, scale, wide(w.vec[2]))
+    st.d = st.d + norm_back(dn, z, scale, wide(w.vec[2]))
+    yield 150
 
 
 def write_grads(sc, out):
@@ -297,9 +330,9 @@
     vt=((HEADS, 32, T), BF),
     kn=((T, CA), BF),
     codes=((T, 128), F32),
-    bias=((HEADS, T, T), F32),
     s=((3, T, T), F32),
 )
+BIAS = dict(bias=((HEADS, T, T), F32))
 KEPT = dict(
     qT=((C, T), BF),
     kT=((C, T), BF),
@@ -324,7 +357,6 @@
     gvec=((5, C, T), F32),
 )
 BWD = dict(
-    **GRADS,
     dab=((CA, HEADS * T), BF),
     rb=((2 * C, 2 * HEADS * T), BF),
     ds=((T, HEADS * T), BF),
@@ -333,8 +365,15 @@
 )
 
 
-def by_step(r):
-    return SimpleNamespace(**{**vars(r), **{n: getattr(r, n).at[0] for n in KEPT}})
+PADS = dict(pad=((C, T), BF), cot=((C, T), BF))
+LAGS = (0, 0, 0)
+
+
+def by_window(r, own):
+    return [
+        SimpleNamespace(**{**vars(r), **{n: getattr(r, n).at[i] for n in own if hasattr(r, n)}})
+        for i in range(WINDOWS)
+    ]
 
 
 def second_norm(sc, w, x):
@@ -361,18 +400,23 @@
     barrier = pltpu.get_barrier_semaphore()
     for peer in peers:
         pl.semaphore_signal(barrier, inc=1, device_id=peer, device_id_type=MESH)
-    pl.semaphore_wait(barrier, len(peers))
+
+
+def await_greetings(peers):
+    pl.semaphore_wait(pltpu.get_barrier_semaphore(), len(peers))
 
 
 def block_copy(r, m, octant, sign, groups_a):
     rows = pl.ds(OCT_OFF[octant], OCT_LEN[octant])
-    source, target = r.stage.at[m % 2, rows], r.got.at[m, rows]
+    slot = m % 2
+    source = r.stage.at[slot, :, rows]
+    target = r.got.at[pl.ds(m * WINDOWS, WINDOWS), rows]
     if octant == 0:
-        return pltpu.make_async_copy(source, target, r.sent.at[m % 2, 0])
+        return pltpu.make_async_copy(source, target, r.sent.at[slot, 0])
     return pltpu.make_async_remote_copy(
         src_ref=source,
         dst_ref=target,
-        send_sem=r.sent.at[m % 2, octant],
+        send_sem=r.sent.at[slot, octant],
         recv_sem=r.arrived.at[m, octant],
         device_id=neighbour(octant, sign, groups_a),
         device_id_type=MESH,
@@ -386,6 +430,10 @@
 
 
 def send_blocks(r, m, sign, groups_a):
+    @pl.when(m == 0)
+    def _():
+        pl.semaphore_wait(pltpu.get_barrier_semaphore(), 7)
+
     for octant in range(8):
         block_copy(r, m, octant, sign, groups_a).start()
 
@@ -402,51 +450,64 @@
     lax.fori_loop(0, steps, arrival, 0)
 
 
-def first_forward_kernel(groups_a, steps, r):
-    w, sc = r, by_step(r)
+def first_forward(r, sc, m, i):
+    w, st = r, SimpleNamespace()
+    slot = m % 2
+    sc.pad[:, 0:WS] = r.tokens[i, 0]
+    st.x = sc.pad[...].astype(F32)
+    sc.xT[...] = st.x
+    places = r.places
+    valid = (
+        (places[0:1, :] < r.info[m * WINDOWS + i, 1])
+        & (places[1:2, :] < r.info[m * WINDOWS + i, 2])
+        & (places[2:3, :] < r.info[m * WINDOWS + i, 3])
+    )
+    valid = jnp.where(valid, 1.0, 0.0)
+    sc.codes[...] = jnp.broadcast_to(valid - 1.0, (128, T)).T
+    yield 100
+    yield from forward_attention(sc, w, st, jnp.zeros((1, T), F32))
+    sc.cot[:, 0:WS] = r.cotangent[i, 0]
+    r.stage[slot, i, :, CA:] = jnp.concatenate(
+        [dot(r.perm[...], sc.cot[...], NT), jnp.zeros((T, CA - C), F32)], axis=1
+    ).astype(BF)
+    yield 100
+    x = st.x + st.branch
+    sc.x1[...] = x
+    second_norm(sc, w, x)
+    yield 150
+    for c in range(6):
+        rows = slice(64 * c, 64 * c + 64)
+        active, slope = gelu_pair(dot(w.upT[rows], sc.n2aug[...]))
+        sc.act[rows, :] = active.astype(BF)
+        sc.gp[rows, :] = slope.astype(BF)
+        yield 100
+    x = x + (dot(w.downT[...], sc.act[...]) + wide(w.vec[4]))
+    yield 100
+    row = lax.broadcasted_iota(jnp.int32, (CA - C, T), 0)
+    label = r.info[m * WINDOWS + i, 0].astype(F32)
+    extra = jnp.where(row == 0, label, jnp.where(row == 1, valid, 0.0))
+    x = jnp.concatenate([x, extra], axis=0).astype(BF)
+    r.stage[slot, i, :, 0:CA] = dot(r.perm[...], x, NT).astype(BF)
+    yield 100
+
+
+def first_forward_kernel(groups_a, steps, lag, r):
+    windows = by_window(r, dict(**FWD, **KEPT, **PADS))
     m = pl.program_id(0)
 
     @pl.when(m == 0)
     def _():
         greet([neighbour(octant, 1, groups_a) for octant in range(1, 8)])
-        init_forward(r, sc)
-        sc.pad[...] = jnp.zeros((C, T), BF)
-        sc.cot[...] = jnp.zeros((C, T), BF)
+        init_forward(r, windows)
+        for sc in windows:
+            sc.pad[...] = jnp.zeros((C, T), BF)
+            sc.cot[...] = jnp.zeros((C, T), BF)
 
     @pl.when(m >= 2)
     def _():
         wait_sent(r, m - 2, -1, groups_a)
 
-    sc.pad[:, 0:WS] = r.tokens[0, 0]
-    sc.cot[:, 0:WS] = r.cotangent[0, 0]
-    slot = m % 2
-    r.stage[slot, :, CA:] = jnp.concatenate(
-        [dot(r.perm[...], sc.cot[...], NT), jnp.zeros((T, CA - C), F32)], axis=1
-    ).astype(BF)
-    places = r.places
-    valid = (
-        (places[0:1, :] < r.info[m, 1])
-        & (places[1:2, :] < r.info[m, 2])
-        & (places[2:3, :] < r.info[m, 3])
-    )
-    valid = jnp.where(valid, 1.0, 0.0)
-    sc.codes[...] = jnp.broadcast_to(valid - 1.0, (128, T)).T
-    x = sc.pad[...].astype(F32)
-    sc.xT[...] = x
-    x = x + forward_attention(sc, w, x, jnp.zeros((1, T), F32))
-    sc.x1[...] = x
-    second_norm(sc, w, x)
-    for c in range(3):
-        rows = slice(128 * c, 128 * c + 128)
-        active, slope = gelu_pair(dot(w.upT[rows], sc.n2aug[...]))
-        sc.act[rows, :] = active.astype(BF)
-        sc.gp[rows, :] = slope.astype(BF)
-    x = x + (dot(w.downT[...], sc.act[...]) + wide(w.vec[4]))
-    row = lax.broadcasted_iota(jnp.int32, (CA - C, T), 0)
-    label = r.info[m, 0].astype(F32)
-    extra = jnp.where(row == 0, label, jnp.where(row == 1, valid, 0.0))
-    x = jnp.concatenate([x, extra], axis=0).astype(BF)
-    r.stage[slot, :, 0:CA] = dot(r.perm[...], x, NT).astype(BF)
+    weave([first_forward(r, sc, m, i) for i, sc in enumerate(windows)], lag)
     send_blocks(r, m, -1, groups_a)
 
     @pl.when(m == steps - 1)
@@ -454,29 +515,17 @@
         finish_blocks(r, steps, -1, groups_a)
 
 
-def second_kernel(groups_a, steps, r):
-    w, sc = r, r
-    m = pl.program_id(0)
-
-    @pl.when(m == 0)
-    def _():
-        greet([neighbour(octant, -1, groups_a) for octant in range(1, 8)])
-        init_forward(r, sc)
-        init_backward(sc)
-
-    @pl.when(m >= 2)
-    def _():
-        wait_sent(r, m - 2, 1, groups_a)
-
-    came = r.came[0, :, 0:CA]
+def second_layer(r, sc, m, i, groups_a):
+    w, st = r, SimpleNamespace()
+    came = r.came[i, :, 0:CA]
     x = dot(r.eye[...], came, NT)
     place, sizes = grid_place(groups_a)
     code_row = []
     for octant in range(8):
         rows = slice(OCT_OFF[octant], OCT_OFF[octant] + OCT_LEN[octant])
         wraps = [
-            bit * jnp.where(p == n - 1, 1, 0)
-            for p, bit, n in zip(place, octant_bits(octant), sizes)
+            bit * jnp.where(p == n_ - 1, 1, 0)
+            for p, bit, n_ in zip(place, octant_bits(octant), sizes)
         ]
         wrap = (wraps[0] * 4 + wraps[1] * 2 + wraps[2]).astype(F32)
         columns = came[rows].astype(F32)
@@ -486,58 +535,92 @@
     code_row = jnp.concatenate(code_row, axis=1) + 8.0 * x[C : C + 1]
     keep = x[C + 1 : C + 2]
     x = x[0:C]
-    d = dot(r.eye[0:C], r.came[0, :, CA:], NT) * keep
-    dd = d.astype(BF)
     sc.xT[...] = x
-    branch = forward_attention(sc, w, x, code_row)
-    x = x + branch.astype(BF).astype(F32)
+    st.x = x
+    yield 150
+    yield from forward_attention(sc, w, st, code_row)
+    st.d = dot(r.eye[0:C], r.came[i, :, CA:], NT) * keep
+    dd = st.d.astype(BF)
+    x = sc.xT[...] + st.branch.astype(BF).astype(F32)
     z, scale = second_norm(sc, w, x)
-    for c in range(3):
-        rows = slice(128 * c, 128 * c + 128)
+    yield 200
+    for c in range(6):
+        rows = slice(64 * c, 64 * c + 64)
         active, slope = gelu_pair(dot(w.upT[rows], sc.n2aug[...]))
         sc.act[rows, :] = active.astype(BF)
         sc.dh[rows, :] = (dot(w.down[rows], dd) * slope).astype(BF)
+        yield 120
     x = x + (dot(w.downT[...], sc.act[...]) + wide(w.vec[4]))
     slot = m % 2
     none = jnp.zeros((CA - C, T), F32)
-    r.stage[slot, :, 0:CA] = jnp.concatenate([x * keep, none], axis=0).T.astype(BF)
-    d = feed_forward_back(sc, w, d, dd, z, scale)
+    r.stage[slot, i, :, 0:CA] = jnp.concatenate([x * keep, none], axis=0).T.astype(BF)
+    yield 150
+    yield from feed_forward_back(sc, w, st, dd, z, scale)
     z, scale = ln_stats(sc.xT[...])
-    d = backward_attention(sc, w, d, z, scale, True)
-    r.stage[slot, :, CA:] = jnp.concatenate([d, none], axis=0).T.astype(BF)
+    yield from backward_attention(sc, w, st, z, scale, True)
+    r.stage[slot, i, :, CA:] = jnp.concatenate([st.d, none], axis=0).T.astype(BF)
+    yield 100
+
+
+def second_kernel(groups_a, steps, lag, r):
+    windows = by_window(r, dict(**FWD, **KEPT, **BWD))
+    m = pl.program_id(0)
+
+    @pl.when(m == 0)
+    def _():
+        greet([neighbour(octant, -1, groups_a) for octant in range(1, 8)])
+        init_forward(r, windows)
+        init_backward(r, windows)
+
+    @pl.when(m >= 2)
+    def _():
+        wait_sent(r, m - 2, 1, groups_a)
+
+    weave(
+        [second_layer(r, sc, m, i, groups_a) for i, sc in enumerate(windows)], lag
+    )
     send_blocks(r, m, 1, groups_a)
 
     @pl.when(m == steps - 1)
     def _():
         finish_blocks(r, steps, 1, groups_a)
-        write_grads(sc, r.grads)
-
-
-def first_backward_kernel(steps, r):
-    w, sc = r, by_step(r)
-    m = pl.program_id(0)
-
-    @pl.when(m == 0)
-    def _():
-        init_backward(sc)
-
-    came = dot(r.eye[...], r.came[0], NT).astype(BF)
+        write_grads(r, r.grads)
+
+
+def first_backward(r, sc, i):
+    w, st = r, SimpleNamespace()
+    came = dot(r.eye[...], r.came[i], NT).astype(BF)
+    yield 200
     came = dot(came, r.perm[...])
-    r.output[0, 0] = came[0:C, 0:WS].astype(BF)
-    d = came[CA : CA + C]
-    dd = d.astype(BF)
+    r.output[i, 0] = came[0:C, 0:WS].astype(BF)
+    st.d = came[CA : CA + C]
+    dd = st.d.astype(BF)
     z, scale = ln_stats(sc.x1[...])
+    yield 200
     for c in range(3):
         rows = slice(128 * c, 128 * c + 128)
         sc.dh[rows, :] = (dot(w.down[rows], dd) * sc.gp[rows, :].astype(F32)).astype(BF)
-    d = feed_forward_back(sc, w, d, dd, z, scale)
+        yield 50
+    yield from feed_forward_back(sc, w, st, dd, z, scale)
     z, scale = ln_stats(sc.xT[...])
-    d = backward_attention(sc, w, d, z, scale, False)
-    r.input_grad[0, 0] = d[:, 0:WS]
+    yield from backward_attention(sc, w, st, z, scale, False)
+    r.input_grad[i, 0] = st.d[:, 0:WS]
+    yield 50
+
+
+def first_backward_kernel(steps, lag, r):
+    windows = by_window(r, dict(**KEPT, **BWD))
+    m = pl.program_id(0)
+
+    @pl.when(m == 0)
+    def _():
+        init_backward(r, windows)
+
+    weave([first_backward(r, sc, i) for i, sc in enumerate(windows)], lag)
 
     @pl.when(m == steps - 1)
     def _():
-        write_grads(sc, r.grads)
+        write_grads(r, r.grads)
 
 
 def shard_rows(device, shard_len):
@@ -575,6 +658,7 @@
     vol, plane, core = own_place()
     peers = all_peers(n_vol, n_plane)
     greet(peers)
+    await_greetings(peers)
     buf = r.buf
 
     def copy(ref, n):
@@ -649,6 +733,7 @@
     vol, plane, core = own_place()
     peers = all_peers(n_vol, n_plane)
     greet(peers)
+    await_greetings(peers)
     work = r.work
     half = 2 * n_vol * n_plane // 2
     for v in range(n_vol):
@@ -708,7 +793,7 @@
             return pl.BlockSpec(memory_space=pl.ANY)
         zeros = (0,) * (len(shape) - 1)
         if kind is BY_STEP:
-            return pl.BlockSpec((1,) + tuple(shape[1:]), lambda m: (m,) + zeros)
+            return pl.BlockSpec((shape[0] // steps,) + tuple(shape[1:]), lambda m: (m,) + zeros)
         if kind in (0, 1):
             return pl.BlockSpec((pl.squeezed,) + tuple(shape[1:]), lambda m: (kind,) + zeros)
         return pl.BlockSpec(tuple(shape), lambda m: (0,) + zeros)
@@ -763,7 +848,8 @@
 ):
     n_vol, n_win = lax.axis_size(VOL), lax.axis_size(WIN)
     groups_a, n_plane = n_win // 4, n_win // 2
-    steps = tokens.shape[0]
+    count = tokens.shape[0]
+    steps = count // WINDOWS
     shard_len = master.shape[0]
     device = lax.axis_index((VOL, WIN))
     slab = slab_rows(shard_len)
@@ -784,6 +870,9 @@
     )
     info = jnp.concatenate((window_volume[:, :, None], clip_extent), axis=2)[:, 0]
 
+    def each(table):
+        return {n: ((WINDOWS,) + shape, dtype) for n, (shape, dtype) in table.items()}
+
     def layer(which):
         return {n: (a, which) for n, a in vars(weights).items()}
 
@@ -792,10 +881,10 @@
 
     perm = (jnp.asarray(PERM, BF), WHOLE)
     eye = (jnp.asarray(np.eye(CA), BF), WHOLE)
-    stage = dict(stage=((2, T, 2 * CA), BF))
+    stage = dict(stage=((2, WINDOWS, T, 2 * CA), BF))
     copies = dict(sent=(2, 8), arrived=(steps, 8))
     got = call(
-        lambda r: first_forward_kernel(groups_a, steps, r),
+        lambda r: first_forward_kernel(groups_a, steps, LAGS[0], r),
         steps,
         dict(
             tokens=(tokens.transpose(0, 1, 3, 2), BY_STEP),
@@ -807,15 +896,15 @@
             **layer(0),
         ),
         dict(
-            got=((steps, T, 2 * CA), BF, HBM),
-            **{n: ((steps,) + shape, dtype, BY_STEP) for n, (shape, dtype) in KEPT.items()},
+            got=((count, T, 2 * CA), BF, HBM),
+            **{n: ((count,) + shape, dtype, BY_STEP) for n, (shape, dtype) in KEPT.items()},
         ),
-        dict(**FWD, **stage, pad=((C, T), BF), cot=((C, T), BF)),
+        dict(**BIAS, **stage, **each(FWD), **each(PADS)),
         copies,
         collective_id=1,
     )
     second = call(
-        lambda r: second_kernel(groups_a, steps, r),
+        lambda r: second_kernel(groups_a, steps, LAGS[1], r),
         steps,
         dict(
             came=(got.got, BY_STEP),
@@ -824,15 +913,15 @@
             **layer(1),
         ),
         dict(
-            got=((steps, T, 2 * CA), BF, HBM),
+            got=((count, T, 2 * CA), BF, HBM),
             grads=((BLOCK_ROWS, C), F32, WHOLE),
         ),
-        dict(**FWD, **KEPT, **BWD, **stage),
+        dict(**BIAS, **stage, **GRADS, **each(FWD), **each(KEPT), **each(BWD)),
         copies,
         collective_id=2,
     )
     first = call(
-        lambda r: first_backward_kernel(steps, r),
+        lambda r: first_backward_kernel(steps, LAGS[2], r),
         steps,
         dict(
             came=(second.got, BY_STEP),
@@ -842,11 +931,11 @@
             **layer(0),
         ),
         dict(
-            output=((steps, 1, C, WS), BF, BY_STEP),
-            input_grad=((steps, 1, C, WS), F32, BY_STEP),
+            output=((count, 1, C, WS), BF, BY_STEP),
+            input_grad=((count, 1, C, WS), F32, BY_STEP),
             grads=((BLOCK_ROWS, C), F32, WHOLE),
         ),
-        BWD,
+        dict(**GRADS, **each(BWD)),
     )
     reduced = call(
         lambda r: reduce_kernel(n_vol, n_plane, shard_len, r),

time: 297 us -> 249 us (0.84)
  Pallas kernels: 288 us -> 239 us
    pallas_call x5, Pallas kernels: 288 us -> 239 us  [call(): pl.pallas_call(body, grid=(steps,), in_specs=[spec(a.shape, kind) for a,...]
where the time goes in v3:
time: 249 us
  Pallas kernels  239 us (96%)
  local copies, waits for them, and re-layouts  6.5 us (3%)
    pallas_call x5, Pallas kernels, call(): pl.pallas_call(body, grid=(steps,), in_specs=[spec(a.shape, kind) for a,...  239 us

profile of v3, /device:TPU:0, one launch (start us, length us, event | category | flops | bytes accessed | tf_op | source)
XLA Modules:
  0.0 248.7 jit_solution(11457736978667005006)
XLA Ops:
  0.7 0.7 pad_add_fusion
  1.3 0.7 copy.21.refs_2_
  2.0 0.8 convert_element_type.6
  2.8 0.3 dynamic_update_slice.3
  3.1 0.7 reshape.18.refs_0_
  3.8 16.9 %shard_map.181 = (bf16[2,288,128]{2,1,0:T(8,128)(2,1)}, bf16[2,128,256]{2,1,0:T(8,128)(2,1)}, bf16[2,96,128]{2,1,0:T(8,128)(2,1)}, bf16[2,96,96]{2,1,0:T(8,128)(...) custom-call(bf16[80,96]{1,0:T(8,128)(2,1)} %reshape.18.refs_0_), custom_call_target="tpu_custom_call" | custom-call | tf_op jit(solution)/shard_map/pallas_call | solution.py:807
  20.7 3.9 %copy.22.refs_6_.refs_3_ = bf16[2,6,343,343]{3,2,1,0:T(8,128)(2,1)} copy(bf16[2,6,343,343]{3,0,2,1:T(2,128)(2,1)} %param.16) | data formatting | bytes 5647152 | tf_op args[2]
  24.6 60.3 %shard_map.182 = (bf16[16,384,256]{2,1,0:T(8,128)(2,1)}, bf16[16,96,384]{2,1,0:T(8,128)(2,1)}, bf16[16,96,384]{2,1,0:T(8,128)(2,1)}, bf16[16,384,128]{2,1,0:T(8,...) custom-call(bf16[16,1,96,343]{3,2,1,0:T(8,128)(2,1)} %bitcast.8, ...), custom_call_target="tpu_custom_call" | custom-call | tf_op jit(solution)/shard_map/pallas_call | solution.py:807
  84.9 93.0 %shard_map.183 = (bf16[16,384,256]{2,1,0:T(8,128)(2,1)}, f32[1164,96]{1,0:T(8,128)}) custom-call(bf16[16,384,256]{2,1,0:T(8,128)(2,1)} %get-tuple-element.47.refs_0_, bf16[128,128]{1,0:T(8,128)(2,1)} %constant.69.clone.refs_1_, bf16[384,343]{1,0:T(8,128)(2,1)} %constant.72.clone.refs_2_, bf16[2,6,343,343]{3,2,1,0:T(8,128)(2,1)} %copy.22.refs_6_.refs_3_, ...), custom_call_target="tpu_custom_call" | custom-call | tf_op jit(solution)/shard_map/pallas_call | solution.py:807
  177.9 0.0 copy-start
  177.9 0.0 copy-start.1
  177.9 0.0 copy-start.2
  178.0 48.9 %shard_map.184 = (bf16[16,1,96,343]{3,2,1,0:T(8,128)(2,1)}, f32[16,1,96,343]{3,2,1,0:T(8,128)}, f32[1164,96]{1,0:T(8,128)}) custom-call(bf16[16,384,256]{2,1,0:T(8,128)(2,1)} %get-tuple-element.48.refs_0_, bf16[384,384]{1,0:T(8,128)(2,1)} %constant.68.clone.refs_3_.refs_1_, bf16[256,256]{1,0:T(8,128)(2,1)} %constant.73.clone.refs_2_, ...), custom_call_target="tpu_custom_call" | custom-call | tf_op jit(solution)/shard_map/pallas_call | solution.py:807
  226.8 20.3 %shard_map.185 = f32[80,96]{1,0:T(8,128)} custom-call(f32[1164,96]{1,0:T(8,128)} %get-tuple-element.64.refs_0_, f32[1164,96]{1,0:T(8,128)} %get-tuple-element.65.refs_1_), custom_call_target="tpu_custom_call" | custom-call | tf_op jit(solution)/shard_map/pallas_call | solution.py:807
  247.1 0.9 reshape.19
  247.9 0.0 copy-done
  248.0 0.0 copy-done.1
  248.0 0.0 copy-done.2
  248.0 0.7 fusion.5
  (1 shorter events, 0.0 us)
Async XLA Ops:
  177.9 70.0 %copy-start = (f32[6984]{0:T(1024)S(1)}, f32[6984]{0:T(1024)}, u32[]{:S(2)}) copy-start(f32[6984]{0:T(1024)} %param.19) | copy-start | bytes 83812
  177.9 70.0 %copy-start.1 = (f32[6984]{0:T(1024)S(1)}, f32[6984]{0:T(1024)}, u32[]{:S(2)}) copy-start(f32[6984]{0:T(1024)} %param.20) | copy-start | bytes 83812
  177.9 70.0 %copy-start.2 = (f32[6984]{0:T(1024)S(1)}, f32[6984]{0:T(1024)}, u32[]{:S(2)}) copy-start(f32[6984]{0:T(1024)} %param.21) | copy-start | bytes 83812

commit v4 on v3

--- a/solution.py
+++ b/solution.py
@@ -18,6 +18,7 @@
 STEP = 6
 T = 384
 WINDOWS = 2
+TABLE_SLOTS = 4
 CA = 128
 BLOCK_ROWS = 1164
 
@@ -34,9 +35,10 @@
 F32 = jnp.float32
 NN = (((1,), (0,)), ((), ()))
 NT = (((1,), (1,)), ((), ()))
-BY_STEP, WHOLE, SMEM, HBM = -1, -2, -3, -4
+BY_STEP, WHOLE, SMEM, HBM = range(4)
 MESH = pl.DeviceIdType.MESH
 VOL, WIN = "vol", "win"
+KEPT_NAMES = ("a0", "a1"), ("b0", "b1")
 
 
 def octant_bits(octant):
@@ -132,22 +134,34 @@
             clocks[n] += cost
 
 
-def init_forward(r, windows):
-    for sc in windows:
-        sc.qb[...] = jnp.zeros((CA, HEADS * T), BF)
+def clear_scratch(r):
+    zeros = jnp.zeros((CA, HEADS * T), BF)
+    for i in range(WINDOWS):
+        r.qb[i] = zeros
+        r.dab[i] = zeros
+        r.rb[i] = jnp.zeros((2, 2 * C, 2 * T), BF)
+        r.pad[i] = jnp.zeros((C, T), BF)
+        r.cot[i] = jnp.zeros((C, T), BF)
         for h in range(HEADS):
-            sc.vt[h, 16:32, :] = ones_row((16, T)).astype(BF)
-    for h in range(HEADS):
-        turned = dot(r.order[...], r.table[h], NT).astype(BF)
-        r.bias[h] = dot(turned, r.order[...], NT)
-
-
-def init_backward(r, windows):
-    for sc in windows:
-        sc.dab[...] = jnp.zeros((CA, HEADS * T), BF)
-        sc.rb[...] = jnp.zeros((2 * C, 2 * HEADS * T), BF)
+            r.vt[i, h, 16:32, :] = ones_row((16, T)).astype(BF)
     for name, (shape, dtype) in GRADS.items():
-        getattr(r, name)[...] = jnp.zeros(shape, dtype)
+        getattr(r, name)[...] = jnp.zeros((2,) + shape, dtype)
+
+
+def table_copy(r, n):
+    slot = n % TABLE_SLOTS
+    return pltpu.make_async_copy(
+        r.table.at[n // HEADS, n % HEADS], r.page.at[slot], r.turned.at[slot]
+    )
+
+
+def turn_tables(r, layer):
+    for n in range(HEADS * layer, HEADS * layer + HEADS):
+        table_copy(r, n).wait()
+        half = dot(r.order[layer], r.page[n % TABLE_SLOTS], NT).astype(BF)
+        if n + TABLE_SLOTS < 2 * HEADS:
+            table_copy(r, n + TABLE_SLOTS).start()
+        r.bias[layer, n % HEADS] = dot(half, r.order[layer], NT)
 
 
 def set_queries(sc, queries):
@@ -190,14 +204,14 @@
             if j == c:
                 allowed = allowed | eye
             part = jnp.where(allowed, x_all[:, lanes] + sc.bias[h, rows, lanes], MASK_FILL)
-            sc.s[h % 3, rows, lanes] = part
+            sc.s[h % 2, rows, lanes] = part
             parts.append(jnp.max(part.reshape(16, 8, 128), axis=0))
         top = jnp.concatenate(parts, axis=1)
         tops[h] = top if tops[h] is None else jnp.maximum(tops[h], top)
 
     def raise_(h, c):
         rows = slice(128 * c, 128 * c + 128)
-        sc.e[rows, T * h : T * h + T] = jnp.exp(sc.s[h % 3, rows] - tops[h]).astype(BF)
+        sc.e[rows, T * h : T * h + T] = jnp.exp(sc.s[h % 2, rows] - tops[h]).astype(BF)
 
     def attend(h):
         out = dot(sc.vt[h], sc.e[:, T * h : T * h + T])
@@ -233,10 +247,6 @@
         part = (d_att[16 * h : 16 * h + 16] * sc.inv[h : h + 1, :]).astype(BF)
         cols = slice(T * h, T * h + T)
         sc.dab[16 * h : 16 * h + 16, cols] = part
-        sc.rb[C + 16 * h : C + 16 * h + 16, 2 * T * h : 2 * T * h + T] = part
-        sc.rb[16 * h : 16 * h + 16, 2 * T * h + T : 2 * T * h + 2 * T] = sc.qT[
-            16 * h : 16 * h + 16, :
-        ]
         inner = -jnp.sum(
             part.astype(F32) * sc.att[16 * h : 16 * h + 16, :], axis=0, keepdims=True
         )
@@ -247,27 +257,36 @@
         ).astype(BF)
     yield 100
     total = None
+    none = jnp.zeros((16, T), BF)
 
     def soft(h):
         cols = slice(T * h, T * h + T)
         pull = dot(sc.vn[...], sc.dab[:, cols])
-        sc.ds[:, cols] = (pull * sc.e[:, cols].astype(F32)).astype(BF)
+        sc.ds[h % 2] = (pull * sc.e[:, cols].astype(F32)).astype(BF)
+
+    def place_rows(h):
+        rb = sc.rb.at[h % 2]
+        last = (h - 2) % HEADS
+        rb[16 * last : 16 * last + 16, T:] = none
+        rb[C + 16 * last : C + 16 * last + 16, 0:T] = none
+        rb[16 * h : 16 * h + 16, T:] = sc.qT[16 * h : 16 * h + 16, :]
+        rb[C + 16 * h : C + 16 * h + 16, 0:T] = sc.dab[
+            16 * h : 16 * h + 16, T * h : T * h + T
+        ]
 
     def to_queries(h):
-        sc.dq[16 * h : 16 * h + 16, :] = dot(
-            sc.kT[16 * h : 16 * h + 16, :], sc.ds[:, T * h : T * h + T]
-        ).astype(BF)
+        sc.dq[16 * h : 16 * h + 16, :] = dot(sc.kT[16 * h : 16 * h + 16, :], sc.ds[h % 2]).astype(BF)
 
     for h in range(HEADS + 1):
         if h < HEADS:
+            place_rows(h)
             soft(h)
             yield 120
         if h > 0:
-            cols = slice(T * (h - 1), T * h)
             to_queries(h - 1)
             yield 60
-            both = jnp.concatenate([sc.e[:, cols], sc.ds[:, cols]], axis=1)
-            term = dot(both, sc.rb[:, 2 * T * (h - 1) : 2 * T * h], NT)
+            both = jnp.concatenate([sc.e[:, T * (h - 1) : T * h], sc.ds[(h - 1) % 2]], axis=1)
+            term = dot(both, sc.rb[(h - 1) % 2], NT)
             total = term if total is None else total + term
             yield 180
     dkv = total.astype(BF)
@@ -330,7 +349,7 @@
     vt=((HEADS, 32, T), BF),
     kn=((T, CA), BF),
     codes=((T, 128), F32),
-    s=((3, T, T), F32),
+    s=((2, T, T), F32),
 )
 BIAS = dict(bias=((HEADS, T, T), F32))
 KEPT = dict(
@@ -358,20 +377,37 @@
 )
 BWD = dict(
     dab=((CA, HEADS * T), BF),
-    rb=((2 * C, 2 * HEADS * T), BF),
-    ds=((T, HEADS * T), BF),
+    rb=((2, 2 * C, 2 * T), BF),
+    ds=((2, T, T), BF),
     dq=((C, T), BF),
     dh=((FF, T), BF),
 )
 
 
 PADS = dict(pad=((C, T), BF), cot=((C, T), BF))
-LAGS = (0, 0, 0)
-
-
-def by_window(r, own):
+WEIGHTS = dict(
+    qkvT=((3 * C, CA), BF),
+    kv=((CA, 2 * CA), BF),
+    projT=((C, CA), BF),
+    proj=((C, C), BF),
+    upT=((FF, CA), BF),
+    up=((C, FF), BF),
+    downT=((C, FF), BF),
+    down=((FF, C), BF),
+    q=((C, C), BF),
+    kv96=((C, 2 * C), BF),
+    vec=((5, C, 128), F32),
+)
+
+
+def of_layer(r, layer, slot):
+    shared = {n: getattr(r, n).at[layer] for n in (*WEIGHTS, *GRADS, *BIAS)}
     return [
-        SimpleNamespace(**{**vars(r), **{n: getattr(r, n).at[i] for n in own if hasattr(r, n)}})
+        SimpleNamespace(
+            **shared,
+            **{n: getattr(r, n).at[i] for n in (*FWD, *BWD, *PADS)},
+            **{n: getattr(r, KEPT_NAMES[layer][i] + n).at[slot] for n in KEPT},
+        )
         for i in range(WINDOWS)
     ]
 
@@ -406,53 +442,42 @@
     pl.semaphore_wait(pltpu.get_barrier_semaphore(), len(peers))
 
 
-def block_copy(r, m, octant, sign, groups_a):
+def block_copy(way, m, octant, groups_a):
     rows = pl.ds(OCT_OFF[octant], OCT_LEN[octant])
     slot = m % 2
-    source = r.stage.at[slot, :, rows]
-    target = r.got.at[pl.ds(m * WINDOWS, WINDOWS), rows]
+    source = way.stage.at[slot, :, rows]
+    target = way.got.at[pl.ds(m * WINDOWS, WINDOWS), rows]
     if octant == 0:
-        return pltpu.make_async_copy(source, target, r.sent.at[slot, 0])
+        return pltpu.make_async_copy(source, target, way.arrived.at[m, 0])
     return pltpu.make_async_remote_copy(
         src_ref=source,
         dst_ref=target,
-        send_sem=r.sent.at[slot, octant],
-        recv_sem=r.arrived.at[m, octant],
-        device_id=neighbour(octant, sign, groups_a),
+        send_sem=way.sent.at[slot, octant],
+        recv_sem=way.arrived.at[m, octant],
+        device_id=neighbour(octant, way.sign, groups_a),
         device_id_type=MESH,
     )
 
 
-def wait_sent(r, m, sign, groups_a):
+def send_blocks(way, m, groups_a):
     for octant in range(8):
-        copy = block_copy(r, m, octant, sign, groups_a)
-        copy.wait_send() if octant else copy.wait()
-
-
-def send_blocks(r, m, sign, groups_a):
-    @pl.when(m == 0)
-    def _():
-        pl.semaphore_wait(pltpu.get_barrier_semaphore(), 7)
-
-    for octant in range(8):
-        block_copy(r, m, octant, sign, groups_a).start()
-
-
-def finish_blocks(r, steps, sign, groups_a):
-    for m in range(max(steps - 2, 0), steps):
-        wait_sent(r, m, sign, groups_a)
-
-    def arrival(m, carry):
-        for octant in range(1, 8):
-            block_copy(r, m, octant, sign, groups_a).wait_recv()
-        return carry
-
-    lax.fori_loop(0, steps, arrival, 0)
+        block_copy(way, m, octant, groups_a).start()
+
+
+def wait_sent(way, m, groups_a):
+    for octant in range(1, 8):
+        block_copy(way, m, octant, groups_a).wait_send()
+
+
+def wait_arrived(way, m, groups_a):
+    block_copy(way, m, 0, groups_a).wait()
+    for octant in range(1, 8):
+        block_copy(way, m, octant, groups_a).wait_recv()
 
 
 def first_forward(r, sc, m, i):
-    w, st = r, SimpleNamespace()
-    slot = m % 2
+    w, st = sc, SimpleNamespace()
+    stage = r.x_stage.at[m % 2, i]
     sc.pad[:, 0:WS] = r.tokens[i, 0]
     st.x = sc.pad[...].astype(F32)
     sc.xT[...] = st.x
@@ -467,7 +492,7 @@
     yield 100
     yield from forward_attention(sc, w, st, jnp.zeros((1, T), F32))
     sc.cot[:, 0:WS] = r.cotangent[i, 0]
-    r.stage[slot, i, :, CA:] = jnp.concatenate(
+    stage[:, CA:] = jnp.concatenate(
         [dot(r.perm[...], sc.cot[...], NT), jnp.zeros((T, CA - C), F32)], axis=1
     ).astype(BF)
     yield 100
@@ -487,38 +512,16 @@
     label = r.info[m * WINDOWS + i, 0].astype(F32)
     extra = jnp.where(row == 0, label, jnp.where(row == 1, valid, 0.0))
     x = jnp.concatenate([x, extra], axis=0).astype(BF)
-    r.stage[slot, i, :, 0:CA] = dot(r.perm[...], x, NT).astype(BF)
+    stage[:, 0:CA] = dot(r.perm[...], x, NT).astype(BF)
     yield 100
 
 
-def first_forward_kernel(groups_a, steps, lag, r):
-    windows = by_window(r, dict(**FWD, **KEPT, **PADS))
-    m = pl.program_id(0)
-
-    @pl.when(m == 0)
-    def _():
-        greet([neighbour(octant, 1, groups_a) for octant in range(1, 8)])
-        init_forward(r, windows)
-        for sc in windows:
-            sc.pad[...] = jnp.zeros((C, T), BF)
-            sc.cot[...] = jnp.zeros((C, T), BF)
-
-    @pl.when(m >= 2)
-    def _():
-        wait_sent(r, m - 2, -1, groups_a)
-
-    weave([first_forward(r, sc, m, i) for i, sc in enumerate(windows)], lag)
-    send_blocks(r, m, -1, groups_a)
-
-    @pl.when(m == steps - 1)
-    def _():
-        finish_blocks(r, steps, -1, groups_a)
-
-
 def second_layer(r, sc, m, i, groups_a):
-    w, st = r, SimpleNamespace()
-    came = r.came[i, :, 0:CA]
-    x = dot(r.eye[...], came, NT)
+    w, st = sc, SimpleNamespace()
+    stage = r.d_stage.at[m % 2, i]
+    n = m * WINDOWS + i
+    came = r.x_got[n, :, 0:CA]
+    x = dot(r.eye[0:CA, 0:CA], came, NT)
     place, sizes = grid_place(groups_a)
     code_row = []
     for octant in range(8):
@@ -539,7 +542,7 @@
     st.x = x
     yield 150
     yield from forward_attention(sc, w, st, code_row)
-    st.d = dot(r.eye[0:C], r.came[i, :, CA:], NT) * keep
+    st.d = dot(r.eye[0:C, 0:CA], r.x_got[n, :, CA:], NT) * keep
     dd = st.d.astype(BF)
     x = sc.xT[...] + st.branch.astype(BF).astype(F32)
     z, scale = second_norm(sc, w, x)
@@ -551,45 +554,19 @@
         sc.dh[rows, :] = (dot(w.down[rows], dd) * slope).astype(BF)
         yield 120
     x = x + (dot(w.downT[...], sc.act[...]) + wide(w.vec[4]))
-    slot = m % 2
     none = jnp.zeros((CA - C, T), F32)
-    r.stage[slot, i, :, 0:CA] = jnp.concatenate([x * keep, none], axis=0).T.astype(BF)
+    stage[:, 0:CA] = jnp.concatenate([x * keep, none], axis=0).T.astype(BF)
     yield 150
     yield from feed_forward_back(sc, w, st, dd, z, scale)
     z, scale = ln_stats(sc.xT[...])
     yield from backward_attention(sc, w, st, z, scale, True)
-    r.stage[slot, i, :, CA:] = jnp.concatenate([st.d, none], axis=0).T.astype(BF)
+    stage[:, CA:] = jnp.concatenate([st.d, none], axis=0).T.astype(BF)
     yield 100
 
 
-def second_kernel(groups_a, steps, lag, r):
-    windows = by_window(r, dict(**FWD, **KEPT, **BWD))
-    m = pl.program_id(0)
-
-    @pl.when(m == 0)
-    def _():
-        greet([neighbour(octant, -1, groups_a) for octant in range(1, 8)])
-        init_forward(r, windows)
-        init_backward(r, windows)
-
-    @pl.when(m >= 2)
-    def _():
-        wait_sent(r, m - 2, 1, groups_a)
-
-    weave(
-        [second_layer(r, sc, m, i, groups_a) for i, sc in enumerate(windows)], lag
-    )
-    send_blocks(r, m, 1, groups_a)
-
-    @pl.when(m == steps - 1)
-    def _():
-        finish_blocks(r, steps, 1, groups_a)
-        write_grads(r, r.grads)
-
-
-def first_backward(r, sc, i):
-    w, st = r, SimpleNamespace()
-    came = dot(r.eye[...], r.came[i], NT).astype(BF)
+def first_backward(r, sc, m, i):
+    w, st = sc, SimpleNamespace()
+    came = dot(r.eye[...], r.d_got[m * WINDOWS + i], NT).astype(BF)
     yield 200
     came = dot(came, r.perm[...])
     r.output[i, 0] = came[0:C, 0:WS].astype(BF)
@@ -608,19 +585,75 @@
     yield 50
 
 
-def first_backward_kernel(steps, lag, r):
-    windows = by_window(r, dict(**KEPT, **BWD))
-    m = pl.program_id(0)
-
-    @pl.when(m == 0)
+def layers_kernel(n_vol, n_plane, shard_len, steps, r):
+    groups_a = n_plane // 2
+    s = pl.program_id(0)
+    forth = SimpleNamespace(
+        stage=r.x_stage, got=r.x_got, sent=r.x_sent, arrived=r.x_arrived, sign=-1
+    )
+    back = SimpleNamespace(
+        stage=r.d_stage, got=r.d_got, sent=r.d_sent, arrived=r.d_arrived, sign=1
+    )
+
+    @pl.when(s == 0)
     def _():
-        init_backward(r, windows)
-
-    weave([first_backward(r, sc, i) for i, sc in enumerate(windows)], lag)
-
-    @pl.when(m == steps - 1)
+        far = all_peers(n_vol, n_plane)
+        peers = far + [
+            neighbour(octant, sign, groups_a) for sign in (1, -1) for octant in range(1, 8)
+        ]
+        greet(peers)
+        for n in range(TABLE_SLOTS):
+            table_copy(r, n).start()
+        vol, plane, core = own_place()
+        r.buf[core, plane, vol] = r.shard[...]
+        clear_scratch(r)
+        await_greetings(peers)
+        meanwhile = (lambda: None, lambda: turn_tables(r, 0), lambda: turn_tables(r, 1))
+        for copies, work in zip(gather_stages(r, far, n_vol, n_plane), meanwhile):
+            for c in copies:
+                c.start()
+            work()
+            for c in copies:
+                c.wait()
+        prepare(r, n_vol, n_plane, shard_len)
+
+    @pl.when(s < steps)
     def _():
-        write_grads(r, r.grads)
+        @pl.when(s >= 2)
+        def _():
+            wait_sent(forth, s - 2, groups_a)
+
+        windows = of_layer(r, 0, s % 3)
+        weave([first_forward(r, sc, s, i) for i, sc in enumerate(windows)], 0)
+        send_blocks(forth, s, groups_a)
+
+    @pl.when((s >= 1) & (s <= steps))
+    def _():
+        m = s - 1
+        wait_arrived(forth, m, groups_a)
+
+        @pl.when(m >= 2)
+        def _():
+            wait_sent(back, m - 2, groups_a)
+
+        windows = of_layer(r, 1, 0)
+        weave([second_layer(r, sc, m, i, groups_a) for i, sc in enumerate(windows)], 0)
+        send_blocks(back, m, groups_a)
+
+    @pl.when(s >= 2)
+    def _():
+        m = s - 2
+        wait_arrived(back, m, groups_a)
+        windows = of_layer(r, 0, m % 3)
+        weave([first_backward(r, sc, m, i) for i, sc in enumerate(windows)], 0)
+
+    @pl.when(s == steps + 1)
+    def _():
+        for m in range(max(steps - 2, 0), steps):
+            wait_sent(forth, m, groups_a)
+            wait_sent(back, m, groups_a)
+        for layer in range(2):
+            write_grads(of_layer(r, layer, 0)[0], r.grads.at[layer])
 
 
 def shard_rows(device, shard_len):
@@ -654,52 +687,46 @@
     return jnp.concatenate([matrix, below], axis=0).T
 
 
-def gather_kernel(n_vol, n_plane, shard_len, r):
+def gather_stages(r, peers, n_vol, n_plane):
     vol, plane, core = own_place()
-    peers = all_peers(n_vol, n_plane)
-    greet(peers)
-    await_greetings(peers)
-    buf = r.buf
 
     def copy(ref, n):
         return pltpu.make_async_remote_copy(
             src_ref=ref,
             dst_ref=ref,
-            send_sem=r.sent.at[n],
-            recv_sem=r.arrived.at[n],
+            send_sem=r.g_sent.at[n],
+            recv_sem=r.g_arrived.at[n],
             device_id=peers[n],
             device_id_type=MESH,
         )
 
-    buf[core, plane, vol] = r.shard[...]
-    stages = [
-        [copy(buf.at[core, plane, vol], n) for n in range(n_vol - 1)],
-        [copy(buf.at[core, plane], n_vol - 1 + n) for n in range(n_plane - 1)],
-        [copy(buf.at[core], n_vol + n_plane - 2)],
-    ]
-    for copies in stages:
-        for c in copies:
-            c.start()
-        for c in copies:
-            c.wait()
-    flat = r.flat
+    return (
+        [copy(r.buf.at[core, plane, vol], n) for n in range(n_vol - 1)],
+        [copy(r.buf.at[core, plane], n_vol - 1 + n) for n in range(n_plane - 1)],
+        [copy(r.buf.at[core], n_vol + n_plane - 2)],
+    )
+
+
+def prepare(r, n_vol, n_plane, shard_len):
+    buf = r.buf
+    flat = r.grads
     flat[...] = jnp.zeros(flat.shape, F32)
+    half = n_vol * n_plane
     for v in range(n_vol):
         for p in range(n_plane):
             for c in range(2):
-                start, stop = shard_rows((v * n_plane + p) * 2 + c, shard_len)
-                flat[start:stop, :] += buf[c, p, v, 0 : stop - start].astype(F32)
+                device = (v * n_plane + p) * 2 + c
+                start, stop = shard_rows(device % half, shard_len)
+                flat[device // half, start:stop, :] += buf[c, p, v, 0 : stop - start].astype(F32)
     for layer in range(2):
-        at = layer * BLOCK_ROWS
 
         def rows(start, count=C, stride=1):
-            return flat[pl.ds(at + start, count, stride), :]
+            return flat[layer, pl.ds(start, count, stride), :]
 
         def vector(n):
             return rows(12 * C + n, 1)
 
-        o = {n: getattr(r, n).at[layer] for n in WEIGHTS}
-        o = SimpleNamespace(**o)
+        o = SimpleNamespace(**{n: getattr(r, n).at[layer] for n in WEIGHTS})
         none = jnp.zeros((1, C), F32)
         wq, wk, wv = (rows(n, C, 3) for n in range(3))
         o.q[...] = wq.astype(BF)
@@ -735,14 +762,13 @@
     greet(peers)
     await_greetings(peers)
     work = r.work
-    half = 2 * n_vol * n_plane // 2
+    half = n_vol * n_plane
     for v in range(n_vol):
         for p in range(n_plane):
             for c in range(2):
                 device = (v * n_plane + p) * 2 + c
-                start, stop = shard_rows(device, shard_len)
-                source = (r.first, r.second)[device // half]
-                start, stop = (n - device // half * BLOCK_ROWS for n in (start, stop))
+                start, stop = shard_rows(device % half, shard_len)
+                source = r.grads.at[device // half]
                 work[c, p, v, 0 : stop - start] = source[start:stop, :]
 
     def copy(source, target, n):
@@ -785,18 +811,20 @@
     r.total[...] = total
 
 
-def call(kernel, steps, ins, outs, scratch, semaphores=(), collective_id=None):
-    def spec(shape, kind):
-        if kind is SMEM:
-            return pl.BlockSpec(memory_space=pltpu.SMEM)
-        if kind is HBM:
-            return pl.BlockSpec(memory_space=pl.ANY)
+def call(kernel, steps, ins, outs, scratch, semaphores=(), collective_id=None, lag=0):
+    def spec(shape, kind, late):
+        if kind in (SMEM, HBM):
+            return pl.BlockSpec(memory_space=pltpu.SMEM if kind is SMEM else pl.ANY)
         zeros = (0,) * (len(shape) - 1)
         if kind is BY_STEP:
-            return pl.BlockSpec((shape[0] // steps,) + tuple(shape[1:]), lambda m: (m,) + zeros)
-        if kind in (0, 1):
-            return pl.BlockSpec((pl.squeezed,) + tuple(shape[1:]), lambda m: (kind,) + zeros)
-        return pl.BlockSpec(tuple(shape), lambda m: (0,) + zeros)
+
+            def index(s):
+                return (jnp.clip(s - late, 0, steps - 1),) + zeros
+
+            return pl.BlockSpec((shape[0] // steps,) + tuple(shape[1:]), index)
+        return pl.BlockSpec(
+            tuple(shape), lambda s: (0,) + zeros, pipeline_mode=None if late else pl.Buffered(1)
+        )
 
     semaphores = dict(semaphores)
     names = tuple(ins) + tuple(outs) + tuple(scratch) + tuple(semaphores)
@@ -806,9 +834,9 @@
 
     results = pl.pallas_call(
         body,
-        grid=(steps,),
-        in_specs=[spec(a.shape, kind) for a, kind in ins.values()],
-        out_specs=[spec(shape, kind) for shape, _, kind in outs.values()],
+        grid=(steps + lag,),
+        in_specs=[spec(a.shape, kind, 0) for a, kind in ins.values()],
+        out_specs=[spec(shape, kind, lag) for shape, _, kind in outs.values()],
         out_shape=[jax.ShapeDtypeStruct(shape, dtype) for shape, dtype, _ in outs.values()],
         scratch_shapes=[pltpu.VMEM(shape, dtype) for shape, dtype in scratch.values()]
         + [pltpu.SemaphoreType.DMA(shape) for shape in semaphores.values()],
@@ -819,21 +847,6 @@
         ),
     )(*[a for a, _ in ins.values()])
     return SimpleNamespace(**dict(zip(outs, results)))
-
-
-WEIGHTS = dict(
-    qkvT=((3 * C, CA), BF),
-    kv=((CA, 2 * CA), BF),
-    projT=((C, CA), BF),
-    proj=((C, C), BF),
-    upT=((FF, CA), BF),
-    up=((C, FF), BF),
-    downT=((C, FF), BF),
-    down=((FF, C), BF),
-    q=((C, C), BF),
-    kv96=((C, 2 * C), BF),
-    vec=((5, C, 128), F32),
-)
 
 
 def on_device(
@@ -847,7 +860,7 @@
     second_moment,
 ):
     n_vol, n_win = lax.axis_size(VOL), lax.axis_size(WIN)
-    groups_a, n_plane = n_win // 4, n_win // 2
+    n_plane = n_win // 2
     count = tokens.shape[0]
     steps = count // WINDOWS
     shard_len = master.shape[0]
@@ -856,91 +869,67 @@
     offset = flat_offset(device, shard_len)
     shard = lax.dynamic_update_slice(jnp.zeros((slab * C,), BF), master.astype(BF), (offset,))
     n_peers = n_vol + n_plane - 1
-    weights = call(
-        lambda r: gather_kernel(n_vol, n_plane, shard_len, r),
-        1,
-        dict(shard=(shard.reshape(slab, C), WHOLE)),
-        {n: ((2,) + shape, dtype, WHOLE) for n, (shape, dtype) in WEIGHTS.items()},
-        dict(
-            buf=((2, n_plane, n_vol, slab, C), BF),
-            flat=((2 * BLOCK_ROWS + 8, C), F32),
-        ),
-        dict(sent=(n_peers,), arrived=(n_peers,)),
-        collective_id=0,
-    )
     info = jnp.concatenate((window_volume[:, :, None], clip_extent), axis=2)[:, 0]
 
-    def each(table):
-        return {n: ((WINDOWS,) + shape, dtype) for n, (shape, dtype) in table.items()}
-
-    def layer(which):
-        return {n: (a, which) for n, a in vars(weights).items()}
-
-    def table(which, order):
-        return dict(order=(jnp.asarray(order, BF), WHOLE), table=(position_bias, which))
-
-    perm = (jnp.asarray(PERM, BF), WHOLE)
-    eye = (jnp.asarray(np.eye(CA), BF), WHOLE)
-    stage = dict(stage=((2, WINDOWS, T, 2 * CA), BF))
-    copies = dict(sent=(2, 8), arrived=(steps, 8))
-    got = call(
-        lambda r: first_forward_kernel(groups_a, steps, LAGS[0], r),
+    def each(table, *sizes):
+        return {n: (sizes + shape, dtype) for n, (shape, dtype) in table.items()}
+
+    def kept(layer, slots):
+        shapes = dict(KEPT, gp=((16, T), BF)) if layer else KEPT
+        return {name + n: v for name in KEPT_NAMES[layer] for n, v in each(shapes, slots).items()}
+
+    stage, landing = ((2, WINDOWS, T, 2 * CA), BF), ((count, T, 2 * CA), BF)
+    layers = call(
+        lambda r: layers_kernel(n_vol, n_plane, shard_len, steps, r),
         steps,
         dict(
             tokens=(tokens.transpose(0, 1, 3, 2), BY_STEP),
             cotangent=(cotangent.transpose(0, 1, 3, 2), BY_STEP),
             info=(info, SMEM),
-            perm=perm,
+            perm=(jnp.asarray(PERM, BF), WHOLE),
             places=(jnp.asarray(PLACES), WHOLE),
-            **table(0, np.eye(T, WS)),
-            **layer(0),
-        ),
-        dict(
-            got=((count, T, 2 * CA), BF, HBM),
-            **{n: ((count,) + shape, dtype, BY_STEP) for n, (shape, dtype) in KEPT.items()},
-        ),
-        dict(**BIAS, **stage, **each(FWD), **each(PADS)),
-        copies,
-        collective_id=1,
-    )
-    second = call(
-        lambda r: second_kernel(groups_a, steps, LAGS[1], r),
-        steps,
-        dict(
-            came=(got.got, BY_STEP),
-            eye=eye,
-            **table(1, ORDER),
-            **layer(1),
-        ),
-        dict(
-            got=((count, T, 2 * CA), BF, HBM),
-            grads=((BLOCK_ROWS, C), F32, WHOLE),
-        ),
-        dict(**BIAS, **stage, **GRADS, **each(FWD), **each(KEPT), **each(BWD)),
-        copies,
-        collective_id=2,
-    )
-    first = call(
-        lambda r: first_backward_kernel(steps, LAGS[2], r),
-        steps,
-        dict(
-            came=(second.got, BY_STEP),
-            perm=perm,
+            order=(jnp.asarray(np.stack([np.eye(T, WS), ORDER]), BF), WHOLE),
+            table=(position_bias, HBM),
+            shard=(shard.reshape(slab, C), WHOLE),
             eye=(jnp.asarray(np.eye(2 * CA), BF), WHOLE),
-            **{n: (getattr(got, n), BY_STEP) for n in KEPT},
-            **layer(0),
         ),
         dict(
             output=((count, 1, C, WS), BF, BY_STEP),
             input_grad=((count, 1, C, WS), F32, BY_STEP),
-            grads=((BLOCK_ROWS, C), F32, WHOLE),
+            grads=((2, BLOCK_ROWS, C), F32, WHOLE),
         ),
-        dict(**GRADS, **each(BWD)),
+        dict(
+            **each(FWD, WINDOWS),
+            **each(BWD, WINDOWS),
+            **each(PADS, WINDOWS),
+            **each(GRADS, 2),
+            **each(BIAS, 2),
+            **kept(0, 3),
+            **kept(1, 1),
+            **each(WEIGHTS, 2),
+            page=((TABLE_SLOTS, WS, WS), BF),
+            buf=((2, n_plane, n_vol, slab, C), BF),
+            x_stage=stage,
+            d_stage=stage,
+            x_got=landing,
+            d_got=landing,
+        ),
+        dict(
+            x_sent=(2, 8),
+            x_arrived=(steps, 8),
+            d_sent=(2, 8),
+            d_arrived=(steps, 8),
+            g_sent=(n_peers,),
+            g_arrived=(n_peers,),
+            turned=(TABLE_SLOTS,),
+        ),
+        collective_id=1,
+        lag=2,
     )
     reduced = call(
         lambda r: reduce_kernel(n_vol, n_plane, shard_len, r),
         1,
-        dict(first=(first.grads, WHOLE), second=(second.grads, WHOLE)),
+        dict(grads=(layers.grads, WHOLE)),
         dict(total=((slab, C), F32, WHOLE)),
         dict(
             work=((2, n_plane, n_vol, slab, C), F32),
@@ -949,7 +938,7 @@
             from_vol=((n_vol - 1, slab, C), F32),
         ),
         dict(sent=(n_peers,), arrived=(n_peers,)),
-        collective_id=3,
+        collective_id=2,
     )
     shard_grad = lax.dynamic_slice(reduced.total.reshape(-1), (offset,), (shard_len,))
     position = (device * shard_len + jnp.arange(shard_len, dtype=jnp.int32)) % (BLOCK_ROWS * C)
@@ -963,8 +952,8 @@
     normalized = corrected_one / (jnp.sqrt(corrected_two) + ADAM_EPS)
     new_master = master - step_rate * (normalized + weight_decay * master)
     return (
-        first.output.transpose(0, 1, 3, 2),
-        first.input_grad.transpose(0, 1, 3, 2),
+        layers.output.transpose(0, 1, 3, 2),
+        layers.input_grad.transpose(0, 1, 3, 2),
         new_master,
         moment_one,
         moment_two,

time: 249 us -> 230 us (0.924)
  Pallas kernels: 239 us -> 217 us
  local copies, waits for them, and re-layouts: 6.5 us -> 10 us
    pallas_call x5 -> x2, Pallas kernels: 239 us -> 217 us  [call(): pl.pallas_call(body, grid=(steps + lag,), in_specs=[spec(a.shape, kind, 0...]
    unnamed x7 -> x13, local copies, waits for them, and re-layouts: 3.96 us -> 7.46 us
where the time goes in v4:
time: 230 us
  Pallas kernels  217 us (94%)
  local copies, waits for them, and re-layouts  10 us (4%)
    pallas_call x2, Pallas kernels, call(): pl.pallas_call(body, grid=(steps + lag,), in_specs=[spec(a.shape, kind, 0...  217 us
    unnamed x13, local copies, waits for them, and re-layouts  7.46 us

profile of v4, /device:TPU:0, one launch (start us, length us, event | category | flops | bytes accessed | tf_op | source)
XLA Modules:
  0.0 229.9 jit_solution(15042941031433889284)
XLA Ops:
  0.7 0.7 pad_add_fusion
  1.3 0.7 copy.19.refs_2_
  2.0 0.8 convert_element_type.6
  2.8 0.3 dynamic_update_slice.3
  3.1 0.7 reshape.18.refs_7_
  3.8 3.9 %copy.20.refs_6_ = bf16[2,6,343,343]{3,2,1,0:T(8,128)(2,1)} copy(bf16[2,6,343,343]{3,0,2,1:T(2,128)(2,1)} %param.14) | data formatting | bytes 5647152 | tf_op args[2]
  7.7 197.0 %shard_map.163 = (bf16[16,1,96,343]{3,2,1,0:T(8,128)(2,1)}, f32[16,1,96,343]{3,2,1,0:T(8,128)}, f32[2,1164,96]{2,1,0:T(8,128)}) custom-call(bf16[16,1,96,343]{3,2,1,0:T(8,128)(2,1)} %bitcast.9, bf16[16,1,96,343]{3,2,1,0:T(8,128)(2,1)} %bitcast.10, s32[16,4]{1,0:T(8,128)} %copy.19.refs_2_, bf16[384,384]{1,0:T(8,128)(2,1)} %constant.64.clone.refs_3_, ...), custom_call_target="tpu_custom_call" | custom-call | tf_op jit(solution)/shard_map/pallas_call | solution.py:835
  204.7 0.0 copy-start.2
  204.7 0.0 copy-start.3
  204.8 0.0 copy-start.4
  204.8 0.0 copy-start.1
  204.8 20.0 %shard_map.164 = f32[80,96]{1,0:T(8,128)} custom-call(f32[2,1164,96]{2,1,0:T(8,128)} %get-tuple-element.11.refs_0_), custom_call_target="tpu_custom_call" | custom-call | tf_op jit(solution)/shard_map/pallas_call | solution.py:835
  224.8 0.9 reshape.19
  225.7 0.0 copy-done.2
  225.7 0.0 copy-done.3
  225.7 0.0 copy-done.4
  225.7 0.7 fusion.5
  226.4 0.0 copy-start
  226.4 0.0 copy-done.1
  226.4 1.0 copy.24
  227.4 1.1 copy-done
  228.5 1.4 copy.25
  (1 shorter events, 0.0 us)
Async XLA Ops:
  204.7 20.9 %copy-start.2 = (f32[6984]{0:T(1024)S(1)}, f32[6984]{0:T(1024)}, u32[]{:S(2)}) copy-start(f32[6984]{0:T(1024)} %param.17) | copy-start | bytes 83812
  204.7 20.9 %copy-start.3 = (f32[6984]{0:T(1024)S(1)}, f32[6984]{0:T(1024)}, u32[]{:S(2)}) copy-start(f32[6984]{0:T(1024)} %param.18) | copy-start | bytes 83812
  204.8 20.9 %copy-start.4 = (f32[6984]{0:T(1024)S(1)}, f32[6984]{0:T(1024)}, u32[]{:S(2)}) copy-start(f32[6984]{0:T(1024)} %param.19) | copy-start | bytes 83812
  204.8 21.6 %copy-start.1 = (bf16[16,1,96,343]{3,2,1,0:T(8,128)(2,1)S(1)}, bf16[16,1,96,343]{3,2,1,0:T(8,128)(2,1)}, u32[]{:S(2)}) copy-start(bf16[16,1,96,343]{3,2,1,0:T(8,128)(2,1)} %get-tuple-element.9) | copy-start | bytes 3161092
  226.4 2.1 copy-start

commit v5 on v4

--- a/solution.py
+++ b/solution.py
@@ -18,7 +18,8 @@
 STEP = 6
 T = 384
 WINDOWS = 2
-TABLE_SLOTS = 4
+TABLE_SLOTS = 3
+ROWS = (352, T)
 CA = 128
 BLOCK_ROWS = 1164
 
@@ -194,7 +195,8 @@
     tops = [None] * HEADS
 
     def scores(h, c):
-        rows = slice(128 * c, 128 * c + 128)
+        rows = slice(128 * c, min(128 * c + 128, sc.rows))
+        count = rows.stop - rows.start
         x_all = dot(sc.kn[rows], sc.qb[:, T * h : T * h + T])
         codes = sc.codes[rows]
         parts = []
@@ -202,19 +204,19 @@
             lanes = slice(128 * j, 128 * j + 128)
             allowed = codes == code_row[:, lanes]
             if j == c:
-                allowed = allowed | eye
+                allowed = allowed | eye[0:count]
             part = jnp.where(allowed, x_all[:, lanes] + sc.bias[h, rows, lanes], MASK_FILL)
             sc.s[h % 2, rows, lanes] = part
-            parts.append(jnp.max(part.reshape(16, 8, 128), axis=0))
+            parts.append(jnp.max(part.reshape(count // 8, 8, 128), axis=0))
         top = jnp.concatenate(parts, axis=1)
         tops[h] = top if tops[h] is None else jnp.maximum(tops[h], top)
 
     def raise_(h, c):
-        rows = slice(128 * c, 128 * c + 128)
+        rows = slice(128 * c, min(128 * c + 128, sc.rows))
         sc.e[rows, T * h : T * h + T] = jnp.exp(sc.s[h % 2, rows] - tops[h]).astype(BF)
 
     def attend(h):
-        out = dot(sc.vt[h], sc.e[:, T * h : T * h + T])
+        out = dot(sc.vt[h, :, 0 : sc.rows], sc.e[:, T * h : T * h + T])
         inverse = 1.0 / out[16:17]
         part = out[0:16] * inverse
         sc.att[16 * h : 16 * h + 16, :] = part
@@ -261,8 +263,8 @@
 
     def soft(h):
         cols = slice(T * h, T * h + T)
-        pull = dot(sc.vn[...], sc.dab[:, cols])
-        sc.ds[h % 2] = (pull * sc.e[:, cols].astype(F32)).astype(BF)
+        pull = dot(sc.vn[0 : sc.rows], sc.dab[:, cols])
+        sc.ds[h % 2, 0 : sc.rows] = (pull * sc.e[:, cols].astype(F32)).astype(BF)
 
     def place_rows(h):
         rb = sc.rb.at[h % 2]
@@ -275,7 +277,9 @@
         ]
 
     def to_queries(h):
-        sc.dq[16 * h : 16 * h + 16, :] = dot(sc.kT[16 * h : 16 * h + 16, :], sc.ds[h % 2]).astype(BF)
+        sc.dq[16 * h : 16 * h + 16, :] = dot(
+            sc.kT[16 * h : 16 * h + 16, 0 : sc.rows], sc.ds[h % 2, 0 : sc.rows]
+        ).astype(BF)
 
     for h in range(HEADS + 1):
         if h < HEADS:
@@ -285,11 +289,15 @@
         if h > 0:
             to_queries(h - 1)
             yield 60
-            both = jnp.concatenate([sc.e[:, T * (h - 1) : T * h], sc.ds[(h - 1) % 2]], axis=1)
+            both = jnp.concatenate(
+                [sc.e[:, T * (h - 1) : T * h], sc.ds[(h - 1) % 2, 0 : sc.rows]], axis=1
+            )
             term = dot(both, sc.rb[(h - 1) % 2], NT)
             total = term if total is None else total + term
             yield 180
     dkv = total.astype(BF)
+    if sc.rows < T:
+        dkv = jnp.concatenate([dkv, jnp.zeros((T - sc.rows, 2 * C), BF)], axis=0)
     dq = sc.dq[...]
     dn = dot(w.q[...], dq) + dot(w.kv96[...], dkv, NT)
     yield 120
@@ -364,7 +372,7 @@
     n2aug=((CA, T), BF),
     act=((FF, T), BF),
     gp=((FF, T), BF),
-    xT=((C, T), F32),
+    xT=((C, T), BF),
     x1=((C, T), F32),
 )
 GRADS = dict(
@@ -404,6 +412,7 @@
     shared = {n: getattr(r, n).at[layer] for n in (*WEIGHTS, *GRADS, *BIAS)}
     return [
         SimpleNamespace(
+            rows=ROWS[layer],
             **shared,
             **{n: getattr(r, n).at[i] for n in (*FWD, *BWD, *PADS)},
             **{n: getattr(r, KEPT_NAMES[layer][i] + n).at[slot] for n in KEPT},
@@ -480,7 +489,7 @@
     stage = r.x_stage.at[m % 2, i]
     sc.pad[:, 0:WS] = r.tokens[i, 0]
     st.x = sc.pad[...].astype(F32)
-    sc.xT[...] = st.x
+    sc.xT[...] = sc.pad[...]
     places = r.places
     valid = (
         (places[0:1, :] < r.info[m * WINDOWS + i, 1])
@@ -521,7 +530,7 @@
     stage = r.d_stage.at[m % 2, i]
     n = m * WINDOWS + i
     came = r.x_got[n, :, 0:CA]
-    x = dot(r.eye[0:CA, 0:CA], came, NT)
+    x = came.T.astype(F32)
     place, sizes = grid_place(groups_a)
     code_row = []
     for octant in range(8):
@@ -538,13 +547,13 @@
     code_row = jnp.concatenate(code_row, axis=1) + 8.0 * x[C : C + 1]
     keep = x[C + 1 : C + 2]
     x = x[0:C]
-    sc.xT[...] = x
+    sc.xT[...] = x.astype(BF)
     st.x = x
     yield 150
     yield from forward_attention(sc, w, st, code_row)
-    st.d = dot(r.eye[0:C, 0:CA], r.x_got[n, :, CA:], NT) * keep
+    st.d = r.x_got[n, :, CA:].T[0:C].astype(F32) * keep
     dd = st.d.astype(BF)
-    x = sc.xT[...] + st.branch.astype(BF).astype(F32)
+    x = sc.xT[...].astype(F32) + st.branch.astype(BF).astype(F32)
     z, scale = second_norm(sc, w, x)
     yield 200
     for c in range(6):
@@ -558,7 +567,7 @@
     stage[:, 0:CA] = jnp.concatenate([x * keep, none], axis=0).T.astype(BF)
     yield 150
     yield from feed_forward_back(sc, w, st, dd, z, scale)
-    z, scale = ln_stats(sc.xT[...])
+    z, scale = ln_stats(sc.xT[...].astype(F32))
     yield from backward_attention(sc, w, st, z, scale, True)
     stage[:, CA:] = jnp.concatenate([st.d, none], axis=0).T.astype(BF)
     yield 100
@@ -566,11 +575,12 @@
 
 def first_backward(r, sc, m, i):
     w, st = sc, SimpleNamespace()
-    came = dot(r.eye[...], r.d_got[m * WINDOWS + i], NT).astype(BF)
+    came = r.d_got[m * WINDOWS + i].T
+    came = jnp.concatenate([came[0:C], came[CA : CA + C]], axis=0)
     yield 200
     came = dot(came, r.perm[...])
     r.output[i, 0] = came[0:C, 0:WS].astype(BF)
-    st.d = came[CA : CA + C]
+    st.d = came[C : 2 * C]
     dd = st.d.astype(BF)
     z, scale = ln_stats(sc.x1[...])
     yield 200
@@ -579,7 +589,7 @@
         sc.dh[rows, :] = (dot(w.down[rows], dd) * sc.gp[rows, :].astype(F32)).astype(BF)
         yield 50
     yield from feed_forward_back(sc, w, st, dd, z, scale)
-    z, scale = ln_stats(sc.xT[...])
+    z, scale = ln_stats(sc.xT[...].astype(F32))
     yield from backward_attention(sc, w, st, z, scale, False)
     r.input_grad[i, 0] = st.d[:, 0:WS]
     yield 50
@@ -595,9 +605,11 @@
         stage=r.d_stage, got=r.d_got, sent=r.d_sent, arrived=r.d_arrived, sign=1
     )
 
+    far = all_peers(n_vol, n_plane)
+    reduction = Reduction(r, far, n_vol, n_plane, shard_len)
+
     @pl.when(s == 0)
     def _():
-        far = all_peers(n_vol, n_plane)
         peers = far + [
             neighbour(octant, sign, groups_a) for sign in (1, -1) for octant in range(1, 8)
         ]
@@ -640,6 +652,15 @@
         weave([second_layer(r, sc, m, i, groups_a) for i, sc in enumerate(windows)], 0)
         send_blocks(back, m, groups_a)
 
+    @pl.when(s == steps)
+    def _():
+        write_grads(of_layer(r, 1, 0)[0], r.grads.at[1])
+        reduction.start_core(1)
+
+    @pl.when(s == steps + 1)
+    def _():
+        reduction.start_plane(1)
+
     @pl.when(s >= 2)
     def _():
         m = s - 2
@@ -649,11 +670,15 @@
 
     @pl.when(s == steps + 1)
     def _():
+        write_grads(of_layer(r, 0, 0)[0], r.grads.at[0])
+        reduction.start_core(0)
+        reduction.end_plane(1)
+        reduction.start_plane(0)
         for m in range(max(steps - 2, 0), steps):
             wait_sent(forth, m, groups_a)
             wait_sent(back, m, groups_a)
-        for layer in range(2):
-            write_grads(of_layer(r, layer, 0)[0], r.grads.at[layer])
+        reduction.end_plane(0)
+        reduction.finish()
 
 
 def shard_rows(device, shard_len):
@@ -756,59 +781,90 @@
             o.vec[n] = jnp.broadcast_to(vector(source), (128, C)).T
 
 
-def reduce_kernel(n_vol, n_plane, shard_len, r):
-    vol, plane, core = own_place()
-    peers = all_peers(n_vol, n_plane)
-    greet(peers)
-    await_greetings(peers)
-    work = r.work
-    half = n_vol * n_plane
-    for v in range(n_vol):
-        for p in range(n_plane):
-            for c in range(2):
-                device = (v * n_plane + p) * 2 + c
-                start, stop = shard_rows(device % half, shard_len)
-                source = r.grads.at[device // half]
-                work[c, p, v, 0 : stop - start] = source[start:stop, :]
-
-    def copy(source, target, n):
+class Reduction:
+    def __init__(self, r, peers, n_vol, n_plane, shard_len):
+        self.r, self.peers, self.shard_len = r, peers, shard_len
+        self.n_vol, self.n_plane, self.half = n_vol, n_plane, n_vol // 2
+        self.vol, self.plane, self.core = own_place()
+
+    def vols(self, layer):
+        return pl.ds(layer * self.half, self.half)
+
+    def copy(self, source, target, peer, n):
         return pltpu.make_async_remote_copy(
             src_ref=source,
             dst_ref=target,
-            send_sem=r.sent.at[n],
-            recv_sem=r.arrived.at[n],
-            device_id=peers[n],
+            send_sem=self.r.r_sent.at[n],
+            recv_sem=self.r.r_arrived.at[n],
+            device_id=self.peers[peer],
             device_id_type=MESH,
         )
 
-    def exchange(copies):
-        for c in copies:
+    def over_core(self, layer):
+        source = self.r.work.at[1 - self.core, :, self.vols(layer)]
+        return [self.copy(source, self.r.from_core.at[layer], len(self.peers) - 1, layer)]
+
+    def over_plane(self, layer):
+        return [
+            self.copy(
+                self.r.wire.at[(self.plane + j) % self.n_plane, self.vols(layer)],
+                self.r.from_plane.at[layer, j - 1],
+                self.n_vol - 2 + j,
+                2 + layer * (self.n_plane - 1) + j - 1,
+            )
+            for j in range(1, self.n_plane)
+        ]
+
+    def over_vol(self):
+        return [
+            self.copy(
+                self.r.wire.at[self.plane, (self.vol + j) % self.n_vol],
+                self.r.from_vol.at[j - 1],
+                j - 1,
+                2 * self.n_plane + j - 1,
+            )
+            for j in range(1, self.n_vol)
+        ]
+
+    def start_core(self, layer):
+        for v in range(layer * self.half, (layer + 1) * self.half):
+            for p in range(self.n_plane):
+                for c in range(2):
+                    device = (v % self.half * self.n_plane + p) * 2 + c
+                    start, stop = shard_rows(device, self.shard_len)
+                    self.r.work[c, p, v, 0 : stop - start] = self.r.grads[layer, start:stop, :]
+        for c in self.over_core(layer):
             c.start()
-        for c in copies:
+
+    def start_plane(self, layer):
+        for c in self.over_core(layer):
             c.wait()
-
-    exchange([copy(work.at[1 - core], r.from_core, n_vol + n_plane - 2)])
-    work[core] += r.from_core[...]
-    exchange(
-        [
-            copy(work.at[core, (plane + j) % n_plane], r.from_plane.at[j - 1], n_vol - 2 + j)
-            for j in range(1, n_plane)
-        ]
-    )
-    total = work[core, plane]
-    for j in range(n_plane - 1):
-        total = total + r.from_plane[j]
-    work[core, plane] = total
-    exchange(
-        [
-            copy(work.at[core, plane, (vol + j) % n_vol], r.from_vol.at[j - 1], j - 1)
-            for j in range(1, n_vol)
-        ]
-    )
-    total = work[core, plane, vol]
-    for j in range(n_vol - 1):
-        total = total + r.from_vol[j]
-    r.total[...] = total
+        vols, work = self.vols(layer), self.r.work
+        total = work[self.core, :, vols] + self.r.from_core[layer]
+        work[self.core, :, vols] = total
+        self.r.wire[:, vols] = total.astype(BF)
+        for c in self.over_plane(layer):
+            c.start()
+
+    def end_plane(self, layer):
+        for c in self.over_plane(layer):
+            c.wait()
+        vols, work = self.vols(layer), self.r.work
+        total = work[self.core, self.plane, vols]
+        for j in range(self.n_plane - 1):
+            total = total + self.r.from_plane[layer, j].astype(F32)
+        work[self.core, self.plane, vols] = total
+        self.r.wire[self.plane, vols] = total.astype(BF)
+
+    def finish(self):
+        for c in self.over_vol():
+            c.start()
+        for c in self.over_vol():
+            c.wait()
+        total = self.r.work[self.core, self.plane, self.vol]
+        for j in range(self.n_vol - 1):
+            total = total + self.r.from_vol[j].astype(F32)
+        self.r.total[...] = total
 
 
 def call(kernel, steps, ins, outs, scratch, semaphores=(), collective_id=None, lag=0):
@@ -841,7 +897,7 @@
         scratch_shapes=[pltpu.VMEM(shape, dtype) for shape, dtype in scratch.values()]
         + [pltpu.SemaphoreType.DMA(shape) for shape in semaphores.values()],
         compiler_params=pltpu.CompilerParams(
-            vmem_limit_bytes=60 * 2**20,
+            vmem_limit_bytes=62 * 2**20,
             collective_id=collective_id,
             has_side_effects=collective_id is not None,
         ),
@@ -875,7 +931,8 @@
         return {n: (sizes + shape, dtype) for n, (shape, dtype) in table.items()}
 
     def kept(layer, slots):
-        shapes = dict(KEPT, gp=((16, T), BF)) if layer else KEPT
+        shapes = dict(KEPT, e=((ROWS[layer], HEADS * T), BF))
+        shapes = dict(shapes, gp=((16, T), BF)) if layer else shapes
         return {name + n: v for name in KEPT_NAMES[layer] for n, v in each(shapes, slots).items()}
 
     stage, landing = ((2, WINDOWS, T, 2 * CA), BF), ((count, T, 2 * CA), BF)
@@ -891,12 +948,11 @@
             order=(jnp.asarray(np.stack([np.eye(T, WS), ORDER]), BF), WHOLE),
             table=(position_bias, HBM),
             shard=(shard.reshape(slab, C), WHOLE),
-            eye=(jnp.asarray(np.eye(2 * CA), BF), WHOLE),
         ),
         dict(
             output=((count, 1, C, WS), BF, BY_STEP),
             input_grad=((count, 1, C, WS), F32, BY_STEP),
-            grads=((2, BLOCK_ROWS, C), F32, WHOLE),
+            total=((slab, C), F32, WHOLE),
         ),
         dict(
             **each(FWD, WINDOWS),
@@ -909,6 +965,12 @@
             **each(WEIGHTS, 2),
             page=((TABLE_SLOTS, WS, WS), BF),
             buf=((2, n_plane, n_vol, slab, C), BF),
+            grads=((2, BLOCK_ROWS, C), F32),
+            work=((2, n_plane, n_vol, slab, C), F32),
+            wire=((n_plane, n_vol, slab, C), BF),
+            from_core=((2, n_plane, n_vol // 2, slab, C), F32),
+            from_plane=((2, n_plane - 1, n_vol // 2, slab, C), BF),
+            from_vol=((n_vol - 1, slab, C), BF),
             x_stage=stage,
             d_stage=stage,
             x_got=landing,
@@ -922,25 +984,13 @@
             g_sent=(n_peers,),
             g_arrived=(n_peers,),
             turned=(TABLE_SLOTS,),
+            r_sent=(2 * n_plane + n_vol - 1,),
+            r_arrived=(2 * n_plane + n_vol - 1,),
         ),
         collective_id=1,
         lag=2,
     )
-    reduced = call(
-        lambda r: reduce_kernel(n_vol, n_plane, shard_len, r),
-        1,
-        dict(grads=(layers.grads, WHOLE)),
-        dict(total=((slab, C), F32, WHOLE)),
-        dict(
-            work=((2, n_plane, n_vol, slab, C), F32),
-            from_core=((n_plane, n_vol, slab, C), F32),
-            from_plane=((n_plane - 1, n_vol, slab, C), F32),
-            from_vol=((n_vol - 1, slab, C), F32),
-        ),
-        dict(sent=(n_peers,), arrived=(n_peers,)),
-        collective_id=2,
-    )
-    shard_grad = lax.dynamic_slice(reduced.total.reshape(-1), (offset,), (shard_len,))
+    shard_grad = lax.dynamic_slice(layers.total.reshape(-1), (offset,), (shard_len,))
     position = (device * shard_len + jnp.arange(shard_len, dtype=jnp.int32)) % (BLOCK_ROWS * C)
     is_vector = position >= 12 * C * C
     step_rate = jnp.where(is_vector, RATE_VECTOR, RATE_MATRIX)

time: 230 us -> 214 us (0.930)
  Pallas kernels: 217 us -> 201 us
    pallas_call x2 -> x1, Pallas kernels: 217 us -> 201 us  [call(): pl.pallas_call(body, grid=(steps + lag,), in_specs=[spec(a.shape, kind, 0...]
    unnamed x13 -> x11, local copies, waits for them, and re-layouts: 7.46 us -> 7.78 us
where the time goes in v5:
time: 214 us
  Pallas kernels  201 us (94%)
  local copies, waits for them, and re-layouts  10.5 us (5%)
  other arithmetic  2.16 us (1%)
    pallas_call x1, Pallas kernels, call(): pl.pallas_call(body, grid=(steps + lag,), in_specs=[spec(a.shape, kind, 0...  201 us
    unnamed x11, local copies, waits for them, and re-layouts  7.78 us

profile of v5, /device:TPU:0, one launch (start us, length us, event | category | flops | bytes accessed | tf_op | source)
XLA Modules:
  0.0 214.0 jit_solution(3643145023563394887)
XLA Ops:
  0.7 0.7 pad_add_fusion
  1.3 0.7 copy.18.refs_2_
  2.0 0.8 convert_element_type.6
  2.8 0.3 dynamic_update_slice.3
  3.1 0.7 reshape.18.refs_7_
  3.8 4.0 %copy.19.refs_6_ = bf16[2,6,343,343]{3,2,1,0:T(8,128)(2,1)} copy(bf16[2,6,343,343]{3,0,2,1:T(2,128)(2,1)} %param.13) | data formatting | bytes 5647152 | tf_op args[2]
  7.7 0.0 copy-start.1
  7.7 0.0 copy-start.2
  7.7 0.0 copy-start.3
  7.7 200.6 %shard_map.154 = (bf16[16,1,96,343]{3,2,1,0:T(8,128)(2,1)}, f32[16,1,96,343]{3,2,1,0:T(8,128)}, f32[80,96]{1,0:T(8,128)}) custom-call(bf16[16,1,96,343]{3,2,1,0:T(8,128)(2,1)} %bitcast.10, bf16[16,1,96,343]{3,2,1,0:T(8,128)(2,1)} %bitcast.11, s32[16,4]{1,0:T(8,128)} %copy.18.refs_2_, bf16[384,384]{1,0:T(8,128)(2,1)} %constant.62.clone.refs_3_, ...), custom_call_target="tpu_custom_call" | custom-call | tf_op jit(solution)/shard_map/pallas_call | solution.py:891
  208.4 0.0 copy-start
  208.4 1.0 reshape.19
  209.4 0.0 copy-done.1
  209.4 0.0 copy-done.2
  209.4 0.0 copy-done.3
  209.5 0.7 fusion.5
  210.2 2.4 %copy.23 = bf16[16,1,343,96]{2,3,1,0:T(8,128)(2,1)} copy(bf16[16,1,343,96]{2,3,1,0:T(8,128)(2,1)} %bitcast.9) | data formatting | bytes 2107392
  212.6 0.0 copy-done
  212.6 1.4 copy.24
  (1 shorter events, 0.0 us)
Async XLA Ops:
  7.7 201.7 %copy-start.1 = (f32[6984]{0:T(1024)S(1)}, f32[6984]{0:T(1024)}, u32[]{:S(2)}) copy-start(f32[6984]{0:T(1024)} %param.16) | copy-start | bytes 83812
  7.7 201.7 %copy-start.2 = (f32[6984]{0:T(1024)S(1)}, f32[6984]{0:T(1024)}, u32[]{:S(2)}) copy-start(f32[6984]{0:T(1024)} %param.17) | copy-start | bytes 83812
  7.7 201.7 %copy-start.3 = (f32[6984]{0:T(1024)S(1)}, f32[6984]{0:T(1024)}, u32[]{:S(2)}) copy-start(f32[6984]{0:T(1024)} %param.18) | copy-start | bytes 83812
  208.4 4.2 %copy-start = (f32[16,1,96,343]{3,2,1,0:T(8,128)S(1)}, f32[16,1,96,343]{3,2,1,0:T(8,128)}, u32[]{:S(2)}) copy-start(f32[16,1,96,343]{3,2,1,0:T(8,128)} %get-tuple-element.10) | copy-start | bytes 6322180

commit v6 on v5

--- a/solution.py
+++ b/solution.py
@@ -18,6 +18,8 @@
 STEP = 6
 T = 384
 WINDOWS = 2
+CHUNK = 64
+LAG = 150
 TABLE_SLOTS = 3
 ROWS = (352, T)
 CA = 128
@@ -195,7 +197,7 @@
     tops = [None] * HEADS
 
     def scores(h, c):
-        rows = slice(128 * c, min(128 * c + 128, sc.rows))
+        rows = slice(CHUNK * c, min(CHUNK * c + CHUNK, sc.rows))
         count = rows.stop - rows.start
         x_all = dot(sc.kn[rows], sc.qb[:, T * h : T * h + T])
         codes = sc.codes[rows]
@@ -203,17 +205,17 @@
         for j in range(3):
             lanes = slice(128 * j, 128 * j + 128)
             allowed = codes == code_row[:, lanes]
-            if j == c:
-                allowed = allowed | eye[0:count]
+            if j == rows.start // 128:
+                allowed = allowed | eye[rows.start % 128 : rows.start % 128 + count]
             part = jnp.where(allowed, x_all[:, lanes] + sc.bias[h, rows, lanes], MASK_FILL)
-            sc.s[h % 2, rows, lanes] = part
+            sc.s[rows, lanes] = part
             parts.append(jnp.max(part.reshape(count // 8, 8, 128), axis=0))
         top = jnp.concatenate(parts, axis=1)
         tops[h] = top if tops[h] is None else jnp.maximum(tops[h], top)
 
     def raise_(h, c):
-        rows = slice(128 * c, min(128 * c + 128, sc.rows))
-        sc.e[rows, T * h : T * h + T] = jnp.exp(sc.s[h % 2, rows] - tops[h]).astype(BF)
+        rows = slice(CHUNK * c, min(CHUNK * c + CHUNK, sc.rows))
+        sc.e[rows, T * h : T * h + T] = jnp.exp(sc.s[rows] - tops[h]).astype(BF)
 
     def attend(h):
         out = dot(sc.vt[h, :, 0 : sc.rows], sc.e[:, T * h : T * h + T])
@@ -224,14 +226,14 @@
         sc.attaug[16 * h : 16 * h + 16, :] = part.astype(BF)
 
     for h in range(HEADS + 2):
-        for c in range(3):
+        for c in range(T // CHUNK):
+            if 0 <= h - 1 < HEADS:
+                raise_(h - 1, c)
             if h < HEADS:
                 scores(h, c)
-            if 0 <= h - 1 < HEADS:
-                raise_(h - 1, c)
             if c == 0 and 0 <= h - 2 < HEADS:
                 attend(h - 2)
-            yield 70
+            yield 35
         if h < HEADS:
             tops[h] = jnp.max(tops[h], axis=0, keepdims=True)
     st.branch = dot(w.projT[...], sc.attaug[...])
@@ -357,7 +359,7 @@
     vt=((HEADS, 32, T), BF),
     kn=((T, CA), BF),
     codes=((T, 128), F32),
-    s=((2, T, T), F32),
+    s=((T, T), F32),
 )
 BIAS = dict(bias=((HEADS, T, T), F32))
 KEPT = dict(
@@ -492,9 +494,9 @@
     sc.xT[...] = sc.pad[...]
     places = r.places
     valid = (
-        (places[0:1, :] < r.info[m * WINDOWS + i, 1])
-        & (places[1:2, :] < r.info[m * WINDOWS + i, 2])
-        & (places[2:3, :] < r.info[m * WINDOWS + i, 3])
+        (places[0:1, :] < r.extent[0, 0, m * WINDOWS + i])
+        & (places[1:2, :] < r.extent[1, 0, m * WINDOWS + i])
+        & (places[2:3, :] < r.extent[2, 0, m * WINDOWS + i])
     )
     valid = jnp.where(valid, 1.0, 0.0)
     sc.codes[...] = jnp.broadcast_to(valid - 1.0, (128, T)).T
@@ -518,7 +520,7 @@
     x = x + (dot(w.downT[...], sc.act[...]) + wide(w.vec[4]))
     yield 100
     row = lax.broadcasted_iota(jnp.int32, (CA - C, T), 0)
-    label = r.info[m * WINDOWS + i, 0].astype(F32)
+    label = r.volume[0, m * WINDOWS + i].astype(F32)
     extra = jnp.where(row == 0, label, jnp.where(row == 1, valid, 0.0))
     x = jnp.concatenate([x, extra], axis=0).astype(BF)
     stage[:, 0:CA] = dot(r.perm[...], x, NT).astype(BF)
@@ -636,7 +638,7 @@
             wait_sent(forth, s - 2, groups_a)
 
         windows = of_layer(r, 0, s % 3)
-        weave([first_forward(r, sc, s, i) for i, sc in enumerate(windows)], 0)
+        weave([first_forward(r, sc, s, i) for i, sc in enumerate(windows)], LAG)
         send_blocks(forth, s, groups_a)
 
     @pl.when((s >= 1) & (s <= steps))
@@ -649,7 +651,7 @@
             wait_sent(back, m - 2, groups_a)
 
         windows = of_layer(r, 1, 0)
-        weave([second_layer(r, sc, m, i, groups_a) for i, sc in enumerate(windows)], 0)
+        weave([second_layer(r, sc, m, i, groups_a) for i, sc in enumerate(windows)], LAG)
         send_blocks(back, m, groups_a)
 
     @pl.when(s == steps)
@@ -666,7 +668,7 @@
         m = s - 2
         wait_arrived(back, m, groups_a)
         windows = of_layer(r, 0, m % 3)
-        weave([first_backward(r, sc, m, i) for i, sc in enumerate(windows)], 0)
+        weave([first_backward(r, sc, m, i) for i, sc in enumerate(windows)], LAG)
 
     @pl.when(s == steps + 1)
     def _():
@@ -925,7 +927,6 @@
     offset = flat_offset(device, shard_len)
     shard = lax.dynamic_update_slice(jnp.zeros((slab * C,), BF), master.astype(BF), (offset,))
     n_peers = n_vol + n_plane - 1
-    info = jnp.concatenate((window_volume[:, :, None], clip_extent), axis=2)[:, 0]
 
     def each(table, *sizes):
         return {n: (sizes + shape, dtype) for n, (shape, dtype) in table.items()}
@@ -942,7 +943,8 @@
         dict(
             tokens=(tokens.transpose(0, 1, 3, 2), BY_STEP),
             cotangent=(cotangent.transpose(0, 1, 3, 2), BY_STEP),
-            info=(info, SMEM),
+            volume=(window_volume.T, SMEM),
+            extent=(clip_extent.transpose(2, 1, 0), SMEM),
             perm=(jnp.asarray(PERM, BF), WHOLE),
             places=(jnp.asarray(PLACES), WHOLE),
             order=(jnp.asarray(np.stack([np.eye(T, WS), ORDER]), BF), WHOLE),

time: 214 us -> 204 us (0.953)
  Pallas kernels: 201 us -> 192 us
    pallas_call x1, Pallas kernels: 201 us -> 192 us  [call(): pl.pallas_call(body, grid=(steps + lag,), in_specs=[spec(a.shape, kind, 0...]
where the time goes in v6:
time: 204 us
  Pallas kernels  192 us (94%)
  local copies, waits for them, and re-layouts  9.79 us (5%)
    pallas_call x1, Pallas kernels, call(): pl.pallas_call(body, grid=(steps + lag,), in_specs=[spec(a.shape, kind, 0...  192 us
    unnamed x11, local copies, waits for them, and re-layouts  7.78 us

profile of v6, /device:TPU:0, one launch (start us, length us, event | category | flops | bytes accessed | tf_op | source)
XLA Modules:
  0.0 203.8 jit_solution(8913858135603671712)
XLA Ops:
  0.7 0.8 convert_element_type.6
  1.4 0.3 dynamic_update_slice.3
  1.7 0.7 reshape.18.refs_8_
  2.4 4.0 %copy.17.refs_7_ = bf16[2,6,343,343]{3,2,1,0:T(8,128)(2,1)} copy(bf16[2,6,343,343]{3,0,2,1:T(2,128)(2,1)} %param.13) | data formatting | bytes 5647152 | tf_op args[2]
  6.4 0.0 copy-start.1
  6.4 0.0 copy-start.2
  6.4 0.0 copy-start.3
  6.4 191.8 %shard_map.154 = (bf16[16,1,96,343]{3,2,1,0:T(8,128)(2,1)}, f32[16,1,96,343]{3,2,1,0:T(8,128)}, f32[80,96]{1,0:T(8,128)}) custom-call(bf16[16,1,96,343]{3,2,1,0:T(8,128)(2,1)} %bitcast.8, bf16[16,1,96,343]{3,2,1,0:T(8,128)(2,1)} %bitcast.9, s32[1,16]{1,0:T(1,128)} %bitcast.11, s32[3,1,16]{2,1,0:T(1,128)} %bitcast.10, ...), custom_call_target="tpu_custom_call" | custom-call | tf_op jit(solution)/shard_map/pallas_call | solution.py:893
  198.2 0.0 copy-start
  198.2 1.0 reshape.19
  199.2 0.0 copy-done.1
  199.2 0.0 copy-done.2
  199.2 0.0 copy-done.3
  199.2 0.7 fusion.5
  199.9 2.4 %copy.21 = bf16[16,1,343,96]{2,3,1,0:T(8,128)(2,1)} copy(bf16[16,1,343,96]{2,3,1,0:T(8,128)(2,1)} %bitcast.7) | data formatting | bytes 2107392
  202.3 0.0 copy-done
  202.4 1.4 copy.22
  (1 shorter events, 0.0 us)
Async XLA Ops:
  6.4 192.8 %copy-start.1 = (f32[6984]{0:T(1024)S(1)}, f32[6984]{0:T(1024)}, u32[]{:S(2)}) copy-start(f32[6984]{0:T(1024)} %param.16) | copy-start | bytes 83812
  6.4 192.8 %copy-start.2 = (f32[6984]{0:T(1024)S(1)}, f32[6984]{0:T(1024)}, u32[]{:S(2)}) copy-start(f32[6984]{0:T(1024)} %param.17) | copy-start | bytes 83812
  6.4 192.8 %copy-start.3 = (f32[6984]{0:T(1024)S(1)}, f32[6984]{0:T(1024)}, u32[]{:S(2)}) copy-start(f32[6984]{0:T(1024)} %param.18) | copy-start | bytes 83812
  198.2 4.2 %copy-start = (f32[16,1,96,343]{3,2,1,0:T(8,128)S(1)}, f32[16,1,96,343]{3,2,1,0:T(8,128)}, u32[]{:S(2)}) copy-start(f32[16,1,96,343]{3,2,1,0:T(8,128)} %get-tuple-element.10) | copy-start | bytes 6322180

commit v7 on v6

--- a/solution.py
+++ b/solution.py
@@ -231,7 +231,7 @@
                 raise_(h - 1, c)
             if h < HEADS:
                 scores(h, c)
-            if c == 0 and 0 <= h - 2 < HEADS:
+            if c == 3 and 0 <= h - 2 < HEADS:
                 attend(h - 2)
             yield 35
         if h < HEADS:
@@ -619,10 +619,10 @@
         for n in range(TABLE_SLOTS):
             table_copy(r, n).start()
         vol, plane, core = own_place()
-        r.buf[core, plane, vol] = r.shard[...]
+        r.buf[core, plane, vol] = r.shard[...].astype(BF)
         clear_scratch(r)
         await_greetings(peers)
-        meanwhile = (lambda: None, lambda: turn_tables(r, 0), lambda: turn_tables(r, 1))
+        meanwhile = (lambda: turn_tables(r, 0), lambda: turn_tables(r, 1), lambda: None)
         for copies, work in zip(gather_stages(r, far, n_vol, n_plane), meanwhile):
             for c in copies:
                 c.start()
@@ -925,7 +925,7 @@
     device = lax.axis_index((VOL, WIN))
     slab = slab_rows(shard_len)
     offset = flat_offset(device, shard_len)
-    shard = lax.dynamic_update_slice(jnp.zeros((slab * C,), BF), master.astype(BF), (offset,))
+    shard = lax.dynamic_update_slice(jnp.zeros((slab * C,), F32), master, (offset,))
     n_peers = n_vol + n_plane - 1
 
     def each(table, *sizes):

time: 204 us -> 202 us (level)
  no operation moved by 1% of the time
where the time goes in v7:
time: 202 us
  Pallas kernels  190 us (94%)
  local copies, waits for them, and re-layouts  10.6 us (5%)
    pallas_call x1, Pallas kernels, call(): pl.pallas_call(body, grid=(steps + lag,), in_specs=[spec(a.shape, kind, 0...  190 us
    unnamed x11, local copies, waits for them, and re-layouts  7.78 us

profile of v7, /device:TPU:0, one launch (start us, length us, event | category | flops | bytes accessed | tf_op | source)
XLA Modules:
  0.0 202.1 jit_solution(11342385567665174093)
XLA Ops:
  0.7 1.1 dynamic_update_slice.3
  1.7 0.7 reshape.18.refs_8_
  2.4 4.0 %copy.17.refs_7_ = bf16[2,6,343,343]{3,2,1,0:T(8,128)(2,1)} copy(bf16[2,6,343,343]{3,0,2,1:T(2,128)(2,1)} %param.13) | data formatting | bytes 5647152 | tf_op args[2]
  6.4 0.0 copy-start.1
  6.4 0.0 copy-start.2
  6.4 0.0 copy-start.3
  6.4 190.1 %shard_map.154 = (bf16[16,1,96,343]{3,2,1,0:T(8,128)(2,1)}, f32[16,1,96,343]{3,2,1,0:T(8,128)}, f32[80,96]{1,0:T(8,128)}) custom-call(bf16[16,1,96,343]{3,2,1,0:T(8,128)(2,1)} %bitcast.8, bf16[16,1,96,343]{3,2,1,0:T(8,128)(2,1)} %bitcast.9, s32[1,16]{1,0:T(1,128)} %bitcast.11, s32[3,1,16]{2,1,0:T(1,128)} %bitcast.10, ...), custom_call_target="tpu_custom_call" | custom-call | tf_op jit(solution)/shard_map/pallas_call | solution.py:893
  196.5 0.0 copy-start
  196.5 1.0 reshape.19
  197.5 0.0 copy-done.1
  197.6 0.0 copy-done.2
  197.6 0.0 copy-done.3
  197.6 0.7 fusion.5
  198.3 2.4 %copy.21 = bf16[16,1,343,96]{2,3,1,0:T(8,128)(2,1)} copy(bf16[16,1,343,96]{2,3,1,0:T(8,128)(2,1)} %bitcast.7) | data formatting | bytes 2107392
  200.7 0.0 copy-done
  200.7 1.4 copy.22
  (1 shorter events, 0.0 us)
Async XLA Ops:
  6.4 191.2 %copy-start.1 = (f32[6984]{0:T(1024)S(1)}, f32[6984]{0:T(1024)}, u32[]{:S(2)}) copy-start(f32[6984]{0:T(1024)} %param.16) | copy-start | bytes 83812
  6.4 191.2 %copy-start.2 = (f32[6984]{0:T(1024)S(1)}, f32[6984]{0:T(1024)}, u32[]{:S(2)}) copy-start(f32[6984]{0:T(1024)} %param.17) | copy-start | bytes 83812
  6.4 191.2 %copy-start.3 = (f32[6984]{0:T(1024)S(1)}, f32[6984]{0:T(1024)}, u32[]{:S(2)}) copy-start(f32[6984]{0:T(1024)} %param.18) | copy-start | bytes 83812
  196.5 4.2 %copy-start = (f32[16,1,96,343]{3,2,1,0:T(8,128)S(1)}, f32[16,1,96,343]{3,2,1,0:T(8,128)}, u32[]{:S(2)}) copy-start(f32[16,1,96,343]{3,2,1,0:T(8,128)} %get-tuple-element.10) | copy-start | bytes 6322180

commit v8 on v7

--- a/solution.py
+++ b/solution.py
@@ -675,11 +675,13 @@
         write_grads(of_layer(r, 0, 0)[0], r.grads.at[0])
         reduction.start_core(0)
         reduction.end_plane(1)
+        reduction.start_vol(1)
         reduction.start_plane(0)
         for m in range(max(steps - 2, 0), steps):
             wait_sent(forth, m, groups_a)
             wait_sent(back, m, groups_a)
         reduction.end_plane(0)
+        reduction.start_vol(0)
         reduction.finish()
 
 
@@ -858,9 +860,15 @@
         work[self.core, self.plane, vols] = total
         self.r.wire[self.plane, vols] = total.astype(BF)
 
+    def start_vol(self, layer):
+        for j, c in enumerate(self.over_vol(), 1):
+            target = (self.vol + j) % self.n_vol
+
+            @pl.when(target // self.half == layer)
+            def _():
+                c.start()
+
     def finish(self):
-        for c in self.over_vol():
-            c.start()
         for c in self.over_vol():
             c.wait()
         total = self.r.work[self.core, self.plane, self.vol]

time: 202 us -> 202 us (level)
  no operation moved by 1% of the time
where the time goes in v8:
time: 202 us
  Pallas kernels  190 us (94%)
  local copies, waits for them, and re-layouts  10.6 us (5%)
    pallas_call x1, Pallas kernels, call(): pl.pallas_call(body, grid=(steps + lag,), in_specs=[spec(a.shape, kind, 0...  190 us
    unnamed x11, local copies, waits for them, and re-layouts  7.78 us

profile of v8, /device:TPU:0, one launch (start us, length us, event | category | flops | bytes accessed | tf_op | source)
XLA Modules:
  0.0 202.1 jit_solution(7995187147769011314)
XLA Ops:
  0.7 1.1 dynamic_update_slice.3
  1.7 0.7 reshape.18.refs_8_
  2.4 4.0 %copy.17.refs_7_ = bf16[2,6,343,343]{3,2,1,0:T(8,128)(2,1)} copy(bf16[2,6,343,343]{3,0,2,1:T(2,128)(2,1)} %param.13) | data formatting | bytes 5647152 | tf_op args[2]
  6.4 0.0 copy-start.1
  6.4 0.0 copy-start.2
  6.4 0.0 copy-start.3
  6.4 190.1 %shard_map.154 = (bf16[16,1,96,343]{3,2,1,0:T(8,128)(2,1)}, f32[16,1,96,343]{3,2,1,0:T(8,128)}, f32[80,96]{1,0:T(8,128)}) custom-call(bf16[16,1,96,343]{3,2,1,0:T(8,128)(2,1)} %bitcast.8, bf16[16,1,96,343]{3,2,1,0:T(8,128)(2,1)} %bitcast.9, s32[1,16]{1,0:T(1,128)} %bitcast.11, s32[3,1,16]{2,1,0:T(1,128)} %bitcast.10, ...), custom_call_target="tpu_custom_call" | custom-call | tf_op jit(solution)/shard_map/pallas_call | solution.py:901
  196.5 0.0 copy-start
  196.5 1.0 reshape.19
  197.5 0.0 copy-done.1
  197.6 0.0 copy-done.2
  197.6 0.0 copy-done.3
  197.6 0.7 fusion.5
  198.3 2.4 %copy.21 = bf16[16,1,343,96]{2,3,1,0:T(8,128)(2,1)} copy(bf16[16,1,343,96]{2,3,1,0:T(8,128)(2,1)} %bitcast.7) | data formatting | bytes 2107392
  200.7 0.0 copy-done
  200.7 1.4 copy.22
  (1 shorter events, 0.0 us)
Async XLA Ops:
  6.4 191.2 %copy-start.1 = (f32[6984]{0:T(1024)S(1)}, f32[6984]{0:T(1024)}, u32[]{:S(2)}) copy-start(f32[6984]{0:T(1024)} %param.16) | copy-start | bytes 83812
  6.4 191.2 %copy-start.2 = (f32[6984]{0:T(1024)S(1)}, f32[6984]{0:T(1024)}, u32[]{:S(2)}) copy-start(f32[6984]{0:T(1024)} %param.17) | copy-start | bytes 83812
  6.4 191.2 %copy-start.3 = (f32[6984]{0:T(1024)S(1)}, f32[6984]{0:T(1024)}, u32[]{:S(2)}) copy-start(f32[6984]{0:T(1024)} %param.18) | copy-start | bytes 83812
  196.5 4.2 %copy-start = (f32[16,1,96,343]{3,2,1,0:T(8,128)S(1)}, f32[16,1,96,343]{3,2,1,0:T(8,128)}, u32[]{:S(2)}) copy-start(f32[16,1,96,343]{3,2,1,0:T(8,128)} %get-tuple-element.10) | copy-start | bytes 6322180
